TPU v7x, 32 devices: a whole 2x2x4 slice. The times are simulated.
32 devices in a mesh: gx: 4 (over z), gy: 4 (over x, core), gz: 2 (over y).
Axes of the slice: x: 2, y: 2, z: 4, core: 2. Of those that a mesh axis runs over, the one named last changes fastest.
Arguments:
- tokens: bfloat16 [2048, 6144], P(('gy', 'gx'), 'gz'), may hold values from -6 to 6
- w_in: bfloat16 [6144, 24576], P('gz', ('gx', 'gy')), may hold values from -0.078125 to 0.078125
- w_out: bfloat16 [24576, 6144], P(('gx', 'gy'), 'gz')
- out_grad: bfloat16 [2048, 6144], P(('gy', 'gx'), 'gz')
Outputs:
- in_grad: bfloat16 [2048, 6144], P(('gy', 'gx'), 'gz')
- grad_in_clipped: bfloat16 [6144, 24576], P('gz', ('gx', 'gy'))
- grad_out_clipped: bfloat16 [24576, 6144], P(('gx', 'gy'), 'gz')
All inputs are finite; a program needn't handle non-finite values.
Results may differ from a plain program's by a relative error of at most 0.025.
Values may be sent and summed in bfloat16 or wider, within the bound.
No kernel may reach another device: no remote copies, remote signals or barrier semaphores. Data moves between devices by JAX's collectives and lax.ppermute only.
A program may use at most 384 MiB of HBM per device.

v0:
```python
import jax
import jax.numpy as jnp
from jax import lax
from jax.sharding import PartitionSpec as P

D = 6144
FW = 24576


GELU_C = 0.7978845608


def gelu_parts(values):
    inner_arg = GELU_C * (values + 0.044715 * values * values * values)
    tanh_val = jnp.tanh(inner_arg)
    value_out = 0.5 * values * (1.0 + tanh_val)
    slope = 0.5 * (1.0 + tanh_val) + 0.5 * values * (1.0 - tanh_val * tanh_val) * GELU_C * (
        1.0 + 3.0 * 0.044715 * values * values
    )
    return (value_out, slope)


def contract(left, right, left_dim, right_dim):
    return lax.dot_general(
        left, right, (((left_dim,), (right_dim,)), ((), ())), preferred_element_type=jnp.float32
    )


def shards(tokens, w_in, w_out, out_grad):
    x_blk, dy_blk = (
        lax.all_gather(tokens, "gx", axis=0, tiled=True),
        lax.all_gather(out_grad, "gx", axis=0, tiled=True),
    )
    w_in_full, w_out_full = (
        lax.all_gather(w_in, "gy", axis=1, tiled=True),
        lax.all_gather(w_out, "gy", axis=0, tiled=True),
    )
    h_term = contract(x_blk, w_in_full, 1, 0)
    d_term = contract(dy_blk, w_out_full, 1, 1)
    pre_act, d_act = (
        lax.psum_scatter(h_term.astype(jnp.bfloat16), "gz", scatter_dimension=0, tiled=True).astype(
            jnp.float32
        ),
        lax.psum_scatter(d_term.astype(jnp.bfloat16), "gz", scatter_dimension=0, tiled=True).astype(
            jnp.float32
        ),
    )
    value_out, slope = gelu_parts(pre_act)
    act_rows = value_out.astype(jnp.bfloat16)
    d_pre = (d_act * slope).astype(jnp.bfloat16)
    act_full, d_pre_full = (
        lax.all_gather(act_rows, "gz", axis=0, tiled=True),
        lax.all_gather(d_pre, "gz", axis=0, tiled=True),
    )
    dx_term = contract(d_pre_full, w_in_full, 1, 1)
    in_grad = lax.psum_scatter(dx_term.astype(jnp.bfloat16), "gx", scatter_dimension=0, tiled=True)
    gin_term = contract(x_blk, d_pre_full, 0, 0)
    gout_term = contract(act_full, dy_blk, 0, 0)
    grad_in, grad_out = (
        lax.psum_scatter(
            gin_term.astype(jnp.bfloat16), "gy", scatter_dimension=1, tiled=True
        ).astype(jnp.float32),
        lax.psum_scatter(
            gout_term.astype(jnp.bfloat16), "gy", scatter_dimension=0, tiled=True
        ).astype(jnp.float32),
    )
    local_square = jnp.sum(grad_in * grad_in) + jnp.sum(grad_out * grad_out)
    grand_total = lax.psum(local_square, ("gx", "gy", "gz"))
    factor = 1.0 / jnp.sqrt(grand_total / (2.0 * D * FW) + 1e-06)
    return (
        in_grad,
        (grad_in * factor).astype(jnp.bfloat16),
        (grad_out * factor).astype(jnp.bfloat16),
    )


def solution(mesh):
    placed = (
        P(("gy", "gx"), "gz"),
        P("gz", ("gx", "gy")),
        P(("gx", "gy"), "gz"),
        P(("gy", "gx"), "gz"),
    )
    return jax.shard_map(
        shards,
        mesh=mesh,
        in_specs=placed,
        out_specs=(P(("gy", "gx"), "gz"), P("gz", ("gx", "gy")), P(("gx", "gy"), "gz")),
        check_vma=False,
    )
```

profile of v0, /device:TPU:8, one launch (start us, length us, event | category | flops | bytes accessed | tf_op | source)
XLA Modules:
  0.0 1547.8 jit_solution(10404001863691294354)
XLA Ops:
  7.2 0.0 all-gather.7.cloned.1.call-start
  7.2 0.7 all-gather.7.cloned.1.call-update
  7.9 0.0 all-gather.9.cloned.1.call-start
  7.9 0.7 all-gather.9.cloned.1.call-update
  8.6 0.0 all-gather.11.cloned.1.call-start
  8.7 0.7 all-gather.11.cloned.1.call-update
  9.4 0.0 all-gather.13.cloned.1.call-start
  9.4 0.5 all-gather.13.cloned.1.call-update
  10.0 0.0 reduce-scatter.6.cloned.1.call-start
  10.0 61.9 %all-gather.7.cloned.1.call-done = bf16[512,3072]{1,0:T(8,128)(2,1)} async-done(((bf16[128,3072]{1,0:T(8,128)(2,1)}), bf16[512,3072]{1,0:T(8,128)(2,1)}) %all-gather.7.cloned.1.call-update) | async-done | bytes 3145744 | tf_op jit(solution)/shard_map/all_gather | solution.py:32
  71.9 229.8 %all-gather.9.cloned.1.call-done = bf16[6144,3072]{1,0:T(8,128)(2,1)} async-done(((bf16[1536,3072]{1,0:T(8,128)(2,1)}), bf16[6144,3072]{1,0:T(8,128)(2,1)}) %all-gather.9.cloned.1.call-update) | async-done | bytes 37748752 | tf_op jit(solution)/shard_map/all_gather | solution.py:36
  301.7 26.9 %convolution_convert_fusion.2 = bf16[512,6144]{1,0:T(8,128)(2,1)} fusion(bf16[512,3072]{1,0:T(8,128)(2,1)} %all-gather.7.cloned.1.call-done, bf16[6144,3072]{1,0:T(8,128)(2,1)} %all-gather.9.cloned.1.call-done), kind=kOutput, calls=%fused_computation.18 | convolution fusion | flops 19330498560 | bytes 47185920 | tf_op jit(solution)/shard_map/dot_general | solution.py:24
  328.6 0.0 reduce-scatter.6.cloned.1.call-update
  328.6 0.0 reduce-scatter.8.cloned.1.call-start
  328.7 35.8 %all-gather.11.cloned.1.call-done = bf16[512,3072]{1,0:T(8,128)(2,1)} async-done(((bf16[128,3072]{1,0:T(8,128)(2,1)}), bf16[512,3072]{1,0:T(8,128)(2,1)}) %all-gather.11.cloned.1.call-update) | async-done | bytes 3145744 | tf_op jit(solution)/shard_map/all_gather | solution.py:31
  364.5 229.6 %all-gather.13.cloned.1.call-done = bf16[3072,6144]{1,0:T(8,128)(2,1)} async-done(((bf16[3072,1536]{1,0:T(8,128)(2,1)}), bf16[3072,6144]{1,0:T(8,128)(2,1)}) %all-gather.13.cloned.1.call-update) | async-done | bytes 37748752 | tf_op jit(solution)/shard_map/all_gather | solution.py:35
  594.1 26.8 %convolution_convert_fusion.1 = bf16[512,6144]{1,0:T(8,128)(2,1)} fusion(bf16[512,3072]{1,0:T(8,128)(2,1)} %all-gather.11.cloned.1.call-done, bf16[3072,6144]{1,0:T(8,128)(2,1)} %all-gather.13.cloned.1.call-done), kind=kOutput, calls=%fused_computation.17 | convolution fusion | flops 19330498560 | bytes 47185920 | tf_op jit(solution)/shard_map/dot_general | solution.py:24
  620.9 0.0 reduce-scatter.8.cloned.1.call-update
  621.0 0.6 all-gather.15.cloned.1.call-start
  621.5 52.4 %reduce-scatter.6.cloned.1.call-done = bf16[256,6144]{1,0:T(8,128)(2,1)} async-done(((bf16[512,6144]{1,0:T(8,128)(2,1)}), bf16[256,6144]{1,0:T(8,128)(2,1)}) %reduce-scatter.6.cloned.1.call-update) | async-done | bytes 3145744 | tf_op jit(solution)/shard_map/reduce_scatter | solution.py:44
  673.9 79.9 %reduce-scatter.8.cloned.1.call-done = bf16[256,6144]{1,0:T(8,128)(2,1)} async-done(((bf16[512,6144]{1,0:T(8,128)(2,1)}), bf16[256,6144]{1,0:T(8,128)(2,1)}) %reduce-scatter.8.cloned.1.call-update) | async-done | bytes 3145744 | tf_op jit(solution)/shard_map/reduce_scatter | solution.py:41
  753.9 8.3 fusion.11
  762.1 0.0 copy-start.1
  762.1 0.0 all-gather.15.cloned.1.call-update
  762.2 0.0 all-gather.17.cloned.1.call-start
  762.2 0.7 all-gather.17.cloned.1.call-update
  762.9 0.0 reduce-scatter.12.cloned.1.call-start
  763.0 79.7 %all-gather.15.cloned.1.call-done = bf16[512,6144]{1,0:T(8,128)(2,1)} async-done(((bf16[256,6144]{1,0:T(8,128)(2,1)}), bf16[512,6144]{1,0:T(8,128)(2,1)}) %all-gather.15.cloned.1.call-update) | async-done | bytes 6291472 | tf_op jit(solution)/shard_map/all_gather | solution.py:53
  842.7 0.0 copy-done.1
  842.7 27.1 %convert_bitcast_fusion = bf16[3072,6144]{0,1:T(8,128)(2,1)} fusion(bf16[512,6144]{1,0:T(8,128)(2,1)} %all-gather.15.cloned.1.call-done, bf16[512,3072]{1,0:T(8,128)(2,1)S(1)} %copy-done.1), kind=kOutput, calls=%fused_computation | convolution fusion | flops 19346227200 | bytes 47185920 | tf_op jit(solution)/shard_map/dot_general | solution.py:24
  869.8 0.0 copy-start
  869.8 0.0 reduce-scatter.12.cloned.1.call-update
  869.8 0.2 reduce-scatter.14.cloned.1.call-start
  870.1 55.2 %all-gather.17.cloned.1.call-done = bf16[512,6144]{1,0:T(8,128)(2,1)} async-done(((bf16[256,6144]{1,0:T(8,128)(2,1)}), bf16[512,6144]{1,0:T(8,128)(2,1)}) %all-gather.17.cloned.1.call-update) | async-done | bytes 6291472 | tf_op jit(solution)/shard_map/all_gather | solution.py:52
  925.2 0.0 copy-done
  925.2 30.1 %convolution_convert_fusion = bf16[6144,3072]{1,0:T(8,128)(2,1)} fusion(bf16[512,6144]{1,0:T(8,128)(2,1)} %all-gather.17.cloned.1.call-done, bf16[512,3072]{1,0:T(8,128)(2,1)S(1)} %copy-done), kind=kOutput, calls=%fused_computation.1 | convolution fusion | flops 19346227200 | bytes 47185920 | tf_op jit(solution)/shard_map/dot_general | solution.py:24
  955.4 0.0 reduce-scatter.14.cloned.1.call-update
  955.4 0.0 reduce-scatter.10.cloned.1.call-start
  955.4 32.1 %convolution_convert_fusion.3 = bf16[512,3072]{1,0:T(8,128)(2,1)} fusion(bf16[512,6144]{1,0:T(8,128)(2,1)} %all-gather.15.cloned.1.call-done, bf16[3072,6144]{1,0:T(8,128)(2,1)} %all-gather.13.cloned.1.call-done), kind=kOutput, calls=%fused_computation.30 | convolution fusion | flops 19328925696 | bytes 47185920 | tf_op jit(solution)/shard_map/dot_general | solution.py:24
  987.6 0.0 reduce-scatter.10.cloned.1.call-update
  987.6 201.8 %reduce-scatter.12.cloned.1.call-done = bf16[3072,1536]{0,1:T(8,128)(2,1)} async-done(((bf16[3072,6144]{0,1:T(8,128)(2,1)}), bf16[3072,1536]{0,1:T(8,128)(2,1)}) %reduce-scatter.12.cloned.1.call-update) | async-done | bytes 9437200 | tf_op jit(solution)/shard_map/reduce_scatter | solution.py:60
  1189.4 9.1 fusion
  1198.6 255.0 %reduce-scatter.14.cloned.1.call-done = bf16[1536,3072]{1,0:T(8,128)(2,1)} async-done(((bf16[6144,3072]{1,0:T(8,128)(2,1)}), bf16[1536,3072]{1,0:T(8,128)(2,1)}) %reduce-scatter.14.cloned.1.call-update) | async-done | bytes 9437200 | tf_op jit(solution)/shard_map/reduce_scatter | solution.py:63
  1453.6 9.1 fusion.2
  1464.0 43.7 %psum.7 = f32[]{:T(128)} all-reduce(f32[]{:T(128)S(6)} %add.35), channel_id=1, replica_groups=mesh['gx'=4,'gy'=4,'gz'=2] {'gx','gy','gz'}, use_global_device_ids=true, to_apply=%region_7.0 | all-reduce | flops 1 | bytes 8 | tf_op jit(solution)/shard_map/psum | solution.py:68
  1508.5 10.0 fusion.1
  1518.5 12.6 copy.7
  1531.1 10.0 fusion.3
  (1 shorter events, 0.0 us)
Async XLA Ops:
  7.2 64.8 %all-gather.7.cloned.1.call-start = ((), (), s32[]{:S(2)}) async-start(), calls=%async_computation.5 | async-start | bytes 3932160 | tf_op jit(solution)/shard_map/all_gather | solution.py:32
  7.9 293.8 %all-gather.9.cloned.1.call-start = ((), (), s32[]{:S(2)}) async-start(), calls=%async_computation.6 | async-start | bytes 47185920 | tf_op jit(solution)/shard_map/all_gather | solution.py:36
  8.6 355.9 %all-gather.11.cloned.1.call-start = ((), (), s32[]{:S(2)}) async-start(), calls=%async_computation.8 | async-start | bytes 3932160 | tf_op jit(solution)/shard_map/all_gather | solution.py:31
  9.4 584.8 %all-gather.13.cloned.1.call-start = ((), (), s32[]{:S(2)}) async-start(), calls=%async_computation.9 | async-start | bytes 47185920 | tf_op jit(solution)/shard_map/all_gather | solution.py:35
  10.0 664.0 %reduce-scatter.6.cloned.1.call-start = ((), (), s32[]{:S(2)}) async-start(), calls=%async_computation.7 | async-start | bytes 9437184 | tf_op jit(solution)/shard_map/reduce_scatter | solution.py:44
  328.6 425.3 %reduce-scatter.8.cloned.1.call-start = ((), (), s32[]{:S(2)}) async-start(), calls=%async_computation.10 | async-start | bytes 9437184 | tf_op jit(solution)/shard_map/reduce_scatter | solution.py:41
  621.0 221.7 %all-gather.15.cloned.1.call-start = ((), (), s32[]{:S(2)}) async-start(), calls=%async_computation.11 | async-start | bytes 9437184 | tf_op jit(solution)/shard_map/all_gather | solution.py:53
  762.1 80.6 %copy-start.1 = (bf16[512,3072]{1,0:T(8,128)(2,1)S(1)}, bf16[512,3072]{1,0:T(8,128)(2,1)}, u32[]{:S(2)}) copy-start(bf16[512,3072]{1,0:T(8,128)(2,1)} %all-gather.11.cloned.1.call-done) | copy-start | bytes 9437188
  762.2 163.1 %all-gather.17.cloned.1.call-start = ((), (), s32[]{:S(2)}) async-start(), calls=%async_computation.14 | async-start | bytes 9437184 | tf_op jit(solution)/shard_map/all_gather | solution.py:52
  762.9 426.5 %reduce-scatter.12.cloned.1.call-start = ((), (), s32[]{:S(2)}) async-start(), calls=%async_computation.13 | async-start | bytes 47185920 | tf_op jit(solution)/shard_map/reduce_scatter | solution.py:60
  869.8 55.4 %copy-start = (bf16[512,3072]{1,0:T(8,128)(2,1)S(1)}, bf16[512,3072]{1,0:T(8,128)(2,1)}, u32[]{:S(2)}) copy-start(bf16[512,3072]{1,0:T(8,128)(2,1)} %all-gather.7.cloned.1.call-done) | copy-start | bytes 9437188
  869.8 583.8 %reduce-scatter.14.cloned.1.call-start = ((), (), s32[]{:S(2)}) async-start(), calls=%async_computation.15 | async-start | bytes 47185920 | tf_op jit(solution)/shard_map/reduce_scatter | solution.py:63
  955.4 585.7 %reduce-scatter.10.cloned.1.call-start = ((), (), s32[]{:S(2)}) async-start(), calls=%async_computation.12 | async-start | bytes 3932160 | tf_op jit(solution)/shard_map/reduce_scatter | solution.py:56
Sparse Core Ops, SparseCore 0:
  9.6 62.3 all-gather.6
  73.5 228.1 all-gather.8
  303.3 61.1 all-gather.10
  366.0 228.1 all-gather.12
  596.9 77.0 reduce-scatter.5
  676.8 77.0 reduce-scatter.7
  762.3 80.3 all-gather.14
  844.8 80.3 all-gather.16
  927.8 261.5 reduce-scatter.11
  1192.0 261.5 reduce-scatter.13
  1456.5 60.8 reduce-scatter.9
where the time goes:
time: 1560 us; the launch traced here: 1550 us
  waiting for transfers between devices  1280 us (82%)
  matrix products  143 us (9%)
  other arithmetic  46.5 us (3%)
  blocking collectives  43.7 us (3%)
  between operations  16.2 us (1%)
    reduce_scatter x1, waiting for transfers between devices, shards(): lax.psum_scatter(gout_term.astype(jnp.bfloat16), 'gy', scatter_dimension=...  255 us
    all_gather x1, waiting for transfers between devices, shards(): lax.all_gather(w_out, 'gy', axis=0, tiled=True)  230 us
    all_gather x1, waiting for transfers between devices, shards(): lax.all_gather(w_in, 'gy', axis=1, tiled=True)  230 us
    reduce_scatter x1, waiting for transfers between devices, shards(): lax.psum_scatter(gin_term.astype(jnp.bfloat16), 'gy', scatter_dimension=1...  202 us
    dot_general x5, matrix products, contract(): lax.dot_general(left, right, (((left_dim,), (right_dim,)), ((), ())), pre...  143 us
    reduce_scatter x1, waiting for transfers between devices, shards(): lax.psum_scatter(h_term.astype(jnp.bfloat16), 'gz', scatter_dimension=0,...  79.9 us
    all_gather x1, waiting for transfers between devices, shards(): lax.all_gather(d_pre, 'gz', axis=0, tiled=True)  79.7 us
    all_gather x1, waiting for transfers between devices, shards(): lax.all_gather(out_grad, 'gx', axis=0, tiled=True)  61.9 us
  transfers between devices with their start and end apart: 11, of which 10 were waited for; matrix products, arithmetic and copies ran while one was open for 13% of the time, Pallas kernels for 0%

commit v1 on v0

v1 whole, which is shorter than its diff:
```python
import jax
import jax.numpy as jnp
from jax import lax
from jax.experimental import pallas as pl
from jax.experimental.pallas import tpu as pltpu
from jax.sharding import PartitionSpec as P

GELU_C = 0.7978845608
MIB = 1 << 20
ANY = pl.BlockSpec(memory_space=pl.ANY)
HELD = pl.BlockSpec(memory_space=pltpu.VMEM)


def gelu_parts(values):
    inner_arg = GELU_C * (values + 0.044715 * values * values * values)
    tanh_val = jnp.tanh(inner_arg)
    value_out = 0.5 * values * (1.0 + tanh_val)
    slope = 0.5 * (1.0 + tanh_val) + 0.5 * values * (1.0 - tanh_val * tanh_val) * GELU_C * (
        1.0 + 3.0 * 0.044715 * values * values
    )
    return (value_out, slope)


def contract(left, right, left_dim, right_dim):
    return lax.dot_general(
        left, right, (((left_dim,), (right_dim,)), ((), ())), preferred_element_type=jnp.float32
    )


def tile_of(extent, most):
    size = most
    while extent % size:
        size //= 2
    return size


def stacked(refs):
    return jnp.concatenate([ref[...] for ref in refs], axis=0) if len(refs) > 1 else refs[0][...]


def params(mib):
    return pltpu.CompilerParams(vmem_limit_bytes=mib * MIB)


def flip_call(weight, after):
    rows, cols = weight.shape
    tile = tile_of(cols, 256)

    def kernel(in_ref, *refs):
        refs[-1][...] = in_ref[...].T

    return pl.pallas_call(
        kernel,
        grid=(cols // tile,),
        in_specs=[pl.BlockSpec((rows, tile), lambda i: (0, i))] + [ANY] * len(after),
        out_specs=pl.BlockSpec((tile, rows), lambda i: (i, 0)),
        out_shape=jax.ShapeDtypeStruct((cols, rows), weight.dtype),
        compiler_params=params(16),
        name="flip",
    )(weight, *after)


def terms_call(blocks, w_in, w_out, after, held):
    hidden, depth = w_out.shape
    rows = blocks[0].shape[0] // 2
    count = len(blocks)
    tile = tile_of(hidden, 768 if held else 384)
    steps = hidden // tile

    def kernel(*refs):
        x_refs, dy_refs = refs[:count], refs[count : 2 * count]
        w_in_ref, w_out_ref = refs[2 * count : 2 * count + 2]
        out_ref = refs[-1]
        step = pl.program_id(0)

        @pl.when(step < steps)
        def _():
            at = pl.ds(pl.multiple_of(step * tile, tile), tile) if held else slice(None)
            out_ref[...] = contract(w_in_ref[at, :], stacked(x_refs), 1, 1).astype(jnp.bfloat16)

        @pl.when(step >= steps)
        def _():
            at = pl.ds(pl.multiple_of((step - steps) * tile, tile), tile) if held else slice(None)
            out_ref[...] = contract(w_out_ref[at, :], stacked(dy_refs), 1, 1).astype(jnp.bfloat16)

    w_specs = [HELD, HELD]
    if not held:
        w_specs = [
            pl.BlockSpec((tile, depth), lambda i: (jnp.minimum(i, steps - 1), 0)),
            pl.BlockSpec((tile, depth), lambda i: (jnp.maximum(i - steps, 0), 0)),
        ]
    return pl.pallas_call(
        kernel,
        grid=(2 * steps,),
        in_specs=[pl.BlockSpec((rows, depth), lambda i: (0, 0))] * count
        + [pl.BlockSpec((rows, depth), lambda i: (1, 0))] * count
        + w_specs
        + [ANY] * len(after),
        out_specs=pl.BlockSpec((tile, count * rows), lambda i: (i, 0)),
        out_shape=jax.ShapeDtypeStruct((2 * hidden, count * rows), jnp.bfloat16),
        compiler_params=params(12 if held else 24),
        name="terms",
    )(*blocks, *blocks, w_in, w_out, *after)


def half_call(blocks, part, weight, weight_dim, after):
    depth, hidden = weight.shape[weight_dim], weight.shape[1 - weight_dim]
    rows = blocks[0].shape[0] // 2
    count = len(blocks)
    tile = tile_of(hidden, 384)

    def kernel(*refs):
        value = contract(refs[count][...], stacked(refs[:count]), weight_dim, 1)
        refs[-1][...] = value.astype(jnp.bfloat16)

    return pl.pallas_call(
        kernel,
        grid=(hidden // tile,),
        in_specs=[pl.BlockSpec((rows, depth), lambda i: (part, 0))] * count
        + [
            pl.BlockSpec((tile, depth), lambda i: (i, 0))
            if weight_dim
            else pl.BlockSpec((depth, tile), lambda i: (0, i))
        ]
        + [ANY] * len(after),
        out_specs=pl.BlockSpec((tile, count * rows), lambda i: (i, 0)),
        out_shape=jax.ShapeDtypeStruct((hidden, count * rows), jnp.bfloat16),
        compiler_params=params(16),
        name="half_terms",
    )(*blocks, weight, *after)


def gelu_call(h_terms, d_terms, w_in, after, w_held, with_dx):
    depth, hidden = w_in.shape
    cols = h_terms[0].shape[1]
    count = len(h_terms)
    row_tile = tile_of(hidden, 384)
    row_steps = hidden // row_tile
    tile = tile_of(depth, 768)
    steps = depth // tile if with_dx else 0
    part = cols // 2

    def kernel(*refs):
        h_refs, d_refs = refs[:count], refs[count : 2 * count]
        w_ref = refs[2 * count]
        outs = refs[2 * count + 1 + len(after) :]
        act_ref, d_pre_ref = outs[:2]
        step = pl.program_id(0)

        @pl.when(step < row_steps)
        def _():
            pre_act = sum(ref[...].astype(jnp.float32) for ref in h_refs)
            d_act = sum(ref[...].astype(jnp.float32) for ref in d_refs)
            value_out, slope = gelu_parts(pre_act)
            d_pre = (d_act * slope).astype(jnp.bfloat16)
            act_ref[...] = value_out.astype(jnp.bfloat16)
            d_pre_ref[...] = d_pre
            if with_dx:
                outs[-1][pl.ds(pl.multiple_of(step * row_tile, row_tile), row_tile), :] = d_pre

        if with_dx:

            @pl.when(step >= row_steps)
            def _():
                at = pl.multiple_of((step - row_steps) * tile, tile)
                left = w_ref[pl.ds(at, tile), :] if w_held else w_ref[...]
                value = contract(left, outs[-1][...], 1, 0).astype(jnp.bfloat16)
                outs[2][...] = value[:, :part]
                outs[3][...] = value[:, part:]

    low = lambda i: (jnp.minimum(i, row_steps - 1), 0)
    d_from = (d_terms[0].shape[0] - hidden) // row_tile
    high = lambda i: (jnp.minimum(i, row_steps - 1) + d_from, 0)
    h_spec, d_spec = pl.BlockSpec((row_tile, cols), low), pl.BlockSpec((row_tile, cols), high)
    shape = jax.ShapeDtypeStruct((hidden, cols), jnp.bfloat16)
    dx_spec = pl.BlockSpec((tile, part), lambda i: (jnp.maximum(i - row_steps, 0), 0))
    w_spec = pl.BlockSpec((tile, hidden), lambda i: (jnp.maximum(i - row_steps, 0), 0))
    if w_held or not with_dx:
        w_spec = HELD if with_dx else ANY
    dx_shape = jax.ShapeDtypeStruct((depth, part), jnp.bfloat16)
    return pl.pallas_call(
        kernel,
        grid=(row_steps + steps,),
        in_specs=[h_spec] * count + [d_spec] * count + [w_spec] + [ANY] * len(after),
        out_specs=[h_spec, h_spec] + [dx_spec, dx_spec] * with_dx,
        out_shape=[shape, shape] + [dx_shape, dx_shape] * with_dx,
        scratch_shapes=[pltpu.VMEM((hidden, cols), jnp.bfloat16)] * with_dx,
        compiler_params=params(12 if w_held else 20),
        name="gelu",
    )(*h_terms, *d_terms, w_in, *after)


def dx_call(d_pre, w_in, after):
    depth, hidden = w_in.shape
    cols = d_pre.shape[1]
    tile = tile_of(depth, 768)
    part = cols // 2

    def kernel(d_pre_ref, w_ref, *refs):
        value = contract(w_ref[...], d_pre_ref[...], 1, 0).astype(jnp.bfloat16)
        refs[-2][...] = value[:, :part]
        refs[-1][...] = value[:, part:]

    return pl.pallas_call(
        kernel,
        grid=(depth // tile,),
        in_specs=[
            pl.BlockSpec((hidden, cols), lambda i: (0, 0)),
            pl.BlockSpec((tile, hidden), lambda i: (i, 0)),
        ]
        + [ANY] * len(after),
        out_specs=[pl.BlockSpec((tile, part), lambda i: (i, 0))] * 2,
        out_shape=[jax.ShapeDtypeStruct((depth, part), jnp.bfloat16)] * 2,
        compiler_params=params(20),
        name="dx",
    )(d_pre, w_in, *after)


def grad_call(lefts, rights, right_at, base, after, square):
    rows, depth = lefts[0].shape
    part, cols = rights[0].shape[0] // 2, rights[0].shape[1]
    tile = tile_of(cols, 512)
    n_left, n_right = len(lefts), len(rights)
    based = base is not None

    def kernel(*refs):
        left, right = refs[:n_left], refs[n_left : n_left + n_right]
        outs = refs[n_left + n_right + int(based) + len(after) :]
        total = contract(
            jnp.concatenate([ref[...] for ref in left], axis=1) if n_left > 1 else left[0][...],
            stacked(right),
            1,
            0,
        )
        if based:
            total = total + refs[n_left + n_right][...].astype(jnp.float32)
        outs[0][...] = total.astype(jnp.bfloat16)
        if square:

            @pl.when(pl.program_id(0) == 0)
            def _():
                outs[1][...] = jnp.zeros_like(outs[1])

            outs[1][...] += jnp.sum((total * total).reshape(rows // 8, 8, tile), axis=0)

    tile_spec = pl.BlockSpec((rows, tile), lambda i: (0, i))
    out_specs = [tile_spec]
    out_shape = [jax.ShapeDtypeStruct((rows, cols), jnp.bfloat16)]
    if square:
        out_specs.append(pl.BlockSpec((8, tile), lambda i: (0, 0)))
        out_shape.append(jax.ShapeDtypeStruct((8, tile), jnp.float32))
    return pl.pallas_call(
        kernel,
        grid=(cols // tile,),
        in_specs=[pl.BlockSpec((rows, depth), lambda i: (0, 0))] * n_left
        + [pl.BlockSpec((part, tile), lambda i: (right_at, i))] * n_right
        + [tile_spec] * int(based)
        + [ANY] * len(after),
        out_specs=out_specs,
        out_shape=out_shape,
        compiler_params=params(40),
        name="grad",
    )(*lefts, *rights, *([base] if based else []), *after)


def scale_call(factor, grad, flip):
    rows, cols = grad.shape
    tile = tile_of(cols if flip else rows, 256)

    def kernel(factor_ref, in_ref, out_ref):
        value = (in_ref[...].astype(jnp.float32) * factor_ref[0, 0]).astype(jnp.bfloat16)
        out_ref[...] = value.T if flip else value

    return pl.pallas_call(
        kernel,
        grid=((cols if flip else rows) // tile,),
        in_specs=[
            pl.BlockSpec(memory_space=pltpu.SMEM),
            pl.BlockSpec((rows, tile), lambda i: (0, i))
            if flip
            else pl.BlockSpec((tile, cols), lambda i: (i, 0)),
        ],
        out_specs=pl.BlockSpec((tile, rows if flip else cols), lambda i: (i, 0)),
        out_shape=jax.ShapeDtypeStruct((cols, rows) if flip else (rows, cols), jnp.bfloat16),
        compiler_params=params(40),
        name="scale",
    )(factor.reshape(1, 1), grad)


def solution(mesh):
    n_gx, n_gy, n_gz = mesh.shape["gx"], mesh.shape["gy"], mesh.shape["gz"]

    def swap(value, mask):
        return lax.ppermute(value, "gy", [(i, i ^ mask) for i in range(n_gy)])

    def shift(value, axis, size, step):
        return lax.ppermute(value, axis, [(i, (i + step) % size) for i in range(size)])

    def over_gx(value):
        return value + sum(shift(value, "gx", n_gx, step) for step in range(1, n_gx))

    def over_gy_gz(value):
        value = value + sum(swap(value, mask) for mask in range(1, n_gy))
        return value + sum(shift(value, "gz", n_gz, step) for step in range(1, n_gz))

    def width_terms(value):
        if n_gz == 2:
            return [value, shift(value, "gz", n_gz, 1)]
        every = lax.all_gather(value, "gz")
        return [every[i] for i in range(n_gz)]

    pairs = range(0, n_gy, 2)
    leads = [(pair, step) for step in range(min(n_gx, 2)) for pair in pairs]
    leads += [(pair, step) for step in range(2, n_gx) for pair in reversed(pairs)]
    groups = [[(mask, step), (mask + 1, step)] for mask, step in leads]
    count = len(groups)
    last = count - 1
    own_tie = {last - 3: ("gin", 0), last - 2: ("gout", 0), last - 1: ("gout", 1)}
    far_tie = {last - 3: ("terms", last)}

    def shards(tokens, w_in, w_out, out_grad):
        hidden = w_in.shape[1]
        blocks = {(0, 0): jnp.concatenate([tokens, out_grad], axis=0)}
        done = ()
        terms, acts, d_pres, ties = {}, {}, {}, {}
        sums, returned = {}, []

        def later(value, *extra):
            waits = done + extra
            return lax.optimization_barrier((value, waits))[0] if waits else value

        def fetch(block, *extra):
            mask, step = block
            if mask % 2:
                blocks[block] = swap(later(blocks[mask - 1, step], *extra), 1)
            elif mask:
                blocks[block] = swap(later(blocks[0, step], *extra), mask)
            else:
                blocks[block] = shift(later(blocks[0, step - 1], *extra), "gx", n_gx, -1)

        def tie(kernel, value):
            ties.setdefault(kernel, []).append(value)

        def waits(kernel):
            return done + tuple(ties.pop(kernel, ()))

        def run_terms(g):
            nonlocal done
            blocks_of = [blocks[b] for b in groups[g]]
            value = terms_call(blocks_of, w_in_t, w_out, waits(("terms", g)), g < last)
            done = (value,)
            terms[g] = (width_terms(value),) * 2

        def plus(one, two):
            return (one.astype(jnp.float32) + two.astype(jnp.float32)).astype(jnp.bfloat16)

        def give_back(g, dx):
            pair, step = leads[g]
            sums[pair, step] = plus(dx[0], swap(dx[1], 1))
            if g < last:
                tie(own_tie.get(g, ("gelu", g + 1)), sums[pair, step])
            if pair:
                sums[pair, step] = swap(sums[pair, step], pair)
                if g < last - 1:
                    tie(far_tie.get(g, ("gelu", g + 3 - (g > 1))), sums[pair, step])
            if g < last and all((p, step) in sums for p in pairs):
                finish(step)
                if step:
                    tie(("gelu", g + 3) if g + 3 < last else ("gin", 2), returned[-1])

        def finish(step):
            total = sums[0, step]
            for p in pairs[1:]:
                total = plus(total, later(sums[p, step]) if step == n_gx - 1 else sums[p, step])
            returned.append(shift(total, "gx", n_gx, step) if step else total)

        def run_gelu(g):
            nonlocal done
            outs = gelu_call(*terms[g], w_in, waits(("gelu", g)), g < last - 2, g < last)
            acts[g], d_pres[g] = outs[:2]
            done = (outs[0],)
            if g < last:
                give_back(g, outs[2:])

        def run_grads(begin, end, name, stage, base=None):
            nonlocal done
            lefts = [(acts if name == "gout" else d_pres)[g] for g in range(begin, end)]
            rights = [blocks[b] for g in range(begin, end) for b in groups[g]]
            after = waits((name, stage))
            outs = grad_call(lefts, rights, int(name == "gout"), base, after, stage == 2)
            done = (outs[0],)
            return outs

        fetch((1, 0))
        for pair in pairs[1:]:
            fetch((pair, 0))
        fetch((0, 1))
        first = [blocks[b] for b in groups[0]]
        h_own = half_call(first, 0, w_in, 0, done)
        d_own = half_call(first, 1, w_out, 1, (h_own,))
        h_terms = width_terms(h_own)
        most = 3 * hidden // 4
        d_parts = [width_terms(d_own[:most]), width_terms(d_own[most:])]
        w_in_t = flip_call(w_in, (d_own,))
        done = (w_in_t,)
        early = (h_terms[-1], d_parts[0][-1], blocks[0, 1])
        for pair in pairs[1:]:
            fetch((pair + 1, 0), *early)
        tie(("terms", 1), blocks[0, 1])

        def next_turn(turn):
            if turn + 1 < n_gx:
                fetch((0, turn + 1))
                tie(("gelu", turn), blocks[0, turn + 1])
            if turn < n_gx:
                for pair in pairs[1:]:
                    fetch((pair, turn))
                    tie(("gelu", turn), blocks[pair, turn])
                fetch((1, turn))
            if turn > 1:
                for pair in pairs[1:]:
                    fetch((pair + 1, turn - 1))

        next_turn(1)
        for g in range(1, count):
            run_terms(g)
            if 1 < g <= n_gx:
                next_turn(g)
            if g == 1:
                others = [[later(v) for v in part[-max(1, len(part) * (n_gz > 2)) :]] for part in d_parts]
                d_terms = [jnp.concatenate(both, axis=0) for both in zip(*others)]
                terms[0] = h_terms, d_terms if n_gz > 2 else [d_own] + d_terms
            if g == last - 1:
                gin = run_grads(0, last - 2, "gin", 0)
            if g == last:
                gout = run_grads(0, last - 2, "gout", 0)
            run_gelu(g - 1)
        gin = run_grads(last - 2, last, "gin", 1, gin[0])
        gout = run_grads(last - 2, last, "gout", 1, gout[0])
        run_gelu(last)
        gin = run_grads(last, count, "gin", 2, gin[0])
        gout = run_grads(last, count, "gout", 2, gout[0])

        square = over_gx(jnp.broadcast_to(jnp.sum(gin[1]) + jnp.sum(gout[1]), (8, 128)))
        give_back(last, dx_call(d_pres[last], w_in, (square,)))
        finish(n_gx - 1)
        square = over_gy_gz(square)[0, 0]
        in_grad = sum(piece.astype(jnp.float32) for piece in returned).astype(jnp.bfloat16).T

        entries = 2.0 * (w_in.shape[0] * n_gz) * (w_in.shape[1] * n_gx * n_gy)
        factor = 1.0 / jnp.sqrt(square / entries + 1e-06)
        return in_grad, scale_call(factor, gin[0], True), scale_call(factor, gout[0], False)

    placed = (
        P(("gy", "gx"), "gz"),
        P("gz", ("gx", "gy")),
        P(("gx", "gy"), "gz"),
        P(("gy", "gx"), "gz"),
    )
    return jax.shard_map(
        shards,
        mesh=mesh,
        in_specs=placed,
        out_specs=(P(("gy", "gx"), "gz"), P("gz", ("gx", "gy")), P(("gx", "gy"), "gz")),
        check_vma=False,
    )
```

time: 1560 us -> 416 us (0.27)
  waiting for transfers between devices: 1280 us -> 113 us
  Pallas kernels: 0 us -> 188 us
  matrix products: 143 us -> 0 us
  local copies, waits for them, and re-layouts: 12.6 us -> 57.4 us
  blocking collectives: 43.7 us -> 0 us
  starting transfers between devices: 1.13 us -> 40.8 us
  other arithmetic: 46.5 us -> 10.9 us
    all_gather x6 -> x0, waiting for transfers between devices: 692 us -> none  [the longest x1 230 us: shards(): lax.all_gather(w_out, 'gy', axis=0, tiled=True)]
    reduce_scatter x5 -> x0, waiting for transfers between devices: 589 us -> none  [the longest x1 255 us: shards(): lax.psum_scatter(gout_term.astype(jnp.bfloat16), 'gy', scatter_dimension=...]
    pallas_call x0 -> x27, Pallas kernels: none -> 188 us  [the longest x6 73.6 us: grad_call(): pl.pallas_call(kernel, grid=(cols // tile,), in_specs=[pl.BlockSpec((rows...]
    dot_general x5 -> x0, matrix products: 143 us -> none  [contract(): lax.dot_general(left, right, (((left_dim,), (right_dim,)), ((), ())), pre...]
    ppermute x0 -> x47, waiting for transfers between devices: none -> 113 us  [the longest x27 63.9 us: swap(): return lax.ppermute(value, 'gy', [(i, i ^ mask) for i in range(n_gy)])]
    unnamed x5 -> x202, local copies, waits for them, and re-layouts: 12.6 us -> 56.7 us
    psum x1 -> x0, blocking collectives: 43.7 us -> none  [shards(): grand_total = lax.psum(local_square, ('gx', 'gy', 'gz'))]
    ppermute x0 -> x47, starting transfers between devices: none -> 40.8 us  [the longest x20 26.8 us: shift(): lax.ppermute(value, axis, [(i, (i + step) % size) for i in range(size)])]
  transfers between devices with their start and end apart: 11 -> 47, of which waited for: 10 -> 18; matrix products, arithmetic and copies ran while one was open for 13% -> 2% of each run, Pallas kernels for 0% -> 41%
where the time goes in v1:
time: 416 us; the launch traced here: 413 us
  Pallas kernels  188 us (45%)
  waiting for transfers between devices  113 us (27%)
  local copies, waits for them, and re-layouts  57.4 us (14%)
  starting transfers between devices  40.8 us (10%)
  other arithmetic  10.9 us (3%)
    pallas_call x6, Pallas kernels, grad_call(): pl.pallas_call(kernel, grid=(cols // tile,), in_specs=[pl.BlockSpec((rows...  73.6 us
    ppermute x27, waiting for transfers between devices, swap(): return lax.ppermute(value, 'gy', [(i, i ^ mask) for i in range(n_gy)])  63.9 us
    unnamed x202, local copies, waits for them, and re-layouts  56.7 us
    ppermute x20, waiting for transfers between devices, shift(): lax.ppermute(value, axis, [(i, (i + step) % size) for i in range(size)])  48.8 us
    pallas_call x7, Pallas kernels, terms_call(): pl.pallas_call(kernel, grid=(2 * steps,), in_specs=[pl.BlockSpec((rows, d...  45.2 us
    pallas_call x8, Pallas kernels, gelu_call(): pl.pallas_call(kernel, grid=(row_steps + steps,), in_specs=[h_spec] * cou...  41.8 us
    ppermute x20, starting transfers between devices, shift(): lax.ppermute(value, axis, [(i, (i + step) % size) for i in range(size)])  26.8 us
    ppermute x27, starting transfers between devices, swap(): return lax.ppermute(value, 'gy', [(i, i ^ mask) for i in range(n_gy)])  14 us
  transfers between devices with their start and end apart: 47, of which 18 were waited for; matrix products, arithmetic and copies ran while one was open for 2% of the time, Pallas kernels for 41%

profile of v1, /device:TPU:8, one launch (start us, length us, event | category | flops | bytes accessed | tf_op | source)
XLA Modules:
  0.0 413.1 jit_solution(15213579095567844152)
XLA Ops:
  5.5 3.7 copy-done
  9.2 4.3 %half_terms.2.refs_3_.refs_0_ = bf16[1536,256]{1,0:T(8,128)(2,1)S(1)} custom-call(bf16[256,3072]{1,0:T(8,128)(2,1)S(1)} %constant_dynamic-update-slice_fusion.refs_0_.refs_5_, bf16[256,3072]{1,0:T(8,128)(2,1)S(1)} %collective-permute-done.refs_1_.refs_6_, bf16[3072,1536]{1,0:T(8,128)(2,1)S(1)} %copy-done), custom_call_target="tpu_custom_call" | custom-call | tf_op jit(solution)/shard_map/half_terms/pallas_call | solution.py:116
  15.2 3.7 copy-done.4
  22.8 3.6 flip.1.refs_4_.refs_6_
  26.4 12.5 %collective-permute-done.4.refs_7_.refs_0_.refs_2_.refs_9_ = bf16[256,3072]{1,0:T(8,128)(2,1)S(1)} collective-permute-done((bf16[256,3072]{1,0:T(8,128)(2,1)S(1)}, bf16[256,3072]{1,0:T(8,128)(2,1)S(1)}, u32[]{:S(2)}, u32[]{:S(2)}) %collective-permute-start.4) | collective-permute-done | bytes 1572896 | tf_op jit(solution)/shard_map/ppermute | solution.py:297
  39.0 6.9 %collective-permute-done.2 = bf16[1152,256]{1,0:T(8,128)(2,1)S(1)} collective-permute-done((bf16[1152,256]{1,0:T(8,128)(2,1)S(1)}, bf16[1152,256]{1,0:T(8,128)(2,1)S(1)}, u32[]{:S(2)}, u32[]{:S(2)}) %collective-permute-start.2) | collective-permute-done | bytes 589856 | tf_op jit(solution)/shard_map/ppermute | solution.py:297
  50.5 5.7 %terms.7.refs_5_.refs_0_.refs_2_ = bf16[3072,256]{1,0:T(8,128)(2,1)S(1)} custom-call(bf16[256,3072]{1,0:T(8,128)(2,1)S(1)} %collective-permute-done.3.refs_0_.refs_2_.refs_7_, bf16[256,3072]{1,0:T(8,128)(2,1)S(1)} %collective-permute-done.5.refs_1_.refs_3_.refs_8_, bf16[256,3072]{1,0:T(8,128)(2,1)S(1)} %collective-permute-done.3.refs_0_.refs_2_.refs_7_, ...), custom_call_target="tpu_custom_call" | custom-call | tf_op jit(solution)/shard_map/terms/pallas_call | solution.py:92
  56.9 4.7 %gelu.8 = (bf16[1536,256]{1,0:T(8,128)(2,1)S(1)}, bf16[1536,256]{1,0:T(8,128)(2,1)S(1)}, bf16[3072,128]{1,0:T(8,128)(2,1)S(1)}, bf16[3072,128]{1,0:T(8,128)(2,1)S(1)}) custom-call(bf16[1536,256]{1,0:T(8,128)(2,1)S(1)} %half_terms.2.refs_3_.refs_0_, bf16[1536,256]{1,0:T(8,128)(2,1)S(1)} %collective-permute-done.1.refs_1_, ...), custom_call_target="tpu_custom_call" | custom-call | tf_op jit(solution)/shard_map/gelu/pallas_call | solution.py:181
  61.7 4.7 %copy-done.5 = bf16[1536,3072]{1,0:T(8,128)(2,1)S(1)} copy-done((bf16[1536,3072]{1,0:T(8,128)(2,1)S(1)}, bf16[1536,3072]{1,0:T(8,128)(2,1)}, u32[]{:S(2)}) %copy-start.5) | copy-done | bytes 9437208
  66.4 5.7 %terms.8.refs_5_.refs_0_.refs_2_ = bf16[3072,256]{1,0:T(8,128)(2,1)S(1)} custom-call(bf16[256,3072]{1,0:T(8,128)(2,1)S(1)} %collective-permute-done.4.refs_7_.refs_0_.refs_2_.refs_9_, bf16[256,3072]{1,0:T(8,128)(2,1)S(1)} %collective-permute-done.9.refs_1_.refs_3_.refs_10_, bf16[256,3072]{1,0:T(8,128)(2,1)S(1)} %collective-permute-done.4.refs_7_.refs_0_.refs_2_.refs_9_, ...), custom_call_target="tpu_custom_call" | custom-call | tf_op jit(solution)/shard_map/terms/pallas_call | solution.py:92
  72.2 10.5 %collective-permute-done.11.refs_7_.refs_0_.refs_2_.refs_11_ = bf16[256,3072]{1,0:T(8,128)(2,1)S(1)} collective-permute-done((bf16[256,3072]{1,0:T(8,128)(2,1)S(1)}, bf16[256,3072]{1,0:T(8,128)(2,1)S(1)}, u32[]{:S(2)}, u32[]{:S(2)}) %collective-permute-start.11) | collective-permute-done | bytes 1572896 | tf_op jit(solution)/shard_map/ppermute | solution.py:294
  88.1 5.5 %collective-permute-done.8.refs_1_.refs_3_ = bf16[3072,256]{1,0:T(8,128)(2,1)S(1)} collective-permute-done((bf16[3072,256]{1,0:T(8,128)(2,1)S(1)}, bf16[3072,256]{1,0:T(8,128)(2,1)S(1)}, u32[]{:S(2)}, u32[]{:S(2)}) %collective-permute-start.8) | collective-permute-done | bytes 1572896 | tf_op jit(solution)/shard_map/ppermute | solution.py:297
  93.6 4.7 %gelu.9 = (bf16[1536,256]{1,0:T(8,128)(2,1)S(1)}, bf16[1536,256]{1,0:T(8,128)(2,1)S(1)}, bf16[3072,128]{1,0:T(8,128)(2,1)S(1)}, bf16[3072,128]{1,0:T(8,128)(2,1)S(1)}) custom-call(bf16[3072,256]{1,0:T(8,128)(2,1)S(1)} %terms.7.refs_5_.refs_0_.refs_2_, bf16[3072,256]{1,0:T(8,128)(2,1)S(1)} %collective-permute-done.8.refs_1_.refs_3_, ...), custom_call_target="tpu_custom_call" | custom-call | tf_op jit(solution)/shard_map/gelu/pallas_call | solution.py:181
  99.3 5.7 %terms.9.refs_5_.refs_0_.refs_2_ = bf16[3072,256]{1,0:T(8,128)(2,1)S(1)} custom-call(bf16[256,3072]{1,0:T(8,128)(2,1)S(1)} %collective-permute-done.11.refs_7_.refs_0_.refs_2_.refs_11_, bf16[256,3072]{1,0:T(8,128)(2,1)S(1)} %collective-permute-done.15.refs_1_.refs_3_.refs_12_, bf16[256,3072]{1,0:T(8,128)(2,1)S(1)} %collective-permute-done.11.refs_7_.refs_0_.refs_2_.refs_11_, ...), custom_call_target="tpu_custom_call" | custom-call | tf_op jit(solution)/shard_map/terms/pallas_call | solution.py:92
  105.1 14.4 %collective-permute-done.17.refs_7_.refs_0_.refs_2_.refs_13_ = bf16[256,3072]{1,0:T(8,128)(2,1)S(1)} collective-permute-done((bf16[256,3072]{1,0:T(8,128)(2,1)S(1)}, bf16[256,3072]{1,0:T(8,128)(2,1)S(1)}, u32[]{:S(2)}, u32[]{:S(2)}) %collective-permute-start.17) | collective-permute-done | bytes 1572896 | tf_op jit(solution)/shard_map/ppermute | solution.py:294
  122.8 4.6 %collective-permute-done.14.refs_1_.refs_3_ = bf16[3072,256]{1,0:T(8,128)(2,1)S(1)} collective-permute-done((bf16[3072,256]{1,0:T(8,128)(2,1)S(1)}, bf16[3072,256]{1,0:T(8,128)(2,1)S(1)}, u32[]{:S(2)}, u32[]{:S(2)}) %collective-permute-start.14) | collective-permute-done | bytes 1572896 | tf_op jit(solution)/shard_map/ppermute | solution.py:297
  127.3 4.7 %gelu.10 = (bf16[1536,256]{1,0:T(8,128)(2,1)S(1)}, bf16[1536,256]{1,0:T(8,128)(2,1)S(1)}, bf16[3072,128]{1,0:T(8,128)(2,1)S(1)}, bf16[3072,128]{1,0:T(8,128)(2,1)S(1)}) custom-call(bf16[3072,256]{1,0:T(8,128)(2,1)S(1)} %terms.8.refs_5_.refs_0_.refs_2_, bf16[3072,256]{1,0:T(8,128)(2,1)S(1)} %collective-permute-done.14.refs_1_.refs_3_, ...), custom_call_target="tpu_custom_call" | custom-call | tf_op jit(solution)/shard_map/gelu/pallas_call | solution.py:181
  133.5 5.7 %terms.10.refs_5_.refs_0_.refs_2_ = bf16[3072,256]{1,0:T(8,128)(2,1)S(1)} custom-call(bf16[256,3072]{1,0:T(8,128)(2,1)S(1)} %collective-permute-done.17.refs_7_.refs_0_.refs_2_.refs_13_, bf16[256,3072]{1,0:T(8,128)(2,1)S(1)} %collective-permute-done.20.refs_1_.refs_3_.refs_14_, ...), custom_call_target="tpu_custom_call" | custom-call | tf_op jit(solution)/shard_map/terms/pallas_call | solution.py:92
  140.0 17.7 %collective-permute-done.21.refs_6_.refs_0_.refs_2_.refs_4_ = bf16[256,3072]{1,0:T(8,128)(2,1)S(1)} collective-permute-done((bf16[256,3072]{1,0:T(8,128)(2,1)}, bf16[256,3072]{1,0:T(8,128)(2,1)S(1)}, u32[]{:S(2)}, u32[]{:S(2)}) %collective-permute-start.21) | collective-permute-done | bytes 1572896 | tf_op jit(solution)/shard_map/ppermute | solution.py:294
  157.8 3.3 collective-permute-done.19.refs_1_.refs_3_
  161.0 4.7 %gelu.11 = (bf16[1536,256]{1,0:T(8,128)(2,1)S(1)}, bf16[1536,256]{1,0:T(8,128)(2,1)S(1)}, bf16[3072,128]{1,0:T(8,128)(2,1)S(1)}, bf16[3072,128]{1,0:T(8,128)(2,1)S(1)}) custom-call(bf16[3072,256]{1,0:T(8,128)(2,1)S(1)} %terms.9.refs_5_.refs_0_.refs_2_, bf16[3072,256]{1,0:T(8,128)(2,1)S(1)} %collective-permute-done.19.refs_1_.refs_3_, ...), custom_call_target="tpu_custom_call" | custom-call | tf_op jit(solution)/shard_map/gelu/pallas_call | solution.py:181
  167.6 6.5 %terms.11.refs_5_.refs_0_.refs_2_ = bf16[3072,256]{1,0:T(8,128)(2,1)} custom-call(bf16[256,3072]{1,0:T(8,128)(2,1)S(1)} %collective-permute-done.10.refs_6_.refs_0_.refs_2_, bf16[256,3072]{1,0:T(8,128)(2,1)S(1)} %collective-permute-done.25.refs_1_.refs_3_, bf16[256,3072]{1,0:T(8,128)(2,1)S(1)} %collective-permute-done.10.refs_6_.refs_0_.refs_2_, ...), custom_call_target="tpu_custom_call" | custom-call | tf_op jit(solution)/shard_map/terms/pallas_call | solution.py:92
  175.8 10.1 %collective-permute-done.13.refs_6_ = bf16[3072,128]{1,0:T(8,128)(2,1)S(1)} collective-permute-done((bf16[3072,128]{1,0:T(8,128)(2,1)S(1)}, bf16[3072,128]{1,0:T(8,128)(2,1)S(1)}, u32[]{:S(2)}, u32[]{:S(2)}) %collective-permute-start.13) | collective-permute-done | bytes 786464 | tf_op jit(solution)/shard_map/ppermute | solution.py:294
  185.8 8.9 %collective-permute-done.27.refs_1_.refs_3_ = bf16[3072,256]{1,0:T(8,128)(2,1)S(1)} collective-permute-done((bf16[3072,256]{1,0:T(8,128)(2,1)S(1)}, bf16[3072,256]{1,0:T(8,128)(2,1)S(1)}, u32[]{:S(2)}, u32[]{:S(2)}) %collective-permute-start.27) | collective-permute-done | bytes 1572896 | tf_op jit(solution)/shard_map/ppermute | solution.py:297
  194.8 4.7 %gelu.12 = (bf16[1536,256]{1,0:T(8,128)(2,1)S(1)}, bf16[1536,256]{1,0:T(8,128)(2,1)S(1)}, bf16[3072,128]{1,0:T(8,128)(2,1)S(1)}, bf16[3072,128]{1,0:T(8,128)(2,1)S(1)}) custom-call(bf16[3072,256]{1,0:T(8,128)(2,1)S(1)} %terms.10.refs_5_.refs_0_.refs_2_, bf16[3072,256]{1,0:T(8,128)(2,1)S(1)} %collective-permute-done.27.refs_1_.refs_3_, ...), custom_call_target="tpu_custom_call" | custom-call | tf_op jit(solution)/shard_map/gelu/pallas_call | solution.py:181
  201.6 6.5 %terms.12.refs_15_.refs_0_.refs_2_ = bf16[3072,256]{1,0:T(8,128)(2,1)} custom-call(bf16[256,3072]{1,0:T(8,128)(2,1)S(1)} %collective-permute-done.21.refs_6_.refs_0_.refs_2_.refs_4_, bf16[256,3072]{1,0:T(8,128)(2,1)S(1)} %collective-permute-done.28.refs_1_.refs_3_.refs_5_, bf16[256,3072]{1,0:T(8,128)(2,1)S(1)} %collective-permute-done.21.refs_6_.refs_0_.refs_2_.refs_4_, ...), custom_call_target="tpu_custom_call" | custom-call | tf_op jit(solution)/shard_map/terms/pallas_call | solution.py:92
  216.0 16.0 %grad.6.refs_5_.refs_6_ = bf16[1536,3072]{1,0:T(8,128)(2,1)} custom-call(bf16[1536,256]{1,0:T(8,128)(2,1)S(1)} %copy-done.68, bf16[1536,256]{1,0:T(8,128)(2,1)S(1)} %copy-done.70, bf16[1536,256]{1,0:T(8,128)(2,1)S(1)} %copy-done.72, bf16[1536,256]{1,0:T(8,128)(2,1)S(1)} %copy-done.74, bf16[1536,256]{1,0:T(8,128)(2,1)S(1)} %get-tuple-element.73.refs_4_, ...), custom_call_target="tpu_custom_call" | custom-call | tf_op jit(solution)/shard_map/grad/pallas_call | solution.py:252
  232.0 3.7 copy-done.9
  235.7 6.9 %gelu.13 = (bf16[1536,256]{1,0:T(8,128)(2,1)S(1)}, bf16[1536,256]{1,0:T(8,128)(2,1)S(1)}, bf16[3072,128]{1,0:T(8,128)(2,1)S(1)}, bf16[3072,128]{1,0:T(8,128)(2,1)S(1)}) custom-call(bf16[3072,256]{1,0:T(8,128)(2,1)} %terms.11.refs_5_.refs_0_.refs_2_, bf16[3072,256]{1,0:T(8,128)(2,1)} %collective-permute-done.26.refs_1_.refs_3_, ...), custom_call_target="tpu_custom_call" | custom-call | tf_op jit(solution)/shard_map/gelu/pallas_call | solution.py:181
  247.0 3.7 copy-done.3
  250.7 3.7 copy-done.6
  254.4 9.4 %terms.13.refs_15_.refs_0_.refs_2_ = bf16[3072,256]{1,0:T(8,128)(2,1)} custom-call(bf16[256,3072]{1,0:T(8,128)(2,1)} %collective-permute-done.16.refs_6_.refs_0_.refs_2_.refs_1_, bf16[256,3072]{1,0:T(8,128)(2,1)} %collective-permute-done.33.refs_1_.refs_3_.refs_2_, bf16[256,3072]{1,0:T(8,128)(2,1)} %collective-permute-done.16.refs_6_.refs_0_.refs_2_.refs_1_, ...), custom_call_target="tpu_custom_call" | custom-call | tf_op jit(solution)/shard_map/terms/pallas_call | solution.py:92
  273.2 16.0 %grad.7.refs_5_.refs_6_ = bf16[1536,3072]{1,0:T(8,128)(2,1)} custom-call(bf16[1536,256]{1,0:T(8,128)(2,1)S(1)} %copy-done.56, bf16[1536,256]{1,0:T(8,128)(2,1)S(1)} %copy-done.58, bf16[1536,256]{1,0:T(8,128)(2,1)S(1)} %copy-done.60, bf16[1536,256]{1,0:T(8,128)(2,1)S(1)} %copy-done.62, bf16[1536,256]{1,0:T(8,128)(2,1)S(1)} %copy-done.64, ...), custom_call_target="tpu_custom_call" | custom-call | tf_op jit(solution)/shard_map/grad/pallas_call | solution.py:252
  289.2 4.0 copy-done.7
  293.2 7.7 %gelu.14 = (bf16[1536,256]{1,0:T(8,128)(2,1)S(1)}, bf16[1536,256]{1,0:T(8,128)(2,1)S(1)}, bf16[3072,128]{1,0:T(8,128)(2,1)S(1)}, bf16[3072,128]{1,0:T(8,128)(2,1)S(1)}) custom-call(bf16[3072,256]{1,0:T(8,128)(2,1)} %terms.12.refs_15_.refs_0_.refs_2_, bf16[3072,256]{1,0:T(8,128)(2,1)} %collective-permute-done.35.refs_1_.refs_3_, ...), custom_call_target="tpu_custom_call" | custom-call | tf_op jit(solution)/shard_map/gelu/pallas_call | solution.py:181
  301.0 4.4 %collective-permute-start.32 = (bf16[3072,128]{1,0:T(8,128)(2,1)S(1)}, bf16[3072,128]{1,0:T(8,128)(2,1)S(1)}, u32[]{:S(2)}, u32[]{:S(2)}) collective-permute-start(bf16[3072,128]{1,0:T(8,128)(2,1)S(1)} %copy-done.78), channel_id=1, source_target_pairs={{0,16},{8,24},{16,0},{24,8},{1,17},{9,25},{17,1},{25,9},{2,18},{10... | collective-permute-start | bytes 2359304 | tf_op jit(solution)/shard_map/ppermute | solution.py:297
  306.9 10.9 %grad.8.refs_7_.refs_3_ = bf16[1536,3072]{1,0:T(8,128)(2,1)} custom-call(bf16[1536,256]{1,0:T(8,128)(2,1)S(1)} %copy-done.76, bf16[1536,256]{1,0:T(8,128)(2,1)S(1)} %get-tuple-element.83.refs_1_, bf16[256,3072]{1,0:T(8,128)(2,1)S(1)} %copy-done.13, bf16[256,3072]{1,0:T(8,128)(2,1)S(1)} %copy-done.32, bf16[256,3072]{1,0:T(8,128)(2,1)S(1)} %copy-done.11, ...), custom_call_target="tpu_custom_call" | custom-call | tf_op jit(solution)/shard_map/grad/pallas_call | solution.py:252
  318.9 11.1 %grad.9.refs_5_.refs_3_ = bf16[1536,3072]{1,0:T(8,128)(2,1)} custom-call(bf16[1536,256]{1,0:T(8,128)(2,1)S(1)} %copy-done.44, bf16[1536,256]{1,0:T(8,128)(2,1)S(1)} %get-tuple-element.81.refs_7_.refs_1_, bf16[256,3072]{1,0:T(8,128)(2,1)S(1)} %copy-done.13, bf16[256,3072]{1,0:T(8,128)(2,1)S(1)} %copy-done.32, bf16[256,3072]{1,0:T(8,128)(2,1)S(1)} %copy-done.11, ...), custom_call_target="tpu_custom_call" | custom-call | tf_op jit(solution)/shard_map/grad/pallas_call | solution.py:252
  330.0 3.7 copy-done.8
  333.7 3.6 gelu.15
  337.5 11.0 %grad.10 = (bf16[1536,3072]{1,0:T(8,128)(2,1)}, f32[8,512]{1,0:T(8,128)S(1)}) custom-call(bf16[1536,256]{1,0:T(8,128)(2,1)S(1)} %get-tuple-element.86.refs_0_.d_pre_ref, bf16[256,3072]{1,0:T(8,128)(2,1)} %collective-permute-done.16.refs_6_.refs_0_.refs_2_.refs_1_, bf16[256,3072]{1,0:T(8,128)(2,1)} %collective-permute-done.33.refs_1_.refs_3_.refs_2_, ...), custom_call_target="tpu_custom_call" | custom-call | tf_op jit(solution)/shard_map/grad/pallas_call | solution.py:252
  348.5 8.6 %grad.11 = (bf16[1536,3072]{1,0:T(8,128)(2,1)S(1)}, f32[8,512]{1,0:T(8,128)S(1)}) custom-call(bf16[1536,256]{1,0:T(8,128)(2,1)S(1)} %get-tuple-element.87.refs_4_.refs_0_, bf16[256,3072]{1,0:T(8,128)(2,1)} %collective-permute-done.16.refs_6_.refs_0_.refs_2_.refs_1_, bf16[256,3072]{1,0:T(8,128)(2,1)} %collective-permute-done.33.refs_1_.refs_3_.refs_2_, ...), custom_call_target="tpu_custom_call" | custom-call | tf_op jit(solution)/shard_map/grad/pallas_call | solution.py:252
  357.2 3.7 copy-done.39
  364.8 4.3 %collective-permute-start.38 = (f32[8,128]{1,0:T(8,128)S(1)}, f32[8,128]{1,0:T(8,128)S(1)}, u32[]{:S(2)}, u32[]{:S(2)}) collective-permute-start(f32[8,128]{1,0:T(8,128)S(1)} %broadcast_in_dim.3), channel_id=1, source_target_pairs={{0,16},{8,24},{16,0},{24,8},{1,17},{9,25},{17,1},{25,9},{2,18},{10... | collective-permute-start | bytes 12296 | tf_op jit(solution)/shard_map/ppermute | solution.py:297
  372.7 3.7 copy-done.1
  379.6 8.0 %collective-permute-done.41 = bf16[3072,128]{1,0:T(8,128)(2,1)S(1)} collective-permute-done((bf16[3072,128]{1,0:T(8,128)(2,1)S(1)}, bf16[3072,128]{1,0:T(8,128)(2,1)S(1)}, u32[]{:S(2)}, u32[]{:S(2)}) %collective-permute-start.41) | collective-permute-done | bytes 786464 | tf_op jit(solution)/shard_map/ppermute | solution.py:294
  398.0 4.8 %scale.3 = bf16[1536,3072]{1,0:T(8,128)(2,1)} custom-call(f32[1,1]{1,0:T(1,128)S(6)} %sqrt.3.factor_ref, bf16[1536,3072]{1,0:T(8,128)(2,1)S(1)} %copy-done.40), custom_call_target="tpu_custom_call" | custom-call | tf_op jit(solution)/shard_map/scale/pallas_call | solution.py:274
  403.5 7.8 %scale.2 = bf16[3072,1536]{1,0:T(8,128)(2,1)} custom-call(f32[1,1]{1,0:T(1,128)S(6)} %sqrt.3.factor_ref, bf16[1536,3072]{1,0:T(8,128)(2,1)S(1)} %bitcast.15), custom_call_target="tpu_custom_call" | custom-call | tf_op jit(solution)/shard_map/scale/pallas_call | solution.py:274
  (303 shorter events, 78.9 us)
Async XLA Ops:
  2.1 3.5 collective-permute-start
  2.1 36.8 %collective-permute-start.4 = (bf16[256,3072]{1,0:T(8,128)(2,1)S(1)}, bf16[256,3072]{1,0:T(8,128)(2,1)S(1)}, u32[]{:S(2)}, u32[]{:S(2)}) collective-permute-start(bf16[256,3072]{1,0:T(8,128)(2,1)S(1)} %constant_dynamic-update-slice_fusion.refs_0_.refs_5_), channel_id=1, source_target_pairs={{0,24},{8,0},{16,8},{24,16},{1,25},{9,1},{17,9},{25,17},{2,26},{10... | collective-permute-start | bytes 4718600 | tf_op jit(solution)/shard_map/ppermute | solution.py:297
  2.2 36.7 %collective-permute-start.3 = (bf16[256,3072]{1,0:T(8,128)(2,1)S(1)}, bf16[256,3072]{1,0:T(8,128)(2,1)S(1)}, u32[]{:S(2)}, u32[]{:S(2)}) collective-permute-start(bf16[256,3072]{1,0:T(8,128)(2,1)S(1)} %constant_dynamic-update-slice_fusion.refs_0_.refs_5_), channel_id=1, source_target_pairs={{0,4},{2,6},{4,0},{6,2},{1,5},{3,7},{5,1},{7,3},{8,12},{10,14},{12... | collective-permute-start | bytes 4718600 | tf_op jit(solution)/shard_map/ppermute | solution.py:294
  13.6 32.3 %collective-permute-start.1 = (bf16[1536,256]{1,0:T(8,128)(2,1)S(1)}, bf16[1536,256]{1,0:T(8,128)(2,1)S(1)}, u32[]{:S(2)}, u32[]{:S(2)}) collective-permute-start(bf16[1536,256]{1,0:T(8,128)(2,1)S(1)} %half_terms.2.refs_3_.refs_0_), channel_id=1, source_target_pairs={{0,1},{1,0},{2,3},{3,2},{4,5},{5,4},{6,7},{7,6},{8,9},{9,8},{10,11... | collective-permute-start | bytes 2359304 | tf_op jit(solution)/shard_map/ppermute | solution.py:297
  22.2 23.7 %collective-permute-start.2 = (bf16[1152,256]{1,0:T(8,128)(2,1)S(1)}, bf16[1152,256]{1,0:T(8,128)(2,1)S(1)}, u32[]{:S(2)}, u32[]{:S(2)}) collective-permute-start(bf16[1152,256]{1,0:T(8,128)(2,1)S(1)} %slice.12), channel_id=1, source_target_pairs={{0,1},{1,0},{2,3},{3,2},{4,5},{5,4},{6,7},{7,6},{8,9},{9,8},{10,11... | collective-permute-start | bytes 1769480 | tf_op jit(solution)/shard_map/ppermute | solution.py:297
  26.4 175.2 %copy-start.2 = (bf16[1536,3072]{1,0:T(8,128)(2,1)}, bf16[1536,3072]{1,0:T(8,128)(2,1)S(1)}, u32[]{:S(2)}) copy-start(bf16[1536,3072]{1,0:T(8,128)(2,1)S(1)} %flip.1.refs_4_.refs_6_) | copy-start | bytes 28311556
  45.9 4.6 %collective-permute-start.5 = (bf16[256,3072]{1,0:T(8,128)(2,1)S(1)}, bf16[256,3072]{1,0:T(8,128)(2,1)S(1)}, u32[]{:S(2)}, u32[]{:S(2)}) collective-permute-start(bf16[256,3072]{1,0:T(8,128)(2,1)S(1)} %collective-permute-done.3.refs_0_.refs_2_.refs_7_), channel_id=1, source_target_pairs={{0,2},{2,0},{4,6},{6,4},{1,3},{3,1},{5,7},{7,5},{8,10},{10,8},{12,... | collective-permute-start | bytes 4718600 | tf_op jit(solution)/shard_map/ppermute | solution.py:294
  45.9 15.8 %collective-permute-start.9 = (bf16[256,3072]{1,0:T(8,128)(2,1)S(1)}, bf16[256,3072]{1,0:T(8,128)(2,1)S(1)}, u32[]{:S(2)}, u32[]{:S(2)}) collective-permute-start(bf16[256,3072]{1,0:T(8,128)(2,1)S(1)} %collective-permute-done.4.refs_7_.refs_0_.refs_2_.refs_9_), channel_id=1, source_target_pairs={{0,2},{2,0},{4,6},{6,4},{1,3},{3,1},{5,7},{7,5},{8,10},{10,8},{12,... | collective-permute-start | bytes 4718600 | tf_op jit(solution)/shard_map/ppermute | solution.py:294
  46.4 36.3 %collective-permute-start.11 = (bf16[256,3072]{1,0:T(8,128)(2,1)S(1)}, bf16[256,3072]{1,0:T(8,128)(2,1)S(1)}, u32[]{:S(2)}, u32[]{:S(2)}) collective-permute-start(bf16[256,3072]{1,0:T(8,128)(2,1)S(1)} %collective-permute-done.4.refs_7_.refs_0_.refs_2_.refs_9_), channel_id=1, source_target_pairs={{0,4},{2,6},{4,0},{6,2},{1,5},{3,7},{5,1},{7,3},{8,12},{10,14},{12... | collective-permute-start | bytes 4718600 | tf_op jit(solution)/shard_map/ppermute | solution.py:294
  47.9 36.0 %collective-permute-start.10 = (bf16[256,3072]{1,0:T(8,128)(2,1)S(1)}, bf16[256,3072]{1,0:T(8,128)(2,1)S(1)}, u32[]{:S(2)}, u32[]{:S(2)}) collective-permute-start(bf16[256,3072]{1,0:T(8,128)(2,1)S(1)} %collective-permute-done.4.refs_7_.refs_0_.refs_2_.refs_9_), channel_id=1, source_target_pairs={{0,24},{8,0},{16,8},{24,16},{1,25},{9,1},{17,9},{25,17},{2,26},{10... | collective-permute-start | bytes 4718600 | tf_op jit(solution)/shard_map/ppermute | solution.py:297
  48.9 7.9 %collective-permute-start.6 = (bf16[384,256]{1,0:T(8,128)(2,1)S(1)}, bf16[384,256]{1,0:T(8,128)(2,1)S(1)}, u32[]{:S(2)}, u32[]{:S(2)}) collective-permute-start(bf16[384,256]{1,0:T(8,128)(2,1)S(1)} %slice.13), channel_id=1, source_target_pairs={{0,1},{1,0},{2,3},{3,2},{4,5},{5,4},{6,7},{7,6},{8,9},{9,8},{10,11... | collective-permute-start | bytes 589832 | tf_op jit(solution)/shard_map/ppermute | solution.py:297
  56.2 37.4 %collective-permute-start.8 = (bf16[3072,256]{1,0:T(8,128)(2,1)S(1)}, bf16[3072,256]{1,0:T(8,128)(2,1)S(1)}, u32[]{:S(2)}, u32[]{:S(2)}) collective-permute-start(bf16[3072,256]{1,0:T(8,128)(2,1)S(1)} %terms.7.refs_5_.refs_0_.refs_2_), channel_id=1, source_target_pairs={{0,1},{1,0},{2,3},{3,2},{4,5},{5,4},{6,7},{7,6},{8,9},{9,8},{10,11... | collective-permute-start | bytes 4718600 | tf_op jit(solution)/shard_map/ppermute | solution.py:297
  61.6 24.8 %collective-permute-start.7 = (bf16[3072,128]{1,0:T(8,128)(2,1)S(1)}, bf16[3072,128]{1,0:T(8,128)(2,1)S(1)}, u32[]{:S(2)}, u32[]{:S(2)}) collective-permute-start(bf16[3072,128]{1,0:T(8,128)(2,1)S(1)} %get-tuple-element.53), channel_id=1, source_target_pairs={{0,2},{2,0},{4,6},{6,4},{1,3},{3,1},{5,7},{7,5},{8,10},{10,8},{12,... | collective-permute-start | bytes 2359304 | tf_op jit(solution)/shard_map/ppermute | solution.py:294
  82.7 16.6 %collective-permute-start.15 = (bf16[256,3072]{1,0:T(8,128)(2,1)S(1)}, bf16[256,3072]{1,0:T(8,128)(2,1)S(1)}, u32[]{:S(2)}, u32[]{:S(2)}) collective-permute-start(bf16[256,3072]{1,0:T(8,128)(2,1)S(1)} %collective-permute-done.11.refs_7_.refs_0_.refs_2_.refs_11_), channel_id=1, source_target_pairs={{0,2},{2,0},{4,6},{6,4},{1,3},{3,1},{5,7},{7,5},{8,10},{10,8},{12,... | collective-permute-start | bytes 4718600 | tf_op jit(solution)/shard_map/ppermute | solution.py:294
  83.9 35.6 %collective-permute-start.17 = (bf16[256,3072]{1,0:T(8,128)(2,1)S(1)}, bf16[256,3072]{1,0:T(8,128)(2,1)S(1)}, u32[]{:S(2)}, u32[]{:S(2)}) collective-permute-start(bf16[256,3072]{1,0:T(8,128)(2,1)S(1)} %collective-permute-done.10.refs_6_.refs_0_.refs_2_), channel_id=1, source_target_pairs={{0,4},{2,6},{4,0},{6,2},{1,5},{3,7},{5,1},{7,3},{8,12},{10,14},{12... | collective-permute-start | bytes 4718600 | tf_op jit(solution)/shard_map/ppermute | solution.py:294
  84.4 36.6 %collective-permute-start.16 = (bf16[256,3072]{1,0:T(8,128)(2,1)S(1)}, bf16[256,3072]{1,0:T(8,128)(2,1)}, u32[]{:S(2)}, u32[]{:S(2)}) collective-permute-start(bf16[256,3072]{1,0:T(8,128)(2,1)S(1)} %collective-permute-done.10.refs_6_.refs_0_.refs_2_), channel_id=1, source_target_pairs={{0,24},{8,0},{16,8},{24,16},{1,25},{9,1},{17,9},{25,17},{2,26},{10... | collective-permute-start | bytes 4718600 | tf_op jit(solution)/shard_map/ppermute | solution.py:297
  86.4 41.0 %collective-permute-start.14 = (bf16[3072,256]{1,0:T(8,128)(2,1)S(1)}, bf16[3072,256]{1,0:T(8,128)(2,1)S(1)}, u32[]{:S(2)}, u32[]{:S(2)}) collective-permute-start(bf16[3072,256]{1,0:T(8,128)(2,1)S(1)} %terms.8.refs_5_.refs_0_.refs_2_), channel_id=1, source_target_pairs={{0,1},{1,0},{2,3},{3,2},{4,5},{5,4},{6,7},{7,6},{8,9},{9,8},{10,11... | collective-permute-start | bytes 4718600 | tf_op jit(solution)/shard_map/ppermute | solution.py:297
  99.3 23.2 %collective-permute-start.12 = (bf16[3072,128]{1,0:T(8,128)(2,1)S(1)}, bf16[3072,128]{1,0:T(8,128)(2,1)S(1)}, u32[]{:S(2)}, u32[]{:S(2)}) collective-permute-start(bf16[3072,128]{1,0:T(8,128)(2,1)S(1)} %get-tuple-element.57), channel_id=1, source_target_pairs={{0,2},{2,0},{4,6},{6,4},{1,3},{3,1},{5,7},{7,5},{8,10},{10,8},{12,... | collective-permute-start | bytes 2359304 | tf_op jit(solution)/shard_map/ppermute | solution.py:294
  119.5 14.0 %collective-permute-start.20 = (bf16[256,3072]{1,0:T(8,128)(2,1)S(1)}, bf16[256,3072]{1,0:T(8,128)(2,1)S(1)}, u32[]{:S(2)}, u32[]{:S(2)}) collective-permute-start(bf16[256,3072]{1,0:T(8,128)(2,1)S(1)} %collective-permute-done.17.refs_7_.refs_0_.refs_2_.refs_13_), channel_id=1, source_target_pairs={{0,2},{2,0},{4,6},{6,4},{1,3},{3,1},{5,7},{7,5},{8,10},{10,8},{12,... | collective-permute-start | bytes 4718600 | tf_op jit(solution)/shard_map/ppermute | solution.py:294
  119.5 41.6 %collective-permute-start.19 = (bf16[3072,256]{1,0:T(8,128)(2,1)S(1)}, bf16[3072,256]{1,0:T(8,128)(2,1)S(1)}, u32[]{:S(2)}, u32[]{:S(2)}) collective-permute-start(bf16[3072,256]{1,0:T(8,128)(2,1)S(1)} %terms.9.refs_5_.refs_0_.refs_2_), channel_id=1, source_target_pairs={{0,1},{1,0},{2,3},{3,2},{4,5},{5,4},{6,7},{7,6},{8,9},{9,8},{10,11... | collective-permute-start | bytes 4718600 | tf_op jit(solution)/shard_map/ppermute | solution.py:297
  121.0 36.7 %collective-permute-start.21 = (bf16[256,3072]{1,0:T(8,128)(2,1)}, bf16[256,3072]{1,0:T(8,128)(2,1)S(1)}, u32[]{:S(2)}, u32[]{:S(2)}) collective-permute-start(bf16[256,3072]{1,0:T(8,128)(2,1)} %collective-permute-done.16.refs_6_.refs_0_.refs_2_.refs_1_), channel_id=1, source_target_pairs={{0,4},{2,6},{4,0},{6,2},{1,5},{3,7},{5,1},{7,3},{8,12},{10,14},{12... | collective-permute-start | bytes 4718600 | tf_op jit(solution)/shard_map/ppermute | solution.py:294
  133.0 6.8 %collective-permute-start.18 = (bf16[3072,128]{1,0:T(8,128)(2,1)S(1)}, bf16[3072,128]{1,0:T(8,128)(2,1)S(1)}, u32[]{:S(2)}, u32[]{:S(2)}) collective-permute-start(bf16[3072,128]{1,0:T(8,128)(2,1)S(1)} %get-tuple-element.62), channel_id=1, source_target_pairs={{0,2},{2,0},{4,6},{6,4},{1,3},{3,1},{5,7},{7,5},{8,10},{10,8},{12,... | collective-permute-start | bytes 2359304 | tf_op jit(solution)/shard_map/ppermute | solution.py:294
  133.0 34.6 %collective-permute-start.25 = (bf16[256,3072]{1,0:T(8,128)(2,1)S(1)}, bf16[256,3072]{1,0:T(8,128)(2,1)S(1)}, u32[]{:S(2)}, u32[]{:S(2)}) collective-permute-start(bf16[256,3072]{1,0:T(8,128)(2,1)S(1)} %collective-permute-done.10.refs_6_.refs_0_.refs_2_), channel_id=1, source_target_pairs={{0,2},{2,0},{4,6},{6,4},{1,3},{3,1},{5,7},{7,5},{8,10},{10,8},{12,... | collective-permute-start | bytes 4718600 | tf_op jit(solution)/shard_map/ppermute | solution.py:294
  139.3 55.5 %collective-permute-start.27 = (bf16[3072,256]{1,0:T(8,128)(2,1)S(1)}, bf16[3072,256]{1,0:T(8,128)(2,1)S(1)}, u32[]{:S(2)}, u32[]{:S(2)}) collective-permute-start(bf16[3072,256]{1,0:T(8,128)(2,1)S(1)} %terms.10.refs_5_.refs_0_.refs_2_), channel_id=1, source_target_pairs={{0,1},{1,0},{2,3},{3,2},{4,5},{5,4},{6,7},{7,6},{8,9},{9,8},{10,11... | collective-permute-start | bytes 4718600 | tf_op jit(solution)/shard_map/ppermute | solution.py:297
  165.8 8.9 %collective-permute-start.22 = (bf16[3072,128]{1,0:T(8,128)(2,1)S(1)}, bf16[3072,128]{1,0:T(8,128)(2,1)S(1)}, u32[]{:S(2)}, u32[]{:S(2)}) collective-permute-start(bf16[3072,128]{1,0:T(8,128)(2,1)S(1)} %get-tuple-element.67), channel_id=1, source_target_pairs={{0,2},{2,0},{4,6},{6,4},{1,3},{3,1},{5,7},{7,5},{8,10},{10,8},{12,... | collective-permute-start | bytes 2359304 | tf_op jit(solution)/shard_map/ppermute | solution.py:294
  165.9 20.0 %collective-permute-start.13 = (bf16[3072,128]{1,0:T(8,128)(2,1)S(1)}, bf16[3072,128]{1,0:T(8,128)(2,1)S(1)}, u32[]{:S(2)}, u32[]{:S(2)}) collective-permute-start(bf16[3072,128]{1,0:T(8,128)(2,1)S(1)} %add_convert_fusion.11.refs_8_), channel_id=1, source_target_pairs={{0,4},{2,6},{4,0},{6,2},{1,5},{3,7},{5,1},{7,3},{8,12},{10,14},{12... | collective-permute-start | bytes 2359304 | tf_op jit(solution)/shard_map/ppermute | solution.py:294
  167.4 34.1 %collective-permute-start.28 = (bf16[256,3072]{1,0:T(8,128)(2,1)S(1)}, bf16[256,3072]{1,0:T(8,128)(2,1)S(1)}, u32[]{:S(2)}, u32[]{:S(2)}) collective-permute-start(bf16[256,3072]{1,0:T(8,128)(2,1)S(1)} %collective-permute-done.21.refs_6_.refs_0_.refs_2_.refs_4_), channel_id=1, source_target_pairs={{0,2},{2,0},{4,6},{6,4},{1,3},{3,1},{5,7},{7,5},{8,10},{10,8},{12,... | collective-permute-start | bytes 4718600 | tf_op jit(solution)/shard_map/ppermute | solution.py:294
  174.1 57.9 %collective-permute-start.26 = (bf16[3072,256]{1,0:T(8,128)(2,1)}, bf16[3072,256]{1,0:T(8,128)(2,1)}, u32[]{:S(2)}, u32[]{:S(2)}) collective-permute-start(bf16[3072,256]{1,0:T(8,128)(2,1)} %terms.11.refs_5_.refs_0_.refs_2_), channel_id=1, source_target_pairs={{0,1},{1,0},{2,3},{3,2},{4,5},{5,4},{6,7},{7,6},{8,9},{9,8},{10,11... | collective-permute-start | bytes 4718600 | tf_op jit(solution)/shard_map/ppermute | solution.py:297
  199.5 9.2 %collective-permute-start.29 = (bf16[3072,128]{1,0:T(8,128)(2,1)S(1)}, bf16[3072,128]{1,0:T(8,128)(2,1)S(1)}, u32[]{:S(2)}, u32[]{:S(2)}) collective-permute-start(bf16[3072,128]{1,0:T(8,128)(2,1)S(1)} %get-tuple-element.77), channel_id=1, source_target_pairs={{0,2},{2,0},{4,6},{6,4},{1,3},{3,1},{5,7},{7,5},{8,10},{10,8},{12,... | collective-permute-start | bytes 2359304 | tf_op jit(solution)/shard_map/ppermute | solution.py:294
  199.6 47.4 %collective-permute-start.33 = (bf16[256,3072]{1,0:T(8,128)(2,1)}, bf16[256,3072]{1,0:T(8,128)(2,1)}, u32[]{:S(2)}, u32[]{:S(2)}) collective-permute-start(bf16[256,3072]{1,0:T(8,128)(2,1)} %collective-permute-done.16.refs_6_.refs_0_.refs_2_.refs_1_), channel_id=1, source_target_pairs={{0,2},{2,0},{4,6},{6,4},{1,3},{3,1},{5,7},{7,5},{8,10},{10,8},{12,... | collective-permute-start | bytes 4718600 | tf_op jit(solution)/shard_map/ppermute | solution.py:294
  200.1 31.9 %collective-permute-start.23 = (bf16[3072,128]{1,0:T(8,128)(2,1)}, bf16[3072,128]{1,0:T(8,128)(2,1)}, u32[]{:S(2)}, u32[]{:S(2)}) collective-permute-start(bf16[3072,128]{1,0:T(8,128)(2,1)} %add_convert_fusion.8.refs_7_), channel_id=1, source_target_pairs={{0,4},{2,6},{4,0},{6,2},{1,5},{3,7},{5,1},{7,3},{8,12},{10,14},{12... | collective-permute-start | bytes 2359304 | tf_op jit(solution)/shard_map/ppermute | solution.py:294
  208.2 81.1 %collective-permute-start.35 = (bf16[3072,256]{1,0:T(8,128)(2,1)}, bf16[3072,256]{1,0:T(8,128)(2,1)}, u32[]{:S(2)}, u32[]{:S(2)}) collective-permute-start(bf16[3072,256]{1,0:T(8,128)(2,1)} %terms.12.refs_15_.refs_0_.refs_2_), channel_id=1, source_target_pairs={{0,1},{1,0},{2,3},{3,2},{4,5},{5,4},{6,7},{7,6},{8,9},{9,8},{10,11... | collective-permute-start | bytes 4718600 | tf_op jit(solution)/shard_map/ppermute | solution.py:297
  209.8 37.2 %collective-permute-start.31 = (bf16[3072,128]{1,0:T(8,128)(2,1)}, bf16[3072,128]{1,0:T(8,128)(2,1)}, u32[]{:S(2)}, u32[]{:S(2)}) collective-permute-start(bf16[3072,128]{1,0:T(8,128)(2,1)} %add_convert_fusion.6.refs_16_), channel_id=1, source_target_pairs={{0,4},{2,6},{4,0},{6,2},{1,5},{3,7},{5,1},{7,3},{8,12},{10,14},{12... | collective-permute-start | bytes 2359304 | tf_op jit(solution)/shard_map/ppermute | solution.py:294
  242.6 22.4 %collective-permute-start.30 = (bf16[3072,128]{1,0:T(8,128)(2,1)S(1)}, bf16[3072,128]{1,0:T(8,128)(2,1)}, u32[]{:S(2)}, u32[]{:S(2)}) collective-permute-start(bf16[3072,128]{1,0:T(8,128)(2,1)S(1)} %get-tuple-element.79), channel_id=1, source_target_pairs={{0,2},{2,0},{4,6},{6,4},{1,3},{3,1},{5,7},{7,5},{8,10},{10,8},{12,... | collective-permute-start | bytes 2359304 | tf_op jit(solution)/shard_map/ppermute | solution.py:294
  245.6 43.6 %collective-permute-start.24 = (bf16[3072,128]{1,0:T(8,128)(2,1)}, bf16[3072,128]{1,0:T(8,128)(2,1)S(1)}, u32[]{:S(2)}, u32[]{:S(2)}) collective-permute-start(bf16[3072,128]{1,0:T(8,128)(2,1)} %add_convert_fusion.7), channel_id=1, source_target_pairs={{0,8},{8,16},{16,24},{24,0},{1,9},{9,17},{17,25},{25,1},{2,10},{10... | collective-permute-start | bytes 2359304 | tf_op jit(solution)/shard_map/ppermute | solution.py:297
  263.7 66.2 %collective-permute-start.34 = (bf16[3072,256]{1,0:T(8,128)(2,1)}, bf16[3072,256]{1,0:T(8,128)(2,1)}, u32[]{:S(2)}, u32[]{:S(2)}) collective-permute-start(bf16[3072,256]{1,0:T(8,128)(2,1)} %terms.13.refs_15_.refs_0_.refs_2_), channel_id=1, source_target_pairs={{0,1},{1,0},{2,3},{3,2},{4,5},{5,4},{6,7},{7,6},{8,9},{9,8},{10,11... | collective-permute-start | bytes 4718600 | tf_op jit(solution)/shard_map/ppermute | solution.py:297
  300.9 16.8 %collective-permute-start.36 = (bf16[3072,128]{1,0:T(8,128)(2,1)S(1)}, bf16[3072,128]{1,0:T(8,128)(2,1)S(1)}, u32[]{:S(2)}, u32[]{:S(2)}) collective-permute-start(bf16[3072,128]{1,0:T(8,128)(2,1)S(1)} %get-tuple-element.85), channel_id=1, source_target_pairs={{0,2},{2,0},{4,6},{6,4},{1,3},{3,1},{5,7},{7,5},{8,10},{10,8},{12,... | collective-permute-start | bytes 2359304 | tf_op jit(solution)/shard_map/ppermute | solution.py:294
  301.0 36.5 %collective-permute-start.32 = (bf16[3072,128]{1,0:T(8,128)(2,1)S(1)}, bf16[3072,128]{1,0:T(8,128)(2,1)S(1)}, u32[]{:S(2)}, u32[]{:S(2)}) collective-permute-start(bf16[3072,128]{1,0:T(8,128)(2,1)S(1)} %copy-done.78), channel_id=1, source_target_pairs={{0,16},{8,24},{16,0},{24,8},{1,17},{9,25},{17,1},{25,9},{2,18},{10... | collective-permute-start | bytes 2359304 | tf_op jit(solution)/shard_map/ppermute | solution.py:297
  363.5 6.5 %collective-permute-start.37 = (f32[8,128]{1,0:T(8,128)S(1)}, f32[8,128]{1,0:T(8,128)S(1)}, u32[]{:S(2)}, u32[]{:S(2)}) collective-permute-start(f32[8,128]{1,0:T(8,128)S(1)} %broadcast_in_dim.3), channel_id=1, source_target_pairs={{0,8},{8,16},{16,24},{24,0},{1,9},{9,17},{17,25},{25,1},{2,10},{10... | collective-permute-start | bytes 12296 | tf_op jit(solution)/shard_map/ppermute | solution.py:297
  364.8 5.9 %collective-permute-start.38 = (f32[8,128]{1,0:T(8,128)S(1)}, f32[8,128]{1,0:T(8,128)S(1)}, u32[]{:S(2)}, u32[]{:S(2)}) collective-permute-start(f32[8,128]{1,0:T(8,128)S(1)} %broadcast_in_dim.3), channel_id=1, source_target_pairs={{0,16},{8,24},{16,0},{24,8},{1,17},{9,25},{17,1},{25,9},{2,18},{10... | collective-permute-start | bytes 12296 | tf_op jit(solution)/shard_map/ppermute | solution.py:297
  369.0 3.6 collective-permute-start.39
  369.1 18.5 %collective-permute-start.41 = (bf16[3072,128]{1,0:T(8,128)(2,1)S(1)}, bf16[3072,128]{1,0:T(8,128)(2,1)S(1)}, u32[]{:S(2)}, u32[]{:S(2)}) collective-permute-start(bf16[3072,128]{1,0:T(8,128)(2,1)S(1)} %copy-done.54), channel_id=1, source_target_pairs={{0,4},{2,6},{4,0},{6,2},{1,5},{3,7},{5,1},{7,3},{8,12},{10,14},{12... | collective-permute-start | bytes 2359304 | tf_op jit(solution)/shard_map/ppermute | solution.py:294
  379.5 8.1 %collective-permute-start.40 = (bf16[3072,128]{1,0:T(8,128)(2,1)S(1)}, bf16[3072,128]{1,0:T(8,128)(2,1)S(1)}, u32[]{:S(2)}, u32[]{:S(2)}) collective-permute-start(bf16[3072,128]{1,0:T(8,128)(2,1)S(1)} %get-tuple-element.92), channel_id=1, source_target_pairs={{0,2},{2,0},{4,6},{6,4},{1,3},{3,1},{5,7},{7,5},{8,10},{10,8},{12,... | collective-permute-start | bytes 2359304 | tf_op jit(solution)/shard_map/ppermute | solution.py:294
  387.9 23.4 %collective-permute-start.42 = (bf16[3072,128]{1,0:T(8,128)(2,1)S(1)}, bf16[3072,128]{1,0:T(8,128)(2,1)S(1)}, u32[]{:S(2)}, u32[]{:S(2)}) collective-permute-start(bf16[3072,128]{1,0:T(8,128)(2,1)S(1)} %add_convert_fusion.1), channel_id=1, source_target_pairs={{0,24},{8,0},{16,8},{24,16},{1,25},{9,1},{17,9},{25,17},{2,26},{10... | collective-permute-start | bytes 2359304 | tf_op jit(solution)/shard_map/ppermute | solution.py:297
  389.4 1.9 collective-permute-start.43
  389.4 3.6 collective-permute-start.44
  389.9 3.1 collective-permute-start.45
  393.0 3.7 collective-permute-start.46
  (99 other events, 1098.2 us)

commit v2 on v1

v2 whole, which is shorter than its diff:
```python
import jax
import jax.numpy as jnp
from jax import lax
from jax.experimental import pallas as pl
from jax.experimental.pallas import tpu as pltpu
from jax.sharding import PartitionSpec as P

GELU_C = 0.7978845608
MIB = 1 << 20
ANY = pl.BlockSpec(memory_space=pl.ANY)
HELD = pl.BlockSpec(memory_space=pltpu.VMEM)
WIDE = 56


def gelu_parts(values):
    inner_arg = GELU_C * (values + 0.044715 * values * values * values)
    tanh_val = jnp.tanh(inner_arg)
    value_out = 0.5 * values * (1.0 + tanh_val)
    slope = 0.5 * (1.0 + tanh_val) + 0.5 * values * (1.0 - tanh_val * tanh_val) * GELU_C * (
        1.0 + 3.0 * 0.044715 * values * values
    )
    return (value_out, slope)


def contract(left, right, left_dim, right_dim):
    return lax.dot_general(
        left, right, (((left_dim,), (right_dim,)), ((), ())), preferred_element_type=jnp.float32
    )


def tile_of(extent, most):
    size = most
    while extent % size:
        size //= 2
    return size


def stacked(refs):
    return jnp.concatenate([ref[...] for ref in refs], axis=0) if len(refs) > 1 else refs[0][...]


def once(shape, at):
    return pl.BlockSpec(shape, lambda i: (at, 0), pipeline_mode=pl.Buffered(1))


def params(mib):
    return pltpu.CompilerParams(vmem_limit_bytes=mib * MIB)


def flip_call(weight, after):
    rows, cols = weight.shape
    tile = tile_of(cols, 256)

    def kernel(in_ref, *refs):
        refs[-1][...] = in_ref[...].T

    return pl.pallas_call(
        kernel,
        grid=(cols // tile,),
        in_specs=[pl.BlockSpec((rows, tile), lambda i: (0, i))] + [ANY] * len(after),
        out_specs=pl.BlockSpec((tile, rows), lambda i: (i, 0)),
        out_shape=jax.ShapeDtypeStruct((cols, rows), weight.dtype),
        compiler_params=params(6),
        name="flip",
    )(weight, *after)


def terms_call(blocks, w_in, w_out, after, split):
    hidden, depth = w_out.shape
    rows = blocks[0].shape[0] // 2
    count = len(blocks)
    tile = tile_of(hidden, 768)
    steps = hidden // tile

    def kernel(*refs):
        x_refs, dy_refs = refs[:count], refs[count : 2 * count]
        w_in_ref, w_out_ref = refs[2 * count : 2 * count + 2]
        h_ref, d_ref = (refs[-2], refs[-1]) if split else (refs[-1], refs[-1])
        step = pl.program_id(0)

        @pl.when(step < steps)
        def _():
            at = pl.ds(pl.multiple_of(step * tile, tile), tile)
            h_ref[...] = contract(w_in_ref[at, :], stacked(x_refs), 1, 1).astype(jnp.bfloat16)

        @pl.when(step >= steps)
        def _():
            at = pl.ds(pl.multiple_of((step - steps) * tile, tile), tile)
            d_ref[...] = contract(w_out_ref[at, :], stacked(dy_refs), 1, 1).astype(jnp.bfloat16)

    cols = count * rows
    out_specs = pl.BlockSpec((tile, cols), lambda i: (i, 0))
    out_shape = jax.ShapeDtypeStruct((2 * hidden, cols), jnp.bfloat16)
    if split:
        out_specs = [
            pl.BlockSpec((tile, cols), lambda i: (jnp.minimum(i, steps - 1), 0)),
            pl.BlockSpec((tile, cols), lambda i: (jnp.maximum(i - steps, 0), 0)),
        ]
        out_shape = [jax.ShapeDtypeStruct((hidden, cols), jnp.bfloat16)] * 2
    return pl.pallas_call(
        kernel,
        grid=(2 * steps,),
        in_specs=[once((rows, depth), 0)] * count
        + [once((rows, depth), 1)] * count
        + [HELD, HELD]
        + [ANY] * len(after),
        out_specs=out_specs,
        out_shape=out_shape,
        compiler_params=params(6),
        name="terms",
    )(*blocks, *blocks, w_in, w_out, *after)


def half_call(blocks, part, weight, weight_dim, after):
    depth, hidden = weight.shape[weight_dim], weight.shape[1 - weight_dim]
    rows = blocks[0].shape[0] // 2
    count = len(blocks)
    tile = tile_of(hidden, 768)

    def kernel(*refs):
        at = pl.ds(pl.multiple_of(pl.program_id(0) * tile, tile), tile)
        left = refs[count][at, :] if weight_dim else refs[count][:, at]
        refs[-1][...] = contract(left, stacked(refs[:count]), weight_dim, 1).astype(jnp.bfloat16)

    return pl.pallas_call(
        kernel,
        grid=(hidden // tile,),
        in_specs=[once((rows, depth), part)] * count
        + [HELD]
        + [ANY] * len(after),
        out_specs=pl.BlockSpec((tile, count * rows), lambda i: (i, 0)),
        out_shape=jax.ShapeDtypeStruct((hidden, count * rows), jnp.bfloat16),
        compiler_params=params(6),
        name="half_terms",
    )(*blocks, weight, *after)


def gelu_call(h_terms, d_terms, w_in, after):
    depth, hidden = w_in.shape
    cols = h_terms[0].shape[1]
    count = len(h_terms)
    row_tile = tile_of(hidden, 384)
    row_steps = hidden // row_tile
    tile = tile_of(depth, 768)
    steps = depth // tile
    part = cols // 2

    def kernel(*refs):
        h_refs, d_refs = refs[:count], refs[count : 2 * count]
        w_ref = refs[2 * count]
        outs = refs[2 * count + 1 + len(after) :]
        act_ref, d_pre_ref = outs[:2]
        held = outs[-1]
        step = pl.program_id(0)

        @pl.when(step < row_steps)
        def _():
            pre_act = sum(ref[...].astype(jnp.float32) for ref in h_refs)
            d_act = sum(ref[...].astype(jnp.float32) for ref in d_refs)
            value_out, slope = gelu_parts(pre_act)
            d_pre = (d_act * slope).astype(jnp.bfloat16)
            act_ref[...] = value_out.astype(jnp.bfloat16)
            d_pre_ref[...] = d_pre
            held[pl.ds(pl.multiple_of(step * row_tile, row_tile), row_tile), :] = d_pre

        @pl.when(step >= row_steps)
        def _():
            at = pl.ds(pl.multiple_of((step - row_steps) * tile, tile), tile)
            value = contract(w_ref[at, :], held[...], 1, 0).astype(jnp.bfloat16)
            outs[2][...] = value[:, :part]
            outs[3][...] = value[:, part:]

    low = lambda i: (jnp.minimum(i, row_steps - 1), 0)
    d_from = (d_terms[0].shape[0] - hidden) // row_tile
    high = lambda i: (jnp.minimum(i, row_steps - 1) + d_from, 0)
    h_spec, d_spec = pl.BlockSpec((row_tile, cols), low), pl.BlockSpec((row_tile, cols), high)
    shape = jax.ShapeDtypeStruct((hidden, cols), jnp.bfloat16)
    dx_spec = pl.BlockSpec((tile, part), lambda i: (jnp.maximum(i - row_steps, 0), 0))
    dx_shape = jax.ShapeDtypeStruct((depth, part), jnp.bfloat16)
    return pl.pallas_call(
        kernel,
        grid=(row_steps + steps,),
        in_specs=[h_spec] * count + [d_spec] * count + [HELD] + [ANY] * len(after),
        out_specs=[h_spec, h_spec] + [dx_spec, dx_spec],
        out_shape=[shape, shape] + [dx_shape, dx_shape],
        scratch_shapes=[pltpu.VMEM((hidden, cols), jnp.bfloat16)],
        compiler_params=params(5),
        name="gelu",
    )(*h_terms, *d_terms, w_in, *after)


def grad_call(jobs, after, square):
    rows = jobs[0][0][0].shape[0]
    part, cols = jobs[0][1][0].shape[0] // 2, jobs[0][1][0].shape[1]
    tile = tile_of(cols, 256)
    operands, specs, places = [], [], []
    tile_spec = pl.BlockSpec((rows, tile), lambda i: (0, i))
    for lefts, rights, right_at, base in jobs:
        begin = len(operands)
        operands += [*lefts, *rights, *([] if base is None else [base])]
        specs += [pl.BlockSpec((rows, lefts[0].shape[1]), lambda i: (0, 0))] * len(lefts)
        specs += [pl.BlockSpec((part, tile), lambda i, at=right_at: (at, i))] * len(rights)
        specs += [] if base is None else [tile_spec]
        middle = begin + len(lefts)
        places.append((begin, middle, middle + len(rights), base is not None))
    shape = jax.ShapeDtypeStruct((rows, cols), jnp.bfloat16)

    def kernel(*refs):
        outs = refs[len(operands) + len(after) :]
        if square:
            outs[-1][...] = jnp.zeros_like(outs[-1])

        def body(*blocks):
            for (begin, middle, end, based), out_ref in zip(places, blocks[len(operands) :]):
                left = jnp.concatenate([ref[...] for ref in blocks[begin:middle]], axis=1)
                total = contract(left, stacked(blocks[middle:end]), 1, 0)
                if based:
                    total = total + blocks[end][...].astype(jnp.float32)
                out_ref[...] = total.astype(jnp.bfloat16)
                if square:
                    outs[-1][...] += jnp.sum((total * total).reshape(rows // 8, 8, tile), axis=0)

        pltpu.emit_pipeline(
            body, grid=(cols // tile,), in_specs=specs, out_specs=[tile_spec] * len(jobs)
        )(*refs[: len(operands)], *outs[: len(jobs)])

    return pl.pallas_call(
        kernel,
        in_specs=[ANY] * (len(operands) + len(after)),
        out_specs=[ANY] * len(jobs) + [HELD] * square,
        out_shape=[shape] * len(jobs) + [jax.ShapeDtypeStruct((8, tile), jnp.float32)] * square,
        compiler_params=params(WIDE),
        name="grad",
    )(*operands, *after)


def scale_call(factor, flipped, plain, after):
    rows, cols = plain.shape
    steps = cols // tile_of(cols, 256)
    wide, high = cols // steps, rows // steps

    def kernel(factor_ref, *refs):
        def body(flipped_ref, plain_ref, grad_in_ref, grad_out_ref):
            value = flipped_ref[...].astype(jnp.float32) * factor_ref[0, 0]
            grad_in_ref[...] = value.astype(jnp.bfloat16).T
            value = plain_ref[...].astype(jnp.float32) * factor_ref[0, 0]
            grad_out_ref[...] = value.astype(jnp.bfloat16)

        high_spec = pl.BlockSpec((high, cols), lambda i: (i, 0))
        pltpu.emit_pipeline(
            body,
            grid=(steps,),
            in_specs=[pl.BlockSpec((rows, wide), lambda i: (0, i)), high_spec],
            out_specs=[pl.BlockSpec((wide, rows), lambda i: (i, 0)), high_spec],
        )(refs[0], refs[1], refs[-2], refs[-1])

    return pl.pallas_call(
        kernel,
        in_specs=[pl.BlockSpec(memory_space=pltpu.SMEM)] + [ANY] * (2 + len(after)),
        out_specs=[ANY, ANY],
        out_shape=[
            jax.ShapeDtypeStruct((cols, rows), jnp.bfloat16),
            jax.ShapeDtypeStruct((rows, cols), jnp.bfloat16),
        ],
        compiler_params=params(WIDE),
        name="scale",
    )(factor.reshape(1, 1), flipped, plain, *after)


def solution(mesh):
    n_gx, n_gy, n_gz = mesh.shape["gx"], mesh.shape["gy"], mesh.shape["gz"]

    def swap(value, mask):
        return lax.ppermute(value, "gy", [(i, i ^ mask) for i in range(n_gy)])

    def shift(value, axis, size, step):
        return lax.ppermute(value, axis, [(i, (i + step) % size) for i in range(size)])

    def over_gx(value):
        return value + sum(shift(value, "gx", n_gx, step) for step in range(1, n_gx))

    def over_gy_gz(value):
        value = value + sum(swap(value, mask) for mask in range(1, n_gy))
        return value + sum(shift(value, "gz", n_gz, step) for step in range(1, n_gz))

    def width_terms(value):
        if n_gz == 2:
            return [value, shift(value, "gz", n_gz, 1)]
        every = lax.all_gather(value, "gz")
        return [every[i] for i in range(n_gz)]

    pairs = range(0, n_gy, 2)
    leads = [(pair, step) for step in range(min(n_gx, 2)) for pair in pairs]
    leads += [(pair, step) for step in range(2, n_gx) for pair in reversed(pairs)]
    groups = [[(mask, step), (mask + 1, step)] for mask, step in leads]
    count = len(groups)
    last = count - 1
    own_tie = {last - 2: "A in", last - 1: "C", last: "norm"}
    far_tie = {last - 3: ("gelu", last - 2), last - 1: "norm"}

    def shards(tokens, w_in, w_out, out_grad):
        hidden = w_in.shape[1]
        blocks = {(0, 0): jnp.concatenate([tokens, out_grad], axis=0)}
        done = ()
        terms, acts, d_pres, ties = {}, {}, {}, {}
        sums, returned = {}, []

        def later(value, *extra):
            waits = done + extra
            return lax.optimization_barrier((value, waits))[0] if waits else value

        def fetch(block, *extra):
            mask, step = block
            if mask % 2:
                blocks[block] = swap(later(blocks[mask - 1, step], *extra), 1)
            elif mask:
                blocks[block] = swap(later(blocks[0, step], *extra), mask)
            else:
                blocks[block] = shift(later(blocks[0, step - 1], *extra), "gx", n_gx, -1)

        def tie(kernel, value):
            ties.setdefault(kernel, []).append(value)

        def waits(kernel):
            return done + tuple(ties.pop(kernel, ()))

        def run_terms(g):
            nonlocal done
            blocks_of = [blocks[b] for b in groups[g]]
            value = terms_call(blocks_of, w_in_t, w_out, waits(("terms", g)), g == last - 1)
            if g == last - 1:
                done = (value[0],)
                terms[g] = width_terms(value[0]), width_terms(value[1])
                tie(("gelu", last - 2), terms[g][0][-1])
            else:
                done = (value,)
                terms[g] = (width_terms(value),) * 2

        def plus(one, two):
            return (one.astype(jnp.float32) + two.astype(jnp.float32)).astype(jnp.bfloat16)

        def give_back(g, dx):
            pair, step = leads[g]
            sums[pair, step] = plus(dx[0], swap(dx[1], 1))
            tie(own_tie.get(g, ("gelu", g + 1)), sums[pair, step])
            if pair:
                sums[pair, step] = swap(sums[pair, step], pair)
                tie(far_tie.get(g, ("gelu", g + 3 - (g > 1))), sums[pair, step])
            if g < last and all((p, step) in sums for p in pairs):
                finish(step)
                if step:
                    tie(("gelu", min(g + 3, last - 1)), returned[-1])

        def finish(step):
            total = sums[0, step]
            for p in pairs[1:]:
                total = plus(total, later(sums[p, step]) if step == n_gx - 1 else sums[p, step])
            returned.append(shift(total, "gx", n_gx, step) if step else total)

        def run_gelu(g):
            nonlocal done
            outs = gelu_call(*terms[g], w_in, waits(("gelu", g)))
            acts[g], d_pres[g] = outs[:2]
            done = (outs[0],)
            give_back(g, outs[2:])

        def run_grads(stage, gin_from, gout_from, end, bases, square=False):
            nonlocal done
            jobs = []
            for which, begin in ((0, gin_from), (1, gout_from)):
                if begin is not None:
                    lefts = [(acts if which else d_pres)[g] for g in range(begin, end)]
                    rights = [blocks[b] for g in range(begin, end) for b in groups[g]]
                    jobs.append((lefts, rights, which, bases[which]))
            outs = grad_call(jobs, waits(stage), square)
            done = (outs[0],)
            return outs

        fetch((1, 0))
        for pair in pairs[1:]:
            fetch((pair, 0))
        fetch((0, 1))
        first = [blocks[b] for b in groups[0]]
        h_own = half_call(first, 0, w_in, 0, done)
        d_own = half_call(first, 1, w_out, 1, (h_own,))
        h_terms = width_terms(h_own)
        most = 3 * hidden // 4
        d_parts = [width_terms(d_own[:most]), width_terms(d_own[most:])]
        w_in_t = flip_call(w_in, (d_own,))
        done = (w_in_t,)
        early = (h_terms[-1], d_parts[0][-1], blocks[0, 1])
        for pair in pairs[1:]:
            fetch((pair + 1, 0), *early)
        tie(("terms", 1), blocks[0, 1])

        def next_turn(turn):
            if turn + 1 < n_gx:
                fetch((0, turn + 1))
                tie(("gelu", turn), blocks[0, turn + 1])
            if turn < n_gx:
                for pair in pairs[1:]:
                    fetch((pair, turn))
                    tie(("gelu", turn), blocks[pair, turn])
                fetch((1, turn))
            if turn > 1:
                for pair in pairs[1:]:
                    fetch((pair + 1, turn - 1))

        next_turn(1)
        none = (None, None)
        for g in range(1, count):
            run_terms(g)
            if 1 < g <= n_gx:
                next_turn(g)
            if g == 1:
                others = [[later(v) for v in part[-max(1, len(part) * (n_gz > 2)) :]] for part in d_parts]
                d_terms = [jnp.concatenate(both, axis=0) for both in zip(*others)]
                terms[0] = h_terms, d_terms if n_gz > 2 else [d_own] + d_terms
            if g < last:
                run_gelu(g - 1)
            else:
                (gin,) = run_grads("A in", 0, None, last - 1, none)
                (gout,) = run_grads("A out", None, 0, last - 1, none)
                run_gelu(g - 1)
        run_gelu(last)
        gin, gout, squares = run_grads("C", last - 1, last - 1, count, (gin, gout), True)

        finish(n_gx - 1)
        square = jnp.broadcast_to(jnp.sum(squares), (8, 128))
        square = lax.optimization_barrier((over_gx(square), waits("norm")))[0]
        square = over_gy_gz(square)[0, 0]
        in_grad = sum(piece.astype(jnp.float32) for piece in returned).astype(jnp.bfloat16).T

        entries = 2.0 * (w_in.shape[0] * n_gz) * (w_in.shape[1] * n_gx * n_gy)
        factor = 1.0 / jnp.sqrt(square / entries + 1e-06)
        return (in_grad, *scale_call(factor, gin, gout, ()))

    placed = (
        P(("gy", "gx"), "gz"),
        P("gz", ("gx", "gy")),
        P(("gx", "gy"), "gz"),
        P(("gy", "gx"), "gz"),
    )
    return jax.shard_map(
        shards,
        mesh=mesh,
        in_specs=placed,
        out_specs=(P(("gy", "gx"), "gz"), P("gz", ("gx", "gy")), P(("gx", "gy"), "gz")),
        check_vma=False,
    )
```

time: 416 us -> 439 us (1.055)
  waiting for transfers between devices: 113 us -> 167 us
  local copies, waits for them, and re-layouts: 57.4 us -> 28.5 us
    ppermute x20 -> x21, waiting for transfers between devices: 48.8 us -> 102 us  [shift(): lax.ppermute(value, axis, [(i, (i + step) % size) for i in range(size)])]
    unnamed x202 -> x114, local copies, waits for them, and re-layouts: 56.7 us -> 27.2 us
    pallas_call x18 -> x13, Pallas kernels: 142 us -> 148 us  [the longest x3 82.4 us: grad_call(): pl.pallas_call(kernel, in_specs=[ANY] * (len(operands) + len(after)), out...]
    convert_element_type x9, other arithmetic: 8.95 us -> 4.12 us  [plus(): (one.astype(jnp.float32) + two.astype(jnp.float32)).astype(jnp.bfloat16)]
    ppermute x20 -> x21, starting transfers between devices: 26.8 us -> 25.7 us  [shift(): lax.ppermute(value, axis, [(i, (i + step) % size) for i in range(size)])]
  transfers between devices with their start and end apart: 47 -> 48, of which waited for: 18 -> 20; matrix products, arithmetic and copies ran while one was open for 2% -> 1% of each run, Pallas kernels for 41% -> 43%
where the time goes in v2:
time: 439 us; the launch traced here: 435 us
  Pallas kernels  191 us (44%)
  waiting for transfers between devices  167 us (38%)
  starting transfers between devices  39.7 us (9%)
  local copies, waits for them, and re-layouts  28.5 us (6%)
  other arithmetic  7.31 us (2%)
    ppermute x21, waiting for transfers between devices, shift(): lax.ppermute(value, axis, [(i, (i + step) % size) for i in range(size)])  102 us
    pallas_call x3, Pallas kernels, grad_call(): pl.pallas_call(kernel, in_specs=[ANY] * (len(operands) + len(after)), out...  82.4 us
    ppermute x27, waiting for transfers between devices, swap(): return lax.ppermute(value, 'gy', [(i, i ^ mask) for i in range(n_gy)])  64.7 us
    pallas_call x7, Pallas kernels, terms_call(): pl.pallas_call(kernel, grid=(2 * steps,), in_specs=[once((rows, depth), 0...  40.8 us
    pallas_call x8, Pallas kernels, gelu_call(): pl.pallas_call(kernel, grid=(row_steps + steps,), in_specs=[h_spec] * cou...  39.5 us
    unnamed x114, local copies, waits for them, and re-layouts  27.2 us
    ppermute x21, starting transfers between devices, shift(): lax.ppermute(value, axis, [(i, (i + step) % size) for i in range(size)])  25.7 us
    pallas_call x1, Pallas kernels, scale_call(): pl.pallas_call(kernel, in_specs=[pl.BlockSpec(memory_space=pltpu.SMEM)] +...  19 us
  transfers between devices with their start and end apart: 48, of which 20 were waited for; matrix products, arithmetic and copies ran while one was open for 1% of the time, Pallas kernels for 43%

profile of v2, /device:TPU:8, one launch (start us, length us, event | category | flops | bytes accessed | tf_op | source)
XLA Modules:
  0.0 435.3 jit_solution(17658505839950802492)
XLA Ops:
  2.2 1.9 collective-permute-start.3
  5.5 3.7 copy-done
  9.2 2.9 half_terms.2.refs_3_.refs_0_
  13.8 3.7 copy-done.3
  17.4 2.8 half_terms.3.refs_0_.refs_2_
  21.0 3.6 flip.1.refs_4_.refs_6_
  24.6 14.4 %collective-permute-done.4.refs_7_.refs_0_.refs_2_.refs_10_ = bf16[256,3072]{1,0:T(8,128)(2,1)S(1)} collective-permute-done((bf16[256,3072]{1,0:T(8,128)(2,1)S(1)}, bf16[256,3072]{1,0:T(8,128)(2,1)S(1)}, u32[]{:S(2)}, u32[]{:S(2)}) %collective-permute-start.4) | collective-permute-done | bytes 1572896 | tf_op jit(solution)/shard_map/ppermute | solution.py:277
  39.0 5.5 %collective-permute-done.2 = bf16[1152,256]{1,0:T(8,128)(2,1)S(1)} collective-permute-done((bf16[1152,256]{1,0:T(8,128)(2,1)S(1)}, bf16[1152,256]{1,0:T(8,128)(2,1)S(1)}, u32[]{:S(2)}, u32[]{:S(2)}) %collective-permute-start.2) | collective-permute-done | bytes 589856 | tf_op jit(solution)/shard_map/ppermute | solution.py:277
  49.1 5.7 %terms.7.refs_5_.refs_0_.refs_2_ = bf16[3072,256]{1,0:T(8,128)(2,1)S(1)} custom-call(bf16[256,3072]{1,0:T(8,128)(2,1)S(1)} %collective-permute-done.3.refs_0_.refs_2_.refs_8_, bf16[256,3072]{1,0:T(8,128)(2,1)S(1)} %collective-permute-done.5.refs_1_.refs_3_.refs_9_, bf16[256,3072]{1,0:T(8,128)(2,1)S(1)} %collective-permute-done.3.refs_0_.refs_2_.refs_8_, ...), custom_call_target="tpu_custom_call" | custom-call | tf_op jit(solution)/shard_map/terms/pallas_call | solution.py:100
  55.5 4.7 %gelu.8 = (bf16[1536,256]{1,0:T(8,128)(2,1)S(1)}, bf16[1536,256]{1,0:T(8,128)(2,1)S(1)}, bf16[3072,128]{1,0:T(8,128)(2,1)S(1)}, bf16[3072,128]{1,0:T(8,128)(2,1)S(1)}) custom-call(bf16[1536,256]{1,0:T(8,128)(2,1)S(1)} %half_terms.2.refs_3_.refs_0_, bf16[1536,256]{1,0:T(8,128)(2,1)S(1)} %collective-permute-done.1.refs_1_, ...), custom_call_target="tpu_custom_call" | custom-call | tf_op jit(solution)/shard_map/gelu/pallas_call | solution.py:180
  60.3 5.7 %terms.8.refs_5_.refs_0_.refs_2_ = bf16[3072,256]{1,0:T(8,128)(2,1)S(1)} custom-call(bf16[256,3072]{1,0:T(8,128)(2,1)S(1)} %collective-permute-done.4.refs_7_.refs_0_.refs_2_.refs_10_, bf16[256,3072]{1,0:T(8,128)(2,1)S(1)} %collective-permute-done.9.refs_1_.refs_3_.refs_11_, bf16[256,3072]{1,0:T(8,128)(2,1)S(1)} %collective-permute-done.4.refs_7_.refs_0_.refs_2_.refs_10_, ...), custom_call_target="tpu_custom_call" | custom-call | tf_op jit(solution)/shard_map/terms/pallas_call | solution.py:100
  66.1 15.2 %collective-permute-done.11.refs_7_.refs_0_.refs_2_.refs_12_ = bf16[256,3072]{1,0:T(8,128)(2,1)S(1)} collective-permute-done((bf16[256,3072]{1,0:T(8,128)(2,1)S(1)}, bf16[256,3072]{1,0:T(8,128)(2,1)S(1)}, u32[]{:S(2)}, u32[]{:S(2)}) %collective-permute-start.11) | collective-permute-done | bytes 1572896 | tf_op jit(solution)/shard_map/ppermute | solution.py:274
  83.0 1.9 collective-permute-start.16
  86.7 5.6 %collective-permute-done.8.refs_1_.refs_3_ = bf16[3072,256]{1,0:T(8,128)(2,1)S(1)} collective-permute-done((bf16[3072,256]{1,0:T(8,128)(2,1)S(1)}, bf16[3072,256]{1,0:T(8,128)(2,1)S(1)}, u32[]{:S(2)}, u32[]{:S(2)}) %collective-permute-start.8) | collective-permute-done | bytes 1572896 | tf_op jit(solution)/shard_map/ppermute | solution.py:277
  94.8 4.7 %gelu.9 = (bf16[1536,256]{1,0:T(8,128)(2,1)S(1)}, bf16[1536,256]{1,0:T(8,128)(2,1)S(1)}, bf16[3072,128]{1,0:T(8,128)(2,1)S(1)}, bf16[3072,128]{1,0:T(8,128)(2,1)S(1)}) custom-call(bf16[3072,256]{1,0:T(8,128)(2,1)S(1)} %copy-done.18, bf16[3072,256]{1,0:T(8,128)(2,1)S(1)} %copy-done.26, bf16[3072,256]{1,0:T(8,128)(2,1)S(1)} %copy-done.18, ...), custom_call_target="tpu_custom_call" | custom-call | tf_op jit(solution)/shard_map/gelu/pallas_call | solution.py:180
  99.7 5.7 %terms.9.refs_5_.refs_0_.refs_2_ = bf16[3072,256]{1,0:T(8,128)(2,1)S(1)} custom-call(bf16[256,3072]{1,0:T(8,128)(2,1)S(1)} %collective-permute-done.11.refs_7_.refs_0_.refs_2_.refs_12_, bf16[256,3072]{1,0:T(8,128)(2,1)S(1)} %collective-permute-done.15.refs_1_.refs_3_.refs_13_, bf16[256,3072]{1,0:T(8,128)(2,1)S(1)} %collective-permute-done.11.refs_7_.refs_0_.refs_2_.refs_12_, ...), custom_call_target="tpu_custom_call" | custom-call | tf_op jit(solution)/shard_map/terms/pallas_call | solution.py:100
  105.4 12.7 %collective-permute-done.17.refs_7_.refs_0_.refs_2_.refs_14_ = bf16[256,3072]{1,0:T(8,128)(2,1)S(1)} collective-permute-done((bf16[256,3072]{1,0:T(8,128)(2,1)S(1)}, bf16[256,3072]{1,0:T(8,128)(2,1)S(1)}, u32[]{:S(2)}, u32[]{:S(2)}) %collective-permute-start.17) | collective-permute-done | bytes 1572896 | tf_op jit(solution)/shard_map/ppermute | solution.py:274
  121.3 4.6 %collective-permute-done.14.refs_1_.refs_3_ = bf16[3072,256]{1,0:T(8,128)(2,1)S(1)} collective-permute-done((bf16[3072,256]{1,0:T(8,128)(2,1)S(1)}, bf16[3072,256]{1,0:T(8,128)(2,1)S(1)}, u32[]{:S(2)}, u32[]{:S(2)}) %collective-permute-start.14) | collective-permute-done | bytes 1572896 | tf_op jit(solution)/shard_map/ppermute | solution.py:277
  126.0 4.7 %gelu.10 = (bf16[1536,256]{1,0:T(8,128)(2,1)S(1)}, bf16[1536,256]{1,0:T(8,128)(2,1)S(1)}, bf16[3072,128]{1,0:T(8,128)(2,1)S(1)}, bf16[3072,128]{1,0:T(8,128)(2,1)S(1)}) custom-call(bf16[3072,256]{1,0:T(8,128)(2,1)S(1)} %terms.8.refs_5_.refs_0_.refs_2_, bf16[3072,256]{1,0:T(8,128)(2,1)S(1)} %collective-permute-done.14.refs_1_.refs_3_, ...), custom_call_target="tpu_custom_call" | custom-call | tf_op jit(solution)/shard_map/gelu/pallas_call | solution.py:180
  131.3 5.7 %terms.10.refs_5_.refs_0_.refs_2_ = bf16[3072,256]{1,0:T(8,128)(2,1)S(1)} custom-call(bf16[256,3072]{1,0:T(8,128)(2,1)S(1)} %collective-permute-done.17.refs_7_.refs_0_.refs_2_.refs_14_, bf16[256,3072]{1,0:T(8,128)(2,1)S(1)} %collective-permute-done.20.refs_1_.refs_3_.refs_15_, ...), custom_call_target="tpu_custom_call" | custom-call | tf_op jit(solution)/shard_map/terms/pallas_call | solution.py:100
  137.8 18.4 %collective-permute-done.21.refs_6_.refs_0_.refs_2_.refs_9_ = bf16[256,3072]{1,0:T(8,128)(2,1)S(1)} collective-permute-done((bf16[256,3072]{1,0:T(8,128)(2,1)S(1)}, bf16[256,3072]{1,0:T(8,128)(2,1)S(1)}, u32[]{:S(2)}, u32[]{:S(2)}) %collective-permute-start.21) | collective-permute-done | bytes 1572896 | tf_op jit(solution)/shard_map/ppermute | solution.py:274
  156.1 3.5 collective-permute-done.19.refs_1_.refs_3_
  159.7 4.7 %gelu.11 = (bf16[1536,256]{1,0:T(8,128)(2,1)S(1)}, bf16[1536,256]{1,0:T(8,128)(2,1)S(1)}, bf16[3072,128]{1,0:T(8,128)(2,1)S(1)}, bf16[3072,128]{1,0:T(8,128)(2,1)S(1)}) custom-call(bf16[3072,256]{1,0:T(8,128)(2,1)S(1)} %terms.9.refs_5_.refs_0_.refs_2_, bf16[3072,256]{1,0:T(8,128)(2,1)S(1)} %collective-permute-done.19.refs_1_.refs_3_, ...), custom_call_target="tpu_custom_call" | custom-call | tf_op jit(solution)/shard_map/gelu/pallas_call | solution.py:180
  166.5 5.7 %terms.11.refs_5_.refs_0_.refs_2_ = bf16[3072,256]{1,0:T(8,128)(2,1)S(1)} custom-call(bf16[256,3072]{1,0:T(8,128)(2,1)S(1)} %collective-permute-done.10.refs_6_.refs_0_.refs_2_.refs_16_, bf16[256,3072]{1,0:T(8,128)(2,1)S(1)} %collective-permute-done.25.refs_1_.refs_3_.refs_17_, ...), custom_call_target="tpu_custom_call" | custom-call | tf_op jit(solution)/shard_map/terms/pallas_call | solution.py:100
  172.4 12.1 %collective-permute-done.13.refs_6_ = bf16[3072,128]{1,0:T(8,128)(2,1)S(1)} collective-permute-done((bf16[3072,128]{1,0:T(8,128)(2,1)S(1)}, bf16[3072,128]{1,0:T(8,128)(2,1)S(1)}, u32[]{:S(2)}, u32[]{:S(2)}) %collective-permute-start.13) | collective-permute-done | bytes 786464 | tf_op jit(solution)/shard_map/ppermute | solution.py:274
  184.5 7.0 %collective-permute-done.28.refs_1_.refs_3_ = bf16[3072,256]{1,0:T(8,128)(2,1)S(1)} collective-permute-done((bf16[3072,256]{1,0:T(8,128)(2,1)S(1)}, bf16[3072,256]{1,0:T(8,128)(2,1)S(1)}, u32[]{:S(2)}, u32[]{:S(2)}) %collective-permute-start.28) | collective-permute-done | bytes 1572896 | tf_op jit(solution)/shard_map/ppermute | solution.py:277
  191.5 4.7 %gelu.12 = (bf16[1536,256]{1,0:T(8,128)(2,1)S(1)}, bf16[1536,256]{1,0:T(8,128)(2,1)S(1)}, bf16[3072,128]{1,0:T(8,128)(2,1)S(1)}, bf16[3072,128]{1,0:T(8,128)(2,1)S(1)}) custom-call(bf16[3072,256]{1,0:T(8,128)(2,1)S(1)} %terms.10.refs_5_.refs_0_.refs_2_, bf16[3072,256]{1,0:T(8,128)(2,1)S(1)} %collective-permute-done.28.refs_1_.refs_3_, ...), custom_call_target="tpu_custom_call" | custom-call | tf_op jit(solution)/shard_map/gelu/pallas_call | solution.py:180
  199.9 6.5 %terms.12 = (bf16[1536,256]{1,0:T(8,128)(2,1)S(1)}, bf16[1536,256]{1,0:T(8,128)(2,1)}) custom-call(bf16[256,3072]{1,0:T(8,128)(2,1)S(1)} %collective-permute-done.21.refs_6_.refs_0_.refs_2_.refs_9_, bf16[256,3072]{1,0:T(8,128)(2,1)S(1)} %collective-permute-done.27.refs_1_.refs_3_.refs_10_, ...), custom_call_target="tpu_custom_call" | custom-call | tf_op jit(solution)/shard_map/terms/pallas_call | solution.py:100
  207.9 26.4 %collective-permute-done.26.refs_1_.refs_3_ = bf16[3072,256]{1,0:T(8,128)(2,1)S(1)} collective-permute-done((bf16[3072,256]{1,0:T(8,128)(2,1)S(1)}, bf16[3072,256]{1,0:T(8,128)(2,1)S(1)}, u32[]{:S(2)}, u32[]{:S(2)}) %collective-permute-start.26) | collective-permute-done | bytes 1572896 | tf_op jit(solution)/shard_map/ppermute | solution.py:277
  234.3 16.5 %collective-permute-done.31.refs_9_.refs_1_ = bf16[1536,256]{1,0:T(8,128)(2,1)S(1)} collective-permute-done((bf16[1536,256]{1,0:T(8,128)(2,1)S(1)}, bf16[1536,256]{1,0:T(8,128)(2,1)S(1)}, u32[]{:S(2)}, u32[]{:S(2)}) %collective-permute-start.31) | collective-permute-done | bytes 786464 | tf_op jit(solution)/shard_map/ppermute | solution.py:277
  250.8 4.7 %gelu.13 = (bf16[1536,256]{1,0:T(8,128)(2,1)S(1)}, bf16[1536,256]{1,0:T(8,128)(2,1)S(1)}, bf16[3072,128]{1,0:T(8,128)(2,1)S(1)}, bf16[3072,128]{1,0:T(8,128)(2,1)S(1)}) custom-call(bf16[3072,256]{1,0:T(8,128)(2,1)S(1)} %terms.11.refs_5_.refs_0_.refs_2_, bf16[3072,256]{1,0:T(8,128)(2,1)S(1)} %collective-permute-done.26.refs_1_.refs_3_, ...), custom_call_target="tpu_custom_call" | custom-call | tf_op jit(solution)/shard_map/gelu/pallas_call | solution.py:180
  261.5 3.1 collective-permute-start.33
  264.6 5.7 %terms.13.refs_18_.refs_0_.refs_2_ = bf16[3072,256]{1,0:T(8,128)(2,1)S(1)} custom-call(bf16[256,3072]{1,0:T(8,128)(2,1)S(1)} %collective-permute-done.16.refs_6_.refs_0_.refs_2_.refs_4_.refs_11_, bf16[256,3072]{1,0:T(8,128)(2,1)S(1)} %collective-permute-done.34.refs_1_.refs_3_.refs_5_.refs_12_, ...), custom_call_target="tpu_custom_call" | custom-call | tf_op jit(solution)/shard_map/terms/pallas_call | solution.py:100
  271.9 27.1 %grad.3.refs_18_.refs_6_ = bf16[1536,3072]{1,0:T(8,128)(2,1)} custom-call(bf16[1536,256]{1,0:T(8,128)(2,1)} %copy-done.39, bf16[1536,256]{1,0:T(8,128)(2,1)} %copy-done.40, bf16[1536,256]{1,0:T(8,128)(2,1)} %copy-done.41, bf16[1536,256]{1,0:T(8,128)(2,1)} %copy-done.42, bf16[1536,256]{1,0:T(8,128)(2,1)} %copy-done.43, bf16[1536,256]{1,0:T(8,128)(2,1)} %copy-done.44, ...), custom_call_target="tpu_custom_call" | custom-call | tf_op jit(solution)/shard_map/grad/pallas_call | solution.py:227
  299.0 27.1 %grad.4.refs_5_.refs_13_ = bf16[1536,3072]{1,0:T(8,128)(2,1)} custom-call(bf16[1536,256]{1,0:T(8,128)(2,1)} %copy-done.34, bf16[1536,256]{1,0:T(8,128)(2,1)} %copy-done.35, bf16[1536,256]{1,0:T(8,128)(2,1)} %copy-done.36, bf16[1536,256]{1,0:T(8,128)(2,1)} %copy-done.37, bf16[1536,256]{1,0:T(8,128)(2,1)} %copy-done.33, bf16[1536,256]{1,0:T(8,128)(2,1)} %copy-done.38, ...), custom_call_target="tpu_custom_call" | custom-call | tf_op jit(solution)/shard_map/grad/pallas_call | solution.py:227
  326.2 3.7 copy-done.1
  329.8 3.7 copy-done.4
  333.5 6.5 %gelu.14 = (bf16[1536,256]{1,0:T(8,128)(2,1)S(1)}, bf16[1536,256]{1,0:T(8,128)(2,1)S(1)}, bf16[3072,128]{1,0:T(8,128)(2,1)S(1)}, bf16[3072,128]{1,0:T(8,128)(2,1)S(1)}) custom-call(bf16[1536,256]{1,0:T(8,128)(2,1)S(1)} %get-tuple-element.75.refs_5_.refs_0_, bf16[1536,256]{1,0:T(8,128)(2,1)S(1)} %collective-permute-done.31.refs_9_.refs_1_, ...), custom_call_target="tpu_custom_call" | custom-call | tf_op jit(solution)/shard_map/gelu/pallas_call | solution.py:180
  340.9 2.3 collective-permute-done.38
  344.0 3.7 copy-done.2
  347.7 4.7 %gelu.15 = (bf16[1536,256]{1,0:T(8,128)(2,1)S(1)}, bf16[1536,256]{1,0:T(8,128)(2,1)S(1)}, bf16[3072,128]{1,0:T(8,128)(2,1)S(1)}, bf16[3072,128]{1,0:T(8,128)(2,1)S(1)}) custom-call(bf16[3072,256]{1,0:T(8,128)(2,1)S(1)} %copy-done.24, bf16[3072,256]{1,0:T(8,128)(2,1)S(1)} %collective-permute-done.35.refs_1_.refs_3_, bf16[3072,256]{1,0:T(8,128)(2,1)S(1)} %copy-done.24, ...), custom_call_target="tpu_custom_call" | custom-call | tf_op jit(solution)/shard_map/gelu/pallas_call | solution.py:180
  354.3 28.2 %grad.5 = (bf16[1536,3072]{1,0:T(8,128)(2,1)}, bf16[1536,3072]{1,0:T(8,128)(2,1)}, f32[8,256]{1,0:T(8,128)}) custom-call(bf16[1536,256]{1,0:T(8,128)(2,1)} %copy-done.45, bf16[1536,256]{1,0:T(8,128)(2,1)} %copy-done.46, bf16[256,3072]{1,0:T(8,128)(2,1)} %copy-done.5, bf16[256,3072]{1,0:T(8,128)(2,1)} %copy-done.14, bf16[256,3072]{1,0:T(8,128)(2,1)} %copy-done.7, ...), custom_call_target="tpu_custom_call" | custom-call | tf_op jit(solution)/shard_map/grad/pallas_call | solution.py:227
  386.2 2.1 collective-permute-start.42
  388.3 14.5 %collective-permute-done.41 = f32[8,128]{1,0:T(8,128)S(1)} collective-permute-done((f32[8,128]{1,0:T(8,128)S(1)}, f32[8,128]{1,0:T(8,128)S(1)}, u32[]{:S(2)}, u32[]{:S(2)}) %collective-permute-start.41) | collective-permute-done | bytes 4128 | tf_op jit(solution)/shard_map/ppermute | solution.py:277
  405.7 1.8 collective-permute-done.45
  409.5 2.6 collective-permute-done.47
  413.3 19.0 %scale.1 = (bf16[3072,1536]{1,0:T(8,128)(2,1)}, bf16[1536,3072]{1,0:T(8,128)(2,1)}) custom-call(f32[1,1]{1,0:T(1,128)S(6)} %sqrt.3.factor_ref, bf16[1536,3072]{1,0:T(8,128)(2,1)} %get-tuple-element.96.refs_0_, bf16[1536,3072]{1,0:T(8,128)(2,1)} %get-tuple-element.100.refs_1_), custom_call_target="tpu_custom_call" | custom-call | tf_op jit(solution)/shard_map/scale/pallas_call | solution.py:257
  432.2 1.9 fusion
  (206 shorter events, 50.1 us)
Async XLA Ops:
  2.1 3.5 collective-permute-start
  2.1 36.8 %collective-permute-start.4 = (bf16[256,3072]{1,0:T(8,128)(2,1)S(1)}, bf16[256,3072]{1,0:T(8,128)(2,1)S(1)}, u32[]{:S(2)}, u32[]{:S(2)}) collective-permute-start(bf16[256,3072]{1,0:T(8,128)(2,1)S(1)} %constant_dynamic-update-slice_fusion.refs_0_.refs_6_), channel_id=1, source_target_pairs={{0,24},{8,0},{16,8},{24,16},{1,25},{9,1},{17,9},{25,17},{2,26},{10... | collective-permute-start | bytes 4718600 | tf_op jit(solution)/shard_map/ppermute | solution.py:277
  2.2 36.7 %collective-permute-start.3 = (bf16[256,3072]{1,0:T(8,128)(2,1)S(1)}, bf16[256,3072]{1,0:T(8,128)(2,1)S(1)}, u32[]{:S(2)}, u32[]{:S(2)}) collective-permute-start(bf16[256,3072]{1,0:T(8,128)(2,1)S(1)} %constant_dynamic-update-slice_fusion.refs_0_.refs_6_), channel_id=1, source_target_pairs={{0,4},{2,6},{4,0},{6,2},{1,5},{3,7},{5,1},{7,3},{8,12},{10,14},{12... | collective-permute-start | bytes 4718600 | tf_op jit(solution)/shard_map/ppermute | solution.py:274
  12.2 32.3 %collective-permute-start.1 = (bf16[1536,256]{1,0:T(8,128)(2,1)S(1)}, bf16[1536,256]{1,0:T(8,128)(2,1)S(1)}, u32[]{:S(2)}, u32[]{:S(2)}) collective-permute-start(bf16[1536,256]{1,0:T(8,128)(2,1)S(1)} %half_terms.2.refs_3_.refs_0_), channel_id=1, source_target_pairs={{0,1},{1,0},{2,3},{3,2},{4,5},{5,4},{6,7},{7,6},{8,9},{9,8},{10,11... | collective-permute-start | bytes 2359304 | tf_op jit(solution)/shard_map/ppermute | solution.py:277
  20.4 24.1 %collective-permute-start.2 = (bf16[1152,256]{1,0:T(8,128)(2,1)S(1)}, bf16[1152,256]{1,0:T(8,128)(2,1)S(1)}, u32[]{:S(2)}, u32[]{:S(2)}) collective-permute-start(bf16[1152,256]{1,0:T(8,128)(2,1)S(1)} %slice.12), channel_id=1, source_target_pairs={{0,1},{1,0},{2,3},{3,2},{4,5},{5,4},{6,7},{7,6},{8,9},{9,8},{10,11... | collective-permute-start | bytes 1769480 | tf_op jit(solution)/shard_map/ppermute | solution.py:277
  44.5 4.6 %collective-permute-start.5 = (bf16[256,3072]{1,0:T(8,128)(2,1)S(1)}, bf16[256,3072]{1,0:T(8,128)(2,1)S(1)}, u32[]{:S(2)}, u32[]{:S(2)}) collective-permute-start(bf16[256,3072]{1,0:T(8,128)(2,1)S(1)} %collective-permute-done.3.refs_0_.refs_2_.refs_8_), channel_id=1, source_target_pairs={{0,2},{2,0},{4,6},{6,4},{1,3},{3,1},{5,7},{7,5},{8,10},{10,8},{12,... | collective-permute-start | bytes 4718600 | tf_op jit(solution)/shard_map/ppermute | solution.py:274
  44.5 15.9 %collective-permute-start.9 = (bf16[256,3072]{1,0:T(8,128)(2,1)S(1)}, bf16[256,3072]{1,0:T(8,128)(2,1)S(1)}, u32[]{:S(2)}, u32[]{:S(2)}) collective-permute-start(bf16[256,3072]{1,0:T(8,128)(2,1)S(1)} %collective-permute-done.4.refs_7_.refs_0_.refs_2_.refs_10_), channel_id=1, source_target_pairs={{0,2},{2,0},{4,6},{6,4},{1,3},{3,1},{5,7},{7,5},{8,10},{10,8},{12,... | collective-permute-start | bytes 4718600 | tf_op jit(solution)/shard_map/ppermute | solution.py:274
  45.0 36.3 %collective-permute-start.11 = (bf16[256,3072]{1,0:T(8,128)(2,1)S(1)}, bf16[256,3072]{1,0:T(8,128)(2,1)S(1)}, u32[]{:S(2)}, u32[]{:S(2)}) collective-permute-start(bf16[256,3072]{1,0:T(8,128)(2,1)S(1)} %collective-permute-done.4.refs_7_.refs_0_.refs_2_.refs_10_), channel_id=1, source_target_pairs={{0,4},{2,6},{4,0},{6,2},{1,5},{3,7},{5,1},{7,3},{8,12},{10,14},{12... | collective-permute-start | bytes 4718600 | tf_op jit(solution)/shard_map/ppermute | solution.py:274
  46.5 36.0 %collective-permute-start.10 = (bf16[256,3072]{1,0:T(8,128)(2,1)S(1)}, bf16[256,3072]{1,0:T(8,128)(2,1)S(1)}, u32[]{:S(2)}, u32[]{:S(2)}) collective-permute-start(bf16[256,3072]{1,0:T(8,128)(2,1)S(1)} %collective-permute-done.4.refs_7_.refs_0_.refs_2_.refs_10_), channel_id=1, source_target_pairs={{0,24},{8,0},{16,8},{24,16},{1,25},{9,1},{17,9},{25,17},{2,26},{10... | collective-permute-start | bytes 4718600 | tf_op jit(solution)/shard_map/ppermute | solution.py:277
  47.5 8.0 %collective-permute-start.6 = (bf16[384,256]{1,0:T(8,128)(2,1)S(1)}, bf16[384,256]{1,0:T(8,128)(2,1)S(1)}, u32[]{:S(2)}, u32[]{:S(2)}) collective-permute-start(bf16[384,256]{1,0:T(8,128)(2,1)S(1)} %slice.13), channel_id=1, source_target_pairs={{0,1},{1,0},{2,3},{3,2},{4,5},{5,4},{6,7},{7,6},{8,9},{9,8},{10,11... | collective-permute-start | bytes 589832 | tf_op jit(solution)/shard_map/ppermute | solution.py:277
  54.9 37.4 %collective-permute-start.8 = (bf16[3072,256]{1,0:T(8,128)(2,1)S(1)}, bf16[3072,256]{1,0:T(8,128)(2,1)S(1)}, u32[]{:S(2)}, u32[]{:S(2)}) collective-permute-start(bf16[3072,256]{1,0:T(8,128)(2,1)S(1)} %terms.7.refs_5_.refs_0_.refs_2_), channel_id=1, source_target_pairs={{0,1},{1,0},{2,3},{3,2},{4,5},{5,4},{6,7},{7,6},{8,9},{9,8},{10,11... | collective-permute-start | bytes 4718600 | tf_op jit(solution)/shard_map/ppermute | solution.py:277
  60.2 24.7 %collective-permute-start.7 = (bf16[3072,128]{1,0:T(8,128)(2,1)S(1)}, bf16[3072,128]{1,0:T(8,128)(2,1)S(1)}, u32[]{:S(2)}, u32[]{:S(2)}) collective-permute-start(bf16[3072,128]{1,0:T(8,128)(2,1)S(1)} %get-tuple-element.57), channel_id=1, source_target_pairs={{0,2},{2,0},{4,6},{6,4},{1,3},{3,1},{5,7},{7,5},{8,10},{10,8},{12,... | collective-permute-start | bytes 2359304 | tf_op jit(solution)/shard_map/ppermute | solution.py:274
  81.3 18.4 %collective-permute-start.15 = (bf16[256,3072]{1,0:T(8,128)(2,1)S(1)}, bf16[256,3072]{1,0:T(8,128)(2,1)S(1)}, u32[]{:S(2)}, u32[]{:S(2)}) collective-permute-start(bf16[256,3072]{1,0:T(8,128)(2,1)S(1)} %collective-permute-done.11.refs_7_.refs_0_.refs_2_.refs_12_), channel_id=1, source_target_pairs={{0,2},{2,0},{4,6},{6,4},{1,3},{3,1},{5,7},{7,5},{8,10},{10,8},{12,... | collective-permute-start | bytes 4718600 | tf_op jit(solution)/shard_map/ppermute | solution.py:274
  82.5 35.6 %collective-permute-start.17 = (bf16[256,3072]{1,0:T(8,128)(2,1)S(1)}, bf16[256,3072]{1,0:T(8,128)(2,1)S(1)}, u32[]{:S(2)}, u32[]{:S(2)}) collective-permute-start(bf16[256,3072]{1,0:T(8,128)(2,1)S(1)} %collective-permute-done.10.refs_6_.refs_0_.refs_2_.refs_16_), channel_id=1, source_target_pairs={{0,4},{2,6},{4,0},{6,2},{1,5},{3,7},{5,1},{7,3},{8,12},{10,14},{12... | collective-permute-start | bytes 4718600 | tf_op jit(solution)/shard_map/ppermute | solution.py:274
  83.0 36.6 %collective-permute-start.16 = (bf16[256,3072]{1,0:T(8,128)(2,1)S(1)}, bf16[256,3072]{1,0:T(8,128)(2,1)S(1)}, u32[]{:S(2)}, u32[]{:S(2)}) collective-permute-start(bf16[256,3072]{1,0:T(8,128)(2,1)S(1)} %collective-permute-done.10.refs_6_.refs_0_.refs_2_.refs_16_), channel_id=1, source_target_pairs={{0,24},{8,0},{16,8},{24,16},{1,25},{9,1},{17,9},{25,17},{2,26},{10... | collective-permute-start | bytes 4718600 | tf_op jit(solution)/shard_map/ppermute | solution.py:277
  85.0 41.0 %collective-permute-start.14 = (bf16[3072,256]{1,0:T(8,128)(2,1)S(1)}, bf16[3072,256]{1,0:T(8,128)(2,1)S(1)}, u32[]{:S(2)}, u32[]{:S(2)}) collective-permute-start(bf16[3072,256]{1,0:T(8,128)(2,1)S(1)} %terms.8.refs_5_.refs_0_.refs_2_), channel_id=1, source_target_pairs={{0,1},{1,0},{2,3},{3,2},{4,5},{5,4},{6,7},{7,6},{8,9},{9,8},{10,11... | collective-permute-start | bytes 4718600 | tf_op jit(solution)/shard_map/ppermute | solution.py:277
  99.6 21.6 %collective-permute-start.12 = (bf16[3072,128]{1,0:T(8,128)(2,1)S(1)}, bf16[3072,128]{1,0:T(8,128)(2,1)S(1)}, u32[]{:S(2)}, u32[]{:S(2)}) collective-permute-start(bf16[3072,128]{1,0:T(8,128)(2,1)S(1)} %get-tuple-element.61), channel_id=1, source_target_pairs={{0,2},{2,0},{4,6},{6,4},{1,3},{3,1},{5,7},{7,5},{8,10},{10,8},{12,... | collective-permute-start | bytes 2359304 | tf_op jit(solution)/shard_map/ppermute | solution.py:274
  118.1 13.2 %collective-permute-start.20 = (bf16[256,3072]{1,0:T(8,128)(2,1)S(1)}, bf16[256,3072]{1,0:T(8,128)(2,1)S(1)}, u32[]{:S(2)}, u32[]{:S(2)}) collective-permute-start(bf16[256,3072]{1,0:T(8,128)(2,1)S(1)} %collective-permute-done.17.refs_7_.refs_0_.refs_2_.refs_14_), channel_id=1, source_target_pairs={{0,2},{2,0},{4,6},{6,4},{1,3},{3,1},{5,7},{7,5},{8,10},{10,8},{12,... | collective-permute-start | bytes 4718600 | tf_op jit(solution)/shard_map/ppermute | solution.py:274
  118.1 41.6 %collective-permute-start.19 = (bf16[3072,256]{1,0:T(8,128)(2,1)S(1)}, bf16[3072,256]{1,0:T(8,128)(2,1)S(1)}, u32[]{:S(2)}, u32[]{:S(2)}) collective-permute-start(bf16[3072,256]{1,0:T(8,128)(2,1)S(1)} %terms.9.refs_5_.refs_0_.refs_2_), channel_id=1, source_target_pairs={{0,1},{1,0},{2,3},{3,2},{4,5},{5,4},{6,7},{7,6},{8,9},{9,8},{10,11... | collective-permute-start | bytes 4718600 | tf_op jit(solution)/shard_map/ppermute | solution.py:277
  119.6 36.5 %collective-permute-start.21 = (bf16[256,3072]{1,0:T(8,128)(2,1)S(1)}, bf16[256,3072]{1,0:T(8,128)(2,1)S(1)}, u32[]{:S(2)}, u32[]{:S(2)}) collective-permute-start(bf16[256,3072]{1,0:T(8,128)(2,1)S(1)} %collective-permute-done.16.refs_6_.refs_0_.refs_2_.refs_4_.refs_11_), channel_id=1, source_target_pairs={{0,4},{2,6},{4,0},{6,2},{1,5},{3,7},{5,1},{7,3},{8,12},{10,14},{12... | collective-permute-start | bytes 4718600 | tf_op jit(solution)/shard_map/ppermute | solution.py:274
  130.7 6.8 %collective-permute-start.18 = (bf16[3072,128]{1,0:T(8,128)(2,1)S(1)}, bf16[3072,128]{1,0:T(8,128)(2,1)S(1)}, u32[]{:S(2)}, u32[]{:S(2)}) collective-permute-start(bf16[3072,128]{1,0:T(8,128)(2,1)S(1)} %get-tuple-element.66), channel_id=1, source_target_pairs={{0,2},{2,0},{4,6},{6,4},{1,3},{3,1},{5,7},{7,5},{8,10},{10,8},{12,... | collective-permute-start | bytes 2359304 | tf_op jit(solution)/shard_map/ppermute | solution.py:274
  130.8 35.7 %collective-permute-start.25 = (bf16[256,3072]{1,0:T(8,128)(2,1)S(1)}, bf16[256,3072]{1,0:T(8,128)(2,1)S(1)}, u32[]{:S(2)}, u32[]{:S(2)}) collective-permute-start(bf16[256,3072]{1,0:T(8,128)(2,1)S(1)} %collective-permute-done.10.refs_6_.refs_0_.refs_2_.refs_16_), channel_id=1, source_target_pairs={{0,2},{2,0},{4,6},{6,4},{1,3},{3,1},{5,7},{7,5},{8,10},{10,8},{12,... | collective-permute-start | bytes 4718600 | tf_op jit(solution)/shard_map/ppermute | solution.py:274
  137.0 54.4 %collective-permute-start.28 = (bf16[3072,256]{1,0:T(8,128)(2,1)S(1)}, bf16[3072,256]{1,0:T(8,128)(2,1)S(1)}, u32[]{:S(2)}, u32[]{:S(2)}) collective-permute-start(bf16[3072,256]{1,0:T(8,128)(2,1)S(1)} %terms.10.refs_5_.refs_0_.refs_2_), channel_id=1, source_target_pairs={{0,1},{1,0},{2,3},{3,2},{4,5},{5,4},{6,7},{7,6},{8,9},{9,8},{10,11... | collective-permute-start | bytes 4718600 | tf_op jit(solution)/shard_map/ppermute | solution.py:277
  164.4 7.8 %collective-permute-start.22 = (bf16[3072,128]{1,0:T(8,128)(2,1)S(1)}, bf16[3072,128]{1,0:T(8,128)(2,1)S(1)}, u32[]{:S(2)}, u32[]{:S(2)}) collective-permute-start(bf16[3072,128]{1,0:T(8,128)(2,1)S(1)} %get-tuple-element.71), channel_id=1, source_target_pairs={{0,2},{2,0},{4,6},{6,4},{1,3},{3,1},{5,7},{7,5},{8,10},{10,8},{12,... | collective-permute-start | bytes 2359304 | tf_op jit(solution)/shard_map/ppermute | solution.py:274
  164.5 35.4 %collective-permute-start.27 = (bf16[256,3072]{1,0:T(8,128)(2,1)S(1)}, bf16[256,3072]{1,0:T(8,128)(2,1)S(1)}, u32[]{:S(2)}, u32[]{:S(2)}) collective-permute-start(bf16[256,3072]{1,0:T(8,128)(2,1)S(1)} %collective-permute-done.21.refs_6_.refs_0_.refs_2_.refs_9_), channel_id=1, source_target_pairs={{0,2},{2,0},{4,6},{6,4},{1,3},{3,1},{5,7},{7,5},{8,10},{10,8},{12,... | collective-permute-start | bytes 4718600 | tf_op jit(solution)/shard_map/ppermute | solution.py:274
  165.0 19.5 %collective-permute-start.13 = (bf16[3072,128]{1,0:T(8,128)(2,1)S(1)}, bf16[3072,128]{1,0:T(8,128)(2,1)S(1)}, u32[]{:S(2)}, u32[]{:S(2)}) collective-permute-start(bf16[3072,128]{1,0:T(8,128)(2,1)S(1)} %copy-done.31), channel_id=1, source_target_pairs={{0,4},{2,6},{4,0},{6,2},{1,5},{3,7},{5,1},{7,3},{8,12},{10,14},{12... | collective-permute-start | bytes 2359304 | tf_op jit(solution)/shard_map/ppermute | solution.py:274
  197.1 10.0 %collective-permute-start.29 = (bf16[3072,128]{1,0:T(8,128)(2,1)S(1)}, bf16[3072,128]{1,0:T(8,128)(2,1)S(1)}, u32[]{:S(2)}, u32[]{:S(2)}) collective-permute-start(bf16[3072,128]{1,0:T(8,128)(2,1)S(1)} %get-tuple-element.77), channel_id=1, source_target_pairs={{0,2},{2,0},{4,6},{6,4},{1,3},{3,1},{5,7},{7,5},{8,10},{10,8},{12,... | collective-permute-start | bytes 2359304 | tf_op jit(solution)/shard_map/ppermute | solution.py:274
  197.1 37.2 %collective-permute-start.26 = (bf16[3072,256]{1,0:T(8,128)(2,1)S(1)}, bf16[3072,256]{1,0:T(8,128)(2,1)S(1)}, u32[]{:S(2)}, u32[]{:S(2)}) collective-permute-start(bf16[3072,256]{1,0:T(8,128)(2,1)S(1)} %terms.11.refs_5_.refs_0_.refs_2_), channel_id=1, source_target_pairs={{0,1},{1,0},{2,3},{3,2},{4,5},{5,4},{6,7},{7,6},{8,9},{9,8},{10,11... | collective-permute-start | bytes 4718600 | tf_op jit(solution)/shard_map/ppermute | solution.py:277
  198.4 35.9 %collective-permute-start.23 = (bf16[3072,128]{1,0:T(8,128)(2,1)S(1)}, bf16[3072,128]{1,0:T(8,128)(2,1)S(1)}, u32[]{:S(2)}, u32[]{:S(2)}) collective-permute-start(bf16[3072,128]{1,0:T(8,128)(2,1)S(1)} %add_convert_fusion.8.refs_7_), channel_id=1, source_target_pairs={{0,4},{2,6},{4,0},{6,2},{1,5},{3,7},{5,1},{7,3},{8,12},{10,14},{12... | collective-permute-start | bytes 2359304 | tf_op jit(solution)/shard_map/ppermute | solution.py:274
  206.4 44.4 %collective-permute-start.31 = (bf16[1536,256]{1,0:T(8,128)(2,1)S(1)}, bf16[1536,256]{1,0:T(8,128)(2,1)S(1)}, u32[]{:S(2)}, u32[]{:S(2)}) collective-permute-start(bf16[1536,256]{1,0:T(8,128)(2,1)S(1)} %get-tuple-element.75.refs_5_.refs_0_), channel_id=1, source_target_pairs={{0,1},{1,0},{2,3},{3,2},{4,5},{5,4},{6,7},{7,6},{8,9},{9,8},{10,11... | collective-permute-start | bytes 2359304 | tf_op jit(solution)/shard_map/ppermute | solution.py:277
  207.3 43.4 %collective-permute-start.30 = (bf16[3072,128]{1,0:T(8,128)(2,1)S(1)}, bf16[3072,128]{1,0:T(8,128)(2,1)S(1)}, u32[]{:S(2)}, u32[]{:S(2)}) collective-permute-start(bf16[3072,128]{1,0:T(8,128)(2,1)S(1)} %add_convert_fusion.6.refs_7_), channel_id=1, source_target_pairs={{0,4},{2,6},{4,0},{6,2},{1,5},{3,7},{5,1},{7,3},{8,12},{10,14},{12... | collective-permute-start | bytes 2359304 | tf_op jit(solution)/shard_map/ppermute | solution.py:274
  255.5 4.5 %collective-permute-start.32 = (bf16[3072,128]{1,0:T(8,128)(2,1)S(1)}, bf16[3072,128]{1,0:T(8,128)(2,1)S(1)}, u32[]{:S(2)}, u32[]{:S(2)}) collective-permute-start(bf16[3072,128]{1,0:T(8,128)(2,1)S(1)} %get-tuple-element.79), channel_id=1, source_target_pairs={{0,2},{2,0},{4,6},{6,4},{1,3},{3,1},{5,7},{7,5},{8,10},{10,8},{12,... | collective-permute-start | bytes 2359304 | tf_op jit(solution)/shard_map/ppermute | solution.py:274
  255.6 9.0 %collective-permute-start.34 = (bf16[256,3072]{1,0:T(8,128)(2,1)S(1)}, bf16[256,3072]{1,0:T(8,128)(2,1)S(1)}, u32[]{:S(2)}, u32[]{:S(2)}) collective-permute-start(bf16[256,3072]{1,0:T(8,128)(2,1)S(1)} %collective-permute-done.16.refs_6_.refs_0_.refs_2_.refs_4_.refs_11_), channel_id=1, source_target_pairs={{0,2},{2,0},{4,6},{6,4},{1,3},{3,1},{5,7},{7,5},{8,10},{10,8},{12,... | collective-permute-start | bytes 4718600 | tf_op jit(solution)/shard_map/ppermute | solution.py:274
  256.1 70.1 %collective-permute-start.36 = (bf16[1536,256]{1,0:T(8,128)(2,1)}, bf16[1536,256]{1,0:T(8,128)(2,1)}, u32[]{:S(2)}, u32[]{:S(2)}) collective-permute-start(bf16[1536,256]{1,0:T(8,128)(2,1)} %get-tuple-element.81.refs_2_), channel_id=1, source_target_pairs={{0,1},{1,0},{2,3},{3,2},{4,5},{5,4},{6,7},{7,6},{8,9},{9,8},{10,11... | collective-permute-start | bytes 2359304 | tf_op jit(solution)/shard_map/ppermute | solution.py:277
  258.5 67.7 %collective-permute-start.24 = (bf16[3072,128]{1,0:T(8,128)(2,1)}, bf16[3072,128]{1,0:T(8,128)(2,1)}, u32[]{:S(2)}, u32[]{:S(2)}) collective-permute-start(bf16[3072,128]{1,0:T(8,128)(2,1)} %add_convert_fusion.7), channel_id=1, source_target_pairs={{0,8},{8,16},{16,24},{24,0},{1,9},{9,17},{17,25},{25,1},{2,10},{10... | collective-permute-start | bytes 2359304 | tf_op jit(solution)/shard_map/ppermute | solution.py:277
  261.5 64.6 %collective-permute-start.33 = (bf16[3072,128]{1,0:T(8,128)(2,1)}, bf16[3072,128]{1,0:T(8,128)(2,1)}, u32[]{:S(2)}, u32[]{:S(2)}) collective-permute-start(bf16[3072,128]{1,0:T(8,128)(2,1)} %get-tuple-element.108), channel_id=1, source_target_pairs={{0,16},{8,24},{16,0},{24,8},{1,17},{9,25},{17,1},{25,9},{2,18},{10... | collective-permute-start | bytes 2359304 | tf_op jit(solution)/shard_map/ppermute | solution.py:277
  270.4 73.7 %collective-permute-start.35 = (bf16[3072,256]{1,0:T(8,128)(2,1)S(1)}, bf16[3072,256]{1,0:T(8,128)(2,1)S(1)}, u32[]{:S(2)}, u32[]{:S(2)}) collective-permute-start(bf16[3072,256]{1,0:T(8,128)(2,1)S(1)} %terms.13.refs_18_.refs_0_.refs_2_), channel_id=1, source_target_pairs={{0,1},{1,0},{2,3},{3,2},{4,5},{5,4},{6,7},{7,6},{8,9},{9,8},{10,11... | collective-permute-start | bytes 4718600 | tf_op jit(solution)/shard_map/ppermute | solution.py:277
  340.9 2.3 collective-permute-start.38
  343.4 39.0 %collective-permute-start.39 = (bf16[3072,128]{1,0:T(8,128)(2,1)S(1)}, bf16[3072,128]{1,0:T(8,128)(2,1)S(1)}, u32[]{:S(2)}, u32[]{:S(2)}) collective-permute-start(bf16[3072,128]{1,0:T(8,128)(2,1)S(1)} %add_convert_fusion.2.refs_15_), channel_id=1, source_target_pairs={{0,4},{2,6},{4,0},{6,2},{1,5},{3,7},{5,1},{7,3},{8,12},{10,14},{12... | collective-permute-start | bytes 2359304 | tf_op jit(solution)/shard_map/ppermute | solution.py:274
  354.3 28.2 %collective-permute-start.37 = (bf16[3072,128]{1,0:T(8,128)(2,1)S(1)}, bf16[3072,128]{1,0:T(8,128)(2,1)S(1)}, u32[]{:S(2)}, u32[]{:S(2)}) collective-permute-start(bf16[3072,128]{1,0:T(8,128)(2,1)S(1)} %get-tuple-element.90), channel_id=1, source_target_pairs={{0,2},{2,0},{4,6},{6,4},{1,3},{3,1},{5,7},{7,5},{8,10},{10,8},{12,... | collective-permute-start | bytes 2359304 | tf_op jit(solution)/shard_map/ppermute | solution.py:274
  382.8 49.5 %collective-permute-start.40 = (bf16[3072,128]{1,0:T(8,128)(2,1)S(1)}, bf16[3072,128]{1,0:T(8,128)(2,1)S(1)}, u32[]{:S(2)}, u32[]{:S(2)}) collective-permute-start(bf16[3072,128]{1,0:T(8,128)(2,1)S(1)} %add_convert_fusion.1), channel_id=1, source_target_pairs={{0,24},{8,0},{16,8},{24,16},{1,25},{9,1},{17,9},{25,17},{2,26},{10... | collective-permute-start | bytes 2359304 | tf_op jit(solution)/shard_map/ppermute | solution.py:277
  384.5 18.2 %collective-permute-start.41 = (f32[8,128]{1,0:T(8,128)S(1)}, f32[8,128]{1,0:T(8,128)S(1)}, u32[]{:S(2)}, u32[]{:S(2)}) collective-permute-start(f32[8,128]{1,0:T(8,128)S(1)} %broadcast_in_dim.3), channel_id=1, source_target_pairs={{0,8},{8,16},{16,24},{24,0},{1,9},{9,17},{17,25},{25,1},{2,10},{10... | collective-permute-start | bytes 12296 | tf_op jit(solution)/shard_map/ppermute | solution.py:277
  386.2 16.6 %collective-permute-start.42 = (f32[8,128]{1,0:T(8,128)S(1)}, f32[8,128]{1,0:T(8,128)S(1)}, u32[]{:S(2)}, u32[]{:S(2)}) collective-permute-start(f32[8,128]{1,0:T(8,128)S(1)} %broadcast_in_dim.3), channel_id=1, source_target_pairs={{0,16},{8,24},{16,0},{24,8},{1,17},{9,25},{17,1},{25,9},{2,18},{10... | collective-permute-start | bytes 12296 | tf_op jit(solution)/shard_map/ppermute | solution.py:277
  388.3 14.8 %collective-permute-start.43 = (f32[8,128]{1,0:T(8,128)S(1)}, f32[8,128]{1,0:T(8,128)S(1)}, u32[]{:S(2)}, u32[]{:S(2)}) collective-permute-start(f32[8,128]{1,0:T(8,128)S(1)} %broadcast_in_dim.3), channel_id=1, source_target_pairs={{0,24},{8,0},{16,8},{24,16},{1,25},{9,1},{17,9},{25,17},{2,26},{10... | collective-permute-start | bytes 12296 | tf_op jit(solution)/shard_map/ppermute | solution.py:277
  403.8 1.9 collective-permute-start.44
  403.9 3.7 collective-permute-start.45
  405.4 3.0 collective-permute-start.46
  408.4 3.6 collective-permute-start.47
  (56 other events, 745.4 us)

commit v3 on v2

--- a/solution.py
+++ b/solution.py
@@ -7,9 +7,9 @@
 
 GELU_C = 0.7978845608
 MIB = 1 << 20
+WIDE = 56
 ANY = pl.BlockSpec(memory_space=pl.ANY)
 HELD = pl.BlockSpec(memory_space=pltpu.VMEM)
-WIDE = 56
 
 
 def gelu_parts(values):
@@ -65,7 +65,7 @@
     )(weight, *after)
 
 
-def terms_call(blocks, w_in, w_out, after, split):
+def terms_call(blocks, w_in, w_out, after):
     hidden, depth = w_out.shape
     rows = blocks[0].shape[0] // 2
     count = len(blocks)
@@ -75,28 +75,19 @@
     def kernel(*refs):
         x_refs, dy_refs = refs[:count], refs[count : 2 * count]
         w_in_ref, w_out_ref = refs[2 * count : 2 * count + 2]
-        h_ref, d_ref = (refs[-2], refs[-1]) if split else (refs[-1], refs[-1])
+        out_ref = refs[-1]
         step = pl.program_id(0)
 
         @pl.when(step < steps)
         def _():
             at = pl.ds(pl.multiple_of(step * tile, tile), tile)
-            h_ref[...] = contract(w_in_ref[at, :], stacked(x_refs), 1, 1).astype(jnp.bfloat16)
+            out_ref[...] = contract(w_in_ref[at, :], stacked(x_refs), 1, 1).astype(jnp.bfloat16)
 
         @pl.when(step >= steps)
         def _():
             at = pl.ds(pl.multiple_of((step - steps) * tile, tile), tile)
-            d_ref[...] = contract(w_out_ref[at, :], stacked(dy_refs), 1, 1).astype(jnp.bfloat16)
-
-    cols = count * rows
-    out_specs = pl.BlockSpec((tile, cols), lambda i: (i, 0))
-    out_shape = jax.ShapeDtypeStruct((2 * hidden, cols), jnp.bfloat16)
-    if split:
-        out_specs = [
-            pl.BlockSpec((tile, cols), lambda i: (jnp.minimum(i, steps - 1), 0)),
-            pl.BlockSpec((tile, cols), lambda i: (jnp.maximum(i - steps, 0), 0)),
-        ]
-        out_shape = [jax.ShapeDtypeStruct((hidden, cols), jnp.bfloat16)] * 2
+            out_ref[...] = contract(w_out_ref[at, :], stacked(dy_refs), 1, 1).astype(jnp.bfloat16)
+
     return pl.pallas_call(
         kernel,
         grid=(2 * steps,),
@@ -104,8 +95,8 @@
         + [once((rows, depth), 1)] * count
         + [HELD, HELD]
         + [ANY] * len(after),
-        out_specs=out_specs,
-        out_shape=out_shape,
+        out_specs=pl.BlockSpec((tile, count * rows), lambda i: (i, 0)),
+        out_shape=jax.ShapeDtypeStruct((2 * hidden, count * rows), jnp.bfloat16),
         compiler_params=params(6),
         name="terms",
     )(*blocks, *blocks, w_in, w_out, *after)
@@ -192,79 +183,73 @@
 def grad_call(jobs, after, square):
     rows = jobs[0][0][0].shape[0]
     part, cols = jobs[0][1][0].shape[0] // 2, jobs[0][1][0].shape[1]
-    tile = tile_of(cols, 256)
+    tile = tile_of(cols, 512)
     operands, specs, places = [], [], []
     tile_spec = pl.BlockSpec((rows, tile), lambda i: (0, i))
+    out_specs, out_shape = [], []
     for lefts, rights, right_at, base in jobs:
         begin = len(operands)
         operands += [*lefts, *rights, *([] if base is None else [base])]
-        specs += [pl.BlockSpec((rows, lefts[0].shape[1]), lambda i: (0, 0))] * len(lefts)
+        specs += [once((rows, lefts[0].shape[1]), 0)] * len(lefts)
         specs += [pl.BlockSpec((part, tile), lambda i, at=right_at: (at, i))] * len(rights)
         specs += [] if base is None else [tile_spec]
         middle = begin + len(lefts)
         places.append((begin, middle, middle + len(rights), base is not None))
-    shape = jax.ShapeDtypeStruct((rows, cols), jnp.bfloat16)
+        out_specs.append(tile_spec)
+        out_shape.append(jax.ShapeDtypeStruct((rows, cols), jnp.bfloat16))
+    out_specs.append(pl.BlockSpec((8, tile), lambda i: (0, 0)))
+    out_shape.append(jax.ShapeDtypeStruct((8, tile), jnp.float32))
 
     def kernel(*refs):
         outs = refs[len(operands) + len(after) :]
-        if square:
+
+        @pl.when(pl.program_id(0) == 0)
+        def _():
             outs[-1][...] = jnp.zeros_like(outs[-1])
 
-        def body(*blocks):
-            for (begin, middle, end, based), out_ref in zip(places, blocks[len(operands) :]):
-                left = jnp.concatenate([ref[...] for ref in blocks[begin:middle]], axis=1)
-                total = contract(left, stacked(blocks[middle:end]), 1, 0)
-                if based:
-                    total = total + blocks[end][...].astype(jnp.float32)
-                out_ref[...] = total.astype(jnp.bfloat16)
-                if square:
-                    outs[-1][...] += jnp.sum((total * total).reshape(rows // 8, 8, tile), axis=0)
-
-        pltpu.emit_pipeline(
-            body, grid=(cols // tile,), in_specs=specs, out_specs=[tile_spec] * len(jobs)
-        )(*refs[: len(operands)], *outs[: len(jobs)])
-
-    return pl.pallas_call(
-        kernel,
-        in_specs=[ANY] * (len(operands) + len(after)),
-        out_specs=[ANY] * len(jobs) + [HELD] * square,
-        out_shape=[shape] * len(jobs) + [jax.ShapeDtypeStruct((8, tile), jnp.float32)] * square,
+        for (begin, middle, end, based), out_ref in zip(places, outs):
+            left = jnp.concatenate([ref[...] for ref in refs[begin:middle]], axis=1)
+            total = contract(left, stacked(refs[middle:end]), 1, 0)
+            if based:
+                total = total + refs[end][...].astype(jnp.float32)
+            out_ref[...] = total.astype(jnp.bfloat16)
+            if square:
+                outs[-1][...] += jnp.sum((total * total).reshape(rows // 8, 8, tile), axis=0)
+
+    return pl.pallas_call(
+        kernel,
+        grid=(cols // tile,),
+        in_specs=specs + [ANY] * len(after),
+        out_specs=out_specs,
+        out_shape=out_shape,
         compiler_params=params(WIDE),
         name="grad",
     )(*operands, *after)
 
 
-def scale_call(factor, flipped, plain, after):
-    rows, cols = plain.shape
-    steps = cols // tile_of(cols, 256)
-    wide, high = cols // steps, rows // steps
-
-    def kernel(factor_ref, *refs):
-        def body(flipped_ref, plain_ref, grad_in_ref, grad_out_ref):
-            value = flipped_ref[...].astype(jnp.float32) * factor_ref[0, 0]
-            grad_in_ref[...] = value.astype(jnp.bfloat16).T
-            value = plain_ref[...].astype(jnp.float32) * factor_ref[0, 0]
-            grad_out_ref[...] = value.astype(jnp.bfloat16)
-
-        high_spec = pl.BlockSpec((high, cols), lambda i: (i, 0))
-        pltpu.emit_pipeline(
-            body,
-            grid=(steps,),
-            in_specs=[pl.BlockSpec((rows, wide), lambda i: (0, i)), high_spec],
-            out_specs=[pl.BlockSpec((wide, rows), lambda i: (i, 0)), high_spec],
-        )(refs[0], refs[1], refs[-2], refs[-1])
-
-    return pl.pallas_call(
-        kernel,
-        in_specs=[pl.BlockSpec(memory_space=pltpu.SMEM)] + [ANY] * (2 + len(after)),
-        out_specs=[ANY, ANY],
-        out_shape=[
-            jax.ShapeDtypeStruct((cols, rows), jnp.bfloat16),
-            jax.ShapeDtypeStruct((rows, cols), jnp.bfloat16),
-        ],
-        compiler_params=params(WIDE),
+def scale_call(factor, grad, flip, after=()):
+    rows, cols = grad.shape
+    tile = tile_of(cols if flip else rows, 256)
+
+    def kernel(factor_ref, in_ref, *refs):
+        value = (in_ref[...].astype(jnp.float32) * factor_ref[0, 0]).astype(jnp.bfloat16)
+        refs[-1][...] = value.T if flip else value
+
+    return pl.pallas_call(
+        kernel,
+        grid=((cols if flip else rows) // tile,),
+        in_specs=[
+            pl.BlockSpec(memory_space=pltpu.SMEM),
+            pl.BlockSpec((rows, tile), lambda i: (0, i))
+            if flip
+            else pl.BlockSpec((tile, cols), lambda i: (i, 0)),
+        ]
+        + [ANY] * len(after),
+        out_specs=pl.BlockSpec((tile, rows if flip else cols), lambda i: (i, 0)),
+        out_shape=jax.ShapeDtypeStruct((cols, rows) if flip else (rows, cols), jnp.bfloat16),
+        compiler_params=params(40),
         name="scale",
-    )(factor.reshape(1, 1), flipped, plain, *after)
+    )(factor.reshape(1, 1), grad, *after)
 
 
 def solution(mesh):
@@ -295,8 +280,8 @@
     groups = [[(mask, step), (mask + 1, step)] for mask, step in leads]
     count = len(groups)
     last = count - 1
-    own_tie = {last - 2: "A in", last - 1: "C", last: "norm"}
-    far_tie = {last - 3: ("gelu", last - 2), last - 1: "norm"}
+    own_tie = {last - 3: "A in", last - 2: "A out", last - 1: "C in", last: "C out"}
+    far_tie = {last - 3: ("terms", last), last - 1: "norm"}
 
     def shards(tokens, w_in, w_out, out_grad):
         hidden = w_in.shape[1]
@@ -327,14 +312,9 @@
         def run_terms(g):
             nonlocal done
             blocks_of = [blocks[b] for b in groups[g]]
-            value = terms_call(blocks_of, w_in_t, w_out, waits(("terms", g)), g == last - 1)
-            if g == last - 1:
-                done = (value[0],)
-                terms[g] = width_terms(value[0]), width_terms(value[1])
-                tie(("gelu", last - 2), terms[g][0][-1])
-            else:
-                done = (value,)
-                terms[g] = (width_terms(value),) * 2
+            value = terms_call(blocks_of, w_in_t, w_out, waits(("terms", g)))
+            done = (value,)
+            terms[g] = (width_terms(value),) * 2
 
         def plus(one, two):
             return (one.astype(jnp.float32) + two.astype(jnp.float32)).astype(jnp.bfloat16)
@@ -349,13 +329,15 @@
             if g < last and all((p, step) in sums for p in pairs):
                 finish(step)
                 if step:
-                    tie(("gelu", min(g + 3, last - 1)), returned[-1])
+                    tie("C in" if g + 3 == last - 1 else ("gelu", g + 3) if g + 3 < last else "norm", returned[-1][0])
 
         def finish(step):
             total = sums[0, step]
             for p in pairs[1:]:
                 total = plus(total, later(sums[p, step]) if step == n_gx - 1 else sums[p, step])
-            returned.append(shift(total, "gx", n_gx, step) if step else total)
+            half = total.shape[0] // 2 if step == n_gx - 2 else total.shape[0]
+            parts = [total[at : at + half] for at in range(0, total.shape[0], half)]
+            returned.append([shift(v, "gx", n_gx, step) if step else v for v in parts])
 
         def run_gelu(g):
             nonlocal done
@@ -373,7 +355,7 @@
                     rights = [blocks[b] for g in range(begin, end) for b in groups[g]]
                     jobs.append((lefts, rights, which, bases[which]))
             outs = grad_call(jobs, waits(stage), square)
-            done = (outs[0],)
+            done = (outs[-1],)
             return outs
 
         fetch((1, 0))
@@ -384,7 +366,7 @@
         h_own = half_call(first, 0, w_in, 0, done)
         d_own = half_call(first, 1, w_out, 1, (h_own,))
         h_terms = width_terms(h_own)
-        most = 3 * hidden // 4
+        most = hidden // 2
         d_parts = [width_terms(d_own[:most]), width_terms(d_own[most:])]
         w_in_t = flip_call(w_in, (d_own,))
         done = (w_in_t,)
@@ -416,24 +398,25 @@
                 others = [[later(v) for v in part[-max(1, len(part) * (n_gz > 2)) :]] for part in d_parts]
                 d_terms = [jnp.concatenate(both, axis=0) for both in zip(*others)]
                 terms[0] = h_terms, d_terms if n_gz > 2 else [d_own] + d_terms
-            if g < last:
-                run_gelu(g - 1)
-            else:
-                (gin,) = run_grads("A in", 0, None, last - 1, none)
-                (gout,) = run_grads("A out", None, 0, last - 1, none)
-                run_gelu(g - 1)
+            if g == last - 1:
+                gin, _ = run_grads("A in", 0, None, last - 2, none)
+            run_gelu(g - 1)
+        gout, _ = run_grads("A out", None, 0, last, none)
         run_gelu(last)
-        gin, gout, squares = run_grads("C", last - 1, last - 1, count, (gin, gout), True)
-
+        gin, gin_squares = run_grads("C in", last - 2, None, count, (gin, gout), True)
         finish(n_gx - 1)
-        square = jnp.broadcast_to(jnp.sum(squares), (8, 128))
-        square = lax.optimization_barrier((over_gx(square), waits("norm")))[0]
+        gout, gout_squares = run_grads("C out", None, last, count, (gin, gout), True)
+
+        square = jnp.broadcast_to(jnp.sum(gin_squares) + jnp.sum(gout_squares), (8, 128))
+        square = over_gx(lax.optimization_barrier((square, waits("norm")))[0])
         square = over_gy_gz(square)[0, 0]
-        in_grad = sum(piece.astype(jnp.float32) for piece in returned).astype(jnp.bfloat16).T
+        pieces = [jnp.concatenate(parts, axis=0) for parts in returned]
+        in_grad = sum(piece.astype(jnp.float32) for piece in pieces).astype(jnp.bfloat16).T
 
         entries = 2.0 * (w_in.shape[0] * n_gz) * (w_in.shape[1] * n_gx * n_gy)
         factor = 1.0 / jnp.sqrt(square / entries + 1e-06)
-        return (in_grad, *scale_call(factor, gin, gout, ()))
+        grad_in = scale_call(factor, gin, True)
+        return in_grad, grad_in, scale_call(factor, gout, False, (grad_in,))
 
     placed = (
         P(("gy", "gx"), "gz"),

time: 439 us -> 386 us (0.88)
  waiting for transfers between devices: 167 us -> 110 us
  Pallas kernels: 191 us -> 179 us
  local copies, waits for them, and re-layouts: 28.5 us -> 38.3 us
  other arithmetic: 7.31 us -> 11.7 us
    ppermute x21, waiting for transfers between devices: 102 us -> 65.8 us  [shift(): lax.ppermute(value, axis, [(i, (i + step) % size) for i in range(size)])]
    pallas_call x4 -> x6, Pallas kernels: 101 us -> 79 us  [the longest x4 66.4 us: grad_call(): pl.pallas_call(kernel, grid=(cols // tile,), in_specs=specs + [ANY] * len...]
    ppermute x27, waiting for transfers between devices: 64.7 us -> 44.4 us  [swap(): return lax.ppermute(value, 'gy', [(i, i ^ mask) for i in range(n_gy)])]
    unnamed x114 -> x138, local copies, waits for them, and re-layouts: 27.2 us -> 36.9 us
    pallas_call x7, Pallas kernels: 40.8 us -> 46.2 us  [terms_call(): pl.pallas_call(kernel, grid=(2 * steps,), in_specs=[once((rows, depth), 0...]
    pallas_call x8, Pallas kernels: 39.5 us -> 44.5 us  [gelu_call(): pl.pallas_call(kernel, grid=(row_steps + steps,), in_specs=[h_spec] * cou...]
    convert_element_type x9, other arithmetic: 4.12 us -> 9.1 us  [plus(): (one.astype(jnp.float32) + two.astype(jnp.float32)).astype(jnp.bfloat16)]
  transfers between devices with their start and end apart: 48 -> 48, of which waited for: 20 -> 21; matrix products, arithmetic and copies ran while one was open for 1% -> 3% of each run, Pallas kernels for 43% -> 47%
where the time goes in v3:
time: 386 us; the launch traced here: 384 us
  Pallas kernels  179 us (46%)
  waiting for transfers between devices  110 us (28%)
  starting transfers between devices  41.5 us (11%)
  local copies, waits for them, and re-layouts  38.3 us (10%)
  other arithmetic  11.7 us (3%)
    pallas_call x4, Pallas kernels, grad_call(): pl.pallas_call(kernel, grid=(cols // tile,), in_specs=specs + [ANY] * len...  66.4 us
    ppermute x21, waiting for transfers between devices, shift(): lax.ppermute(value, axis, [(i, (i + step) % size) for i in range(size)])  65.8 us
    pallas_call x7, Pallas kernels, terms_call(): pl.pallas_call(kernel, grid=(2 * steps,), in_specs=[once((rows, depth), 0...  46.2 us
    pallas_call x8, Pallas kernels, gelu_call(): pl.pallas_call(kernel, grid=(row_steps + steps,), in_specs=[h_spec] * cou...  44.5 us
    ppermute x27, waiting for transfers between devices, swap(): return lax.ppermute(value, 'gy', [(i, i ^ mask) for i in range(n_gy)])  44.4 us
    unnamed x138, local copies, waits for them, and re-layouts  36.9 us
    ppermute x21, starting transfers between devices, shift(): lax.ppermute(value, axis, [(i, (i + step) % size) for i in range(size)])  28.9 us
    ppermute x27, starting transfers between devices, swap(): return lax.ppermute(value, 'gy', [(i, i ^ mask) for i in range(n_gy)])  12.6 us
  transfers between devices with their start and end apart: 48, of which 21 were waited for; matrix products, arithmetic and copies ran while one was open for 3% of the time, Pallas kernels for 47%

profile of v3, /device:TPU:8, one launch (start us, length us, event | category | flops | bytes accessed | tf_op | source)
XLA Modules:
  0.0 384.2 jit_solution(1407886693038844455)
XLA Ops:
  5.5 3.7 copy-done
  9.2 2.9 half_terms.2.refs_3_.refs_0_
  13.8 3.7 copy-done.4
  17.4 2.8 half_terms.3.refs_0_.refs_2_
  20.9 3.6 flip.1.refs_4_.refs_6_
  24.6 14.4 %collective-permute-done.4.refs_7_.refs_0_.refs_2_.refs_9_.refs_11_ = bf16[256,3072]{1,0:T(8,128)(2,1)S(1)} collective-permute-done((bf16[256,3072]{1,0:T(8,128)(2,1)S(1)}, bf16[256,3072]{1,0:T(8,128)(2,1)S(1)}, u32[]{:S(2)}, u32[]{:S(2)}) %collective-permute-start.4) | collective-permute-done | bytes 1572896 | tf_op jit(solution)/shard_map/ppermute | solution.py:262
  42.2 2.6 collective-permute-start.10
  46.4 5.7 %terms.7.refs_5_.refs_0_.refs_2_ = bf16[3072,256]{1,0:T(8,128)(2,1)S(1)} custom-call(bf16[256,3072]{1,0:T(8,128)(2,1)S(1)} %collective-permute-done.3.refs_0_.refs_2_.refs_7_.refs_9_, bf16[256,3072]{1,0:T(8,128)(2,1)S(1)} %collective-permute-done.5.refs_1_.refs_3_.refs_8_.refs_10_, ...), custom_call_target="tpu_custom_call" | custom-call | tf_op jit(solution)/shard_map/terms/pallas_call | solution.py:91
  52.7 3.9 %collective-permute-done.6 = bf16[768,256]{1,0:T(8,128)(2,1)S(1)} collective-permute-done((bf16[768,256]{1,0:T(8,128)(2,1)S(1)}, bf16[768,256]{1,0:T(8,128)(2,1)S(1)}, u32[]{:S(2)}, u32[]{:S(2)}) %collective-permute-start.6) | collective-permute-done | bytes 393248 | tf_op jit(solution)/shard_map/ppermute | solution.py:262
  56.6 4.7 %gelu.8 = (bf16[1536,256]{1,0:T(8,128)(2,1)S(1)}, bf16[1536,256]{1,0:T(8,128)(2,1)S(1)}, bf16[3072,128]{1,0:T(8,128)(2,1)S(1)}, bf16[3072,128]{1,0:T(8,128)(2,1)S(1)}) custom-call(bf16[1536,256]{1,0:T(8,128)(2,1)S(1)} %half_terms.2.refs_3_.refs_0_, bf16[1536,256]{1,0:T(8,128)(2,1)S(1)} %collective-permute-done.1.refs_1_, ...), custom_call_target="tpu_custom_call" | custom-call | tf_op jit(solution)/shard_map/gelu/pallas_call | solution.py:171
  62.3 6.5 %terms.8.refs_5_.refs_0_.refs_2_ = bf16[3072,256]{1,0:T(8,128)(2,1)} custom-call(bf16[256,3072]{1,0:T(8,128)(2,1)S(1)} %collective-permute-done.4.refs_7_.refs_0_.refs_2_.refs_9_.refs_11_, bf16[256,3072]{1,0:T(8,128)(2,1)S(1)} %collective-permute-done.9.refs_1_.refs_3_.refs_10_.refs_12_, ...), custom_call_target="tpu_custom_call" | custom-call | tf_op jit(solution)/shard_map/terms/pallas_call | solution.py:91
  69.6 7.4 %collective-permute-done.11.refs_7_.refs_0_.refs_2_.refs_11_.refs_13_ = bf16[256,3072]{1,0:T(8,128)(2,1)S(1)} collective-permute-done((bf16[256,3072]{1,0:T(8,128)(2,1)S(1)}, bf16[256,3072]{1,0:T(8,128)(2,1)S(1)}, u32[]{:S(2)}, u32[]{:S(2)}) %collective-permute-start.11) | collective-permute-done | bytes 1572896 | tf_op jit(solution)/shard_map/ppermute | solution.py:259
  78.9 2.5 collective-permute-start.16
  83.2 7.1 %collective-permute-done.8.refs_1_.refs_3_ = bf16[3072,256]{1,0:T(8,128)(2,1)S(1)} collective-permute-done((bf16[3072,256]{1,0:T(8,128)(2,1)S(1)}, bf16[3072,256]{1,0:T(8,128)(2,1)S(1)}, u32[]{:S(2)}, u32[]{:S(2)}) %collective-permute-start.8) | collective-permute-done | bytes 1572896 | tf_op jit(solution)/shard_map/ppermute | solution.py:262
  92.9 4.7 %gelu.9 = (bf16[1536,256]{1,0:T(8,128)(2,1)S(1)}, bf16[1536,256]{1,0:T(8,128)(2,1)S(1)}, bf16[3072,128]{1,0:T(8,128)(2,1)S(1)}, bf16[3072,128]{1,0:T(8,128)(2,1)S(1)}) custom-call(bf16[3072,256]{1,0:T(8,128)(2,1)S(1)} %copy-done.17, bf16[3072,256]{1,0:T(8,128)(2,1)S(1)} %copy-done.26, bf16[3072,256]{1,0:T(8,128)(2,1)S(1)} %copy-done.17, ...), custom_call_target="tpu_custom_call" | custom-call | tf_op jit(solution)/shard_map/gelu/pallas_call | solution.py:171
  97.7 5.7 %terms.9.refs_5_.refs_0_.refs_2_ = bf16[3072,256]{1,0:T(8,128)(2,1)S(1)} custom-call(bf16[256,3072]{1,0:T(8,128)(2,1)S(1)} %collective-permute-done.11.refs_7_.refs_0_.refs_2_.refs_11_.refs_13_, bf16[256,3072]{1,0:T(8,128)(2,1)S(1)} %collective-permute-done.15.refs_1_.refs_3_.refs_12_.refs_14_, ...), custom_call_target="tpu_custom_call" | custom-call | tf_op jit(solution)/shard_map/terms/pallas_call | solution.py:91
  103.5 10.5 %collective-permute-done.17.refs_7_.refs_0_.refs_2_.refs_13_.refs_15_ = bf16[256,3072]{1,0:T(8,128)(2,1)} collective-permute-done((bf16[256,3072]{1,0:T(8,128)(2,1)S(1)}, bf16[256,3072]{1,0:T(8,128)(2,1)}, u32[]{:S(2)}, u32[]{:S(2)}) %collective-permute-start.17) | collective-permute-done | bytes 1572896 | tf_op jit(solution)/shard_map/ppermute | solution.py:259
  117.2 6.9 %collective-permute-done.14.refs_1_.refs_3_ = bf16[3072,256]{1,0:T(8,128)(2,1)} collective-permute-done((bf16[3072,256]{1,0:T(8,128)(2,1)}, bf16[3072,256]{1,0:T(8,128)(2,1)}, u32[]{:S(2)}, u32[]{:S(2)}) %collective-permute-start.14) | collective-permute-done | bytes 1572896 | tf_op jit(solution)/shard_map/ppermute | solution.py:262
  124.1 6.9 %gelu.10 = (bf16[1536,256]{1,0:T(8,128)(2,1)S(1)}, bf16[1536,256]{1,0:T(8,128)(2,1)S(1)}, bf16[3072,128]{1,0:T(8,128)(2,1)S(1)}, bf16[3072,128]{1,0:T(8,128)(2,1)S(1)}) custom-call(bf16[3072,256]{1,0:T(8,128)(2,1)} %terms.8.refs_5_.refs_0_.refs_2_, bf16[3072,256]{1,0:T(8,128)(2,1)} %collective-permute-done.14.refs_1_.refs_3_, ...), custom_call_target="tpu_custom_call" | custom-call | tf_op jit(solution)/shard_map/gelu/pallas_call | solution.py:171
  131.6 7.6 %terms.10.refs_5_.refs_0_.refs_2_ = bf16[3072,256]{1,0:T(8,128)(2,1)S(1)} custom-call(bf16[256,3072]{1,0:T(8,128)(2,1)} %collective-permute-done.17.refs_7_.refs_0_.refs_2_.refs_13_.refs_15_, bf16[256,3072]{1,0:T(8,128)(2,1)S(1)} %collective-permute-done.20.refs_1_.refs_3_.refs_14_.refs_16_, ...), custom_call_target="tpu_custom_call" | custom-call | tf_op jit(solution)/shard_map/terms/pallas_call | solution.py:91
  141.3 10.9 %collective-permute-done.21.refs_6_.refs_0_.refs_2_.refs_19_.refs_5_ = bf16[256,3072]{1,0:T(8,128)(2,1)S(1)} collective-permute-done((bf16[256,3072]{1,0:T(8,128)(2,1)}, bf16[256,3072]{1,0:T(8,128)(2,1)S(1)}, u32[]{:S(2)}, u32[]{:S(2)}) %collective-permute-start.21) | collective-permute-done | bytes 1572896 | tf_op jit(solution)/shard_map/ppermute | solution.py:259
  152.2 5.5 %collective-permute-done.19.refs_1_.refs_3_ = bf16[3072,256]{1,0:T(8,128)(2,1)S(1)} collective-permute-done((bf16[3072,256]{1,0:T(8,128)(2,1)S(1)}, bf16[3072,256]{1,0:T(8,128)(2,1)S(1)}, u32[]{:S(2)}, u32[]{:S(2)}) %collective-permute-start.19) | collective-permute-done | bytes 1572896 | tf_op jit(solution)/shard_map/ppermute | solution.py:262
  157.7 4.7 %gelu.11 = (bf16[1536,256]{1,0:T(8,128)(2,1)S(1)}, bf16[1536,256]{1,0:T(8,128)(2,1)S(1)}, bf16[3072,128]{1,0:T(8,128)(2,1)S(1)}, bf16[3072,128]{1,0:T(8,128)(2,1)S(1)}) custom-call(bf16[3072,256]{1,0:T(8,128)(2,1)S(1)} %terms.9.refs_5_.refs_0_.refs_2_, bf16[3072,256]{1,0:T(8,128)(2,1)S(1)} %collective-permute-done.19.refs_1_.refs_3_, ...), custom_call_target="tpu_custom_call" | custom-call | tf_op jit(solution)/shard_map/gelu/pallas_call | solution.py:171
  163.6 6.5 %terms.11.refs_5_.refs_0_.refs_2_ = bf16[3072,256]{1,0:T(8,128)(2,1)} custom-call(bf16[256,3072]{1,0:T(8,128)(2,1)S(1)} %collective-permute-done.10.refs_6_.refs_0_.refs_2_.refs_17_.refs_3_, bf16[256,3072]{1,0:T(8,128)(2,1)S(1)} %collective-permute-done.25.refs_1_.refs_3_.refs_18_.refs_4_, ...), custom_call_target="tpu_custom_call" | custom-call | tf_op jit(solution)/shard_map/terms/pallas_call | solution.py:91
  171.2 11.4 %collective-permute-done.13.refs_6_ = bf16[3072,128]{1,0:T(8,128)(2,1)S(1)} collective-permute-done((bf16[3072,128]{1,0:T(8,128)(2,1)S(1)}, bf16[3072,128]{1,0:T(8,128)(2,1)S(1)}, u32[]{:S(2)}, u32[]{:S(2)}) %collective-permute-start.13) | collective-permute-done | bytes 786464 | tf_op jit(solution)/shard_map/ppermute | solution.py:259
  182.6 7.6 %collective-permute-done.27.refs_1_.refs_3_ = bf16[3072,256]{1,0:T(8,128)(2,1)S(1)} collective-permute-done((bf16[3072,256]{1,0:T(8,128)(2,1)S(1)}, bf16[3072,256]{1,0:T(8,128)(2,1)S(1)}, u32[]{:S(2)}, u32[]{:S(2)}) %collective-permute-start.27) | collective-permute-done | bytes 1572896 | tf_op jit(solution)/shard_map/ppermute | solution.py:262
  190.2 4.7 %gelu.12 = (bf16[1536,256]{1,0:T(8,128)(2,1)S(1)}, bf16[1536,256]{1,0:T(8,128)(2,1)S(1)}, bf16[3072,128]{1,0:T(8,128)(2,1)S(1)}, bf16[3072,128]{1,0:T(8,128)(2,1)S(1)}) custom-call(bf16[3072,256]{1,0:T(8,128)(2,1)S(1)} %terms.10.refs_5_.refs_0_.refs_2_, bf16[3072,256]{1,0:T(8,128)(2,1)S(1)} %collective-permute-done.27.refs_1_.refs_3_, ...), custom_call_target="tpu_custom_call" | custom-call | tf_op jit(solution)/shard_map/gelu/pallas_call | solution.py:171
  196.8 6.5 %terms.12.refs_15_.refs_0_.refs_2_ = bf16[3072,256]{1,0:T(8,128)(2,1)} custom-call(bf16[256,3072]{1,0:T(8,128)(2,1)S(1)} %collective-permute-done.21.refs_6_.refs_0_.refs_2_.refs_19_.refs_5_, bf16[256,3072]{1,0:T(8,128)(2,1)S(1)} %collective-permute-done.28.refs_1_.refs_3_.refs_20_.refs_6_, ...), custom_call_target="tpu_custom_call" | custom-call | tf_op jit(solution)/shard_map/terms/pallas_call | solution.py:91
  207.0 17.8 %grad.4 = (bf16[1536,3072]{1,0:T(8,128)(2,1)}, f32[8,512]{1,0:T(8,128)}) custom-call(bf16[1536,256]{1,0:T(8,128)(2,1)} %copy-done.41, bf16[1536,256]{1,0:T(8,128)(2,1)} %copy-done.42, bf16[1536,256]{1,0:T(8,128)(2,1)} %copy-done.44, bf16[1536,256]{1,0:T(8,128)(2,1)} %copy-done.46, bf16[1536,256]{1,0:T(8,128)(2,1)} %copy-done.47, ...), custom_call_target="tpu_custom_call" | custom-call | tf_op jit(solution)/shard_map/grad/pallas_call | solution.py:219
  224.9 7.7 %collective-permute-done.26.refs_1_.refs_3_ = bf16[3072,256]{1,0:T(8,128)(2,1)} collective-permute-done((bf16[3072,256]{1,0:T(8,128)(2,1)}, bf16[3072,256]{1,0:T(8,128)(2,1)}, u32[]{:S(2)}, u32[]{:S(2)}) %collective-permute-start.26) | collective-permute-done | bytes 1572896 | tf_op jit(solution)/shard_map/ppermute | solution.py:262
  232.6 4.0 %copy-done.1 = bf16[3072,1536]{1,0:T(8,128)(2,1)S(1)} copy-done((bf16[3072,1536]{1,0:T(8,128)(2,1)S(1)}, bf16[3072,1536]{1,0:T(8,128)(2,1)}, u32[]{:S(2)}) %copy-start.1) | copy-done | bytes 9437208
  237.3 7.1 %gelu.13 = (bf16[1536,256]{1,0:T(8,128)(2,1)S(1)}, bf16[1536,256]{1,0:T(8,128)(2,1)S(1)}, bf16[3072,128]{1,0:T(8,128)(2,1)S(1)}, bf16[3072,128]{1,0:T(8,128)(2,1)S(1)}) custom-call(bf16[3072,256]{1,0:T(8,128)(2,1)} %terms.11.refs_5_.refs_0_.refs_2_, bf16[3072,256]{1,0:T(8,128)(2,1)} %collective-permute-done.26.refs_1_.refs_3_, ...), custom_call_target="tpu_custom_call" | custom-call | tf_op jit(solution)/shard_map/gelu/pallas_call | solution.py:171
  246.2 3.8 copy-done.5
  251.3 7.7 %terms.13.refs_5_.refs_0_.refs_2_ = bf16[3072,256]{1,0:T(8,128)(2,1)S(1)} custom-call(bf16[256,3072]{1,0:T(8,128)(2,1)} %collective-permute-done.16.refs_6_.refs_0_.refs_2_.refs_7_.refs_1_, bf16[256,3072]{1,0:T(8,128)(2,1)} %collective-permute-done.34.refs_1_.refs_3_.refs_8_.refs_2_, ...), custom_call_target="tpu_custom_call" | custom-call | tf_op jit(solution)/shard_map/terms/pallas_call | solution.py:91
  261.4 4.9 %collective-permute-done.36.refs_1_.refs_3_ = bf16[3072,256]{1,0:T(8,128)(2,1)} collective-permute-done((bf16[3072,256]{1,0:T(8,128)(2,1)}, bf16[3072,256]{1,0:T(8,128)(2,1)}, u32[]{:S(2)}, u32[]{:S(2)}) %collective-permute-start.36) | collective-permute-done | bytes 1572896 | tf_op jit(solution)/shard_map/ppermute | solution.py:262
  266.3 6.9 %gelu.14 = (bf16[1536,256]{1,0:T(8,128)(2,1)S(1)}, bf16[1536,256]{1,0:T(8,128)(2,1)S(1)}, bf16[3072,128]{1,0:T(8,128)(2,1)S(1)}, bf16[3072,128]{1,0:T(8,128)(2,1)S(1)}) custom-call(bf16[3072,256]{1,0:T(8,128)(2,1)} %terms.12.refs_15_.refs_0_.refs_2_, bf16[3072,256]{1,0:T(8,128)(2,1)} %collective-permute-done.36.refs_1_.refs_3_, ...), custom_call_target="tpu_custom_call" | custom-call | tf_op jit(solution)/shard_map/gelu/pallas_call | solution.py:171
  275.9 22.9 %grad.5 = (bf16[1536,3072]{1,0:T(8,128)(2,1)}, f32[8,512]{1,0:T(8,128)}) custom-call(bf16[1536,256]{1,0:T(8,128)(2,1)} %copy-done.35, bf16[1536,256]{1,0:T(8,128)(2,1)} %copy-done.36, bf16[1536,256]{1,0:T(8,128)(2,1)} %copy-done.37, bf16[1536,256]{1,0:T(8,128)(2,1)} %copy-done.38, bf16[1536,256]{1,0:T(8,128)(2,1)} %copy-done.39, ...), custom_call_target="tpu_custom_call" | custom-call | tf_op jit(solution)/shard_map/grad/pallas_call | solution.py:219
  300.8 3.7 copy-done.2
  304.5 4.7 %gelu.15 = (bf16[1536,256]{1,0:T(8,128)(2,1)S(1)}, bf16[1536,256]{1,0:T(8,128)(2,1)S(1)}, bf16[3072,128]{1,0:T(8,128)(2,1)S(1)}, bf16[3072,128]{1,0:T(8,128)(2,1)S(1)}) custom-call(bf16[3072,256]{1,0:T(8,128)(2,1)S(1)} %terms.13.refs_5_.refs_0_.refs_2_, bf16[3072,256]{1,0:T(8,128)(2,1)S(1)} %collective-permute-done.35.refs_1_.refs_3_, ...), custom_call_target="tpu_custom_call" | custom-call | tf_op jit(solution)/shard_map/gelu/pallas_call | solution.py:171
  311.8 4.4 %collective-permute-start.32 = (bf16[1536,128]{1,0:T(8,128)(2,1)}, bf16[1536,128]{1,0:T(8,128)(2,1)S(1)}, u32[]{:S(2)}, u32[]{:S(2)}) collective-permute-start(bf16[1536,128]{1,0:T(8,128)(2,1)} %get-tuple-element.112), channel_id=1, source_target_pairs={{0,16},{8,24},{16,0},{24,8},{1,17},{9,25},{17,1},{25,9},{2,18},{10... | collective-permute-start | bytes 1179656 | tf_op jit(solution)/shard_map/ppermute | solution.py:262
  317.2 14.7 %grad.6 = (bf16[1536,3072]{1,0:T(8,128)(2,1)}, f32[8,512]{1,0:T(8,128)}) custom-call(bf16[1536,256]{1,0:T(8,128)(2,1)} %copy-done.43, bf16[1536,256]{1,0:T(8,128)(2,1)} %copy-done.45, bf16[1536,256]{1,0:T(8,128)(2,1)} %copy-done.48, bf16[256,3072]{1,0:T(8,128)(2,1)} %copy-done.8, bf16[256,3072]{1,0:T(8,128)(2,1)} %copy-done.14, bf16[256,3072]{1,0:T(8,128)(2,1)} %copy-done.7, ...), custom_call_target="tpu_custom_call" | custom-call | tf_op jit(solution)/shard_map/grad/pallas_call | solution.py:219
  331.9 2.4 add_convert_fusion.1
  335.0 11.0 %grad.7 = (bf16[1536,3072]{1,0:T(8,128)(2,1)}, f32[8,512]{1,0:T(8,128)}) custom-call(bf16[1536,256]{1,0:T(8,128)(2,1)} %copy-done.34, bf16[256,3072]{1,0:T(8,128)(2,1)} %collective-permute-done.16.refs_6_.refs_0_.refs_2_.refs_7_.refs_1_, bf16[256,3072]{1,0:T(8,128)(2,1)} %collective-permute-done.34.refs_1_.refs_3_.refs_8_.refs_2_, ...), custom_call_target="tpu_custom_call" | custom-call | tf_op jit(solution)/shard_map/grad/pallas_call | solution.py:219
  348.6 2.1 collective-permute-start.41
  362.9 2.1 collective-permute-done.47
  366.2 3.7 copy-done.21
  369.9 7.8 %scale.2.refs_0_ = bf16[3072,1536]{1,0:T(8,128)(2,1)} custom-call(f32[1,1]{1,0:T(1,128)S(6)} %sqrt.3.factor_ref, bf16[1536,3072]{1,0:T(8,128)(2,1)S(1)} %copy-done.21), custom_call_target="tpu_custom_call" | custom-call | tf_op jit(solution)/shard_map/scale/pallas_call | solution.py:238
  377.8 4.7 %scale.3 = bf16[1536,3072]{1,0:T(8,128)(2,1)} custom-call(f32[1,1]{1,0:T(1,128)S(6)} %sqrt.3.factor_ref, bf16[1536,3072]{1,0:T(8,128)(2,1)S(1)} %copy-done.22, bf16[3072,1536]{1,0:T(8,128)(2,1)} %scale.2.refs_0_), custom_call_target="tpu_custom_call" | custom-call | tf_op jit(solution)/shard_map/scale/pallas_call | solution.py:238
  (235 shorter events, 65.0 us)
Async XLA Ops:
  2.1 3.5 collective-permute-start
  2.1 36.8 %collective-permute-start.4 = (bf16[256,3072]{1,0:T(8,128)(2,1)S(1)}, bf16[256,3072]{1,0:T(8,128)(2,1)S(1)}, u32[]{:S(2)}, u32[]{:S(2)}) collective-permute-start(bf16[256,3072]{1,0:T(8,128)(2,1)S(1)} %constant_dynamic-update-slice_fusion.refs_0_.refs_5_.refs_7_), channel_id=1, source_target_pairs={{0,24},{8,0},{16,8},{24,16},{1,25},{9,1},{17,9},{25,17},{2,26},{10... | collective-permute-start | bytes 4718600 | tf_op jit(solution)/shard_map/ppermute | solution.py:262
  2.2 36.7 %collective-permute-start.3 = (bf16[256,3072]{1,0:T(8,128)(2,1)S(1)}, bf16[256,3072]{1,0:T(8,128)(2,1)S(1)}, u32[]{:S(2)}, u32[]{:S(2)}) collective-permute-start(bf16[256,3072]{1,0:T(8,128)(2,1)S(1)} %constant_dynamic-update-slice_fusion.refs_0_.refs_5_.refs_7_), channel_id=1, source_target_pairs={{0,4},{2,6},{4,0},{6,2},{1,5},{3,7},{5,1},{7,3},{8,12},{10,14},{12... | collective-permute-start | bytes 4718600 | tf_op jit(solution)/shard_map/ppermute | solution.py:259
  12.2 28.1 %collective-permute-start.1 = (bf16[1536,256]{1,0:T(8,128)(2,1)S(1)}, bf16[1536,256]{1,0:T(8,128)(2,1)S(1)}, u32[]{:S(2)}, u32[]{:S(2)}) collective-permute-start(bf16[1536,256]{1,0:T(8,128)(2,1)S(1)} %half_terms.2.refs_3_.refs_0_), channel_id=1, source_target_pairs={{0,1},{1,0},{2,3},{3,2},{4,5},{5,4},{6,7},{7,6},{8,9},{9,8},{10,11... | collective-permute-start | bytes 2359304 | tf_op jit(solution)/shard_map/ppermute | solution.py:262
  20.4 19.9 %collective-permute-start.2 = (bf16[768,256]{1,0:T(8,128)(2,1)S(1)}, bf16[768,256]{1,0:T(8,128)(2,1)S(1)}, u32[]{:S(2)}, u32[]{:S(2)}) collective-permute-start(bf16[768,256]{1,0:T(8,128)(2,1)S(1)} %get-tuple-element.114), channel_id=1, source_target_pairs={{0,1},{1,0},{2,3},{3,2},{4,5},{5,4},{6,7},{7,6},{8,9},{9,8},{10,11... | collective-permute-start | bytes 1179656 | tf_op jit(solution)/shard_map/ppermute | solution.py:262
  40.2 6.1 %collective-permute-start.5 = (bf16[256,3072]{1,0:T(8,128)(2,1)S(1)}, bf16[256,3072]{1,0:T(8,128)(2,1)S(1)}, u32[]{:S(2)}, u32[]{:S(2)}) collective-permute-start(bf16[256,3072]{1,0:T(8,128)(2,1)S(1)} %collective-permute-done.3.refs_0_.refs_2_.refs_7_.refs_9_), channel_id=1, source_target_pairs={{0,2},{2,0},{4,6},{6,4},{1,3},{3,1},{5,7},{7,5},{8,10},{10,8},{12,... | collective-permute-start | bytes 4718600 | tf_op jit(solution)/shard_map/ppermute | solution.py:259
  40.2 22.0 %collective-permute-start.9 = (bf16[256,3072]{1,0:T(8,128)(2,1)S(1)}, bf16[256,3072]{1,0:T(8,128)(2,1)S(1)}, u32[]{:S(2)}, u32[]{:S(2)}) collective-permute-start(bf16[256,3072]{1,0:T(8,128)(2,1)S(1)} %collective-permute-done.4.refs_7_.refs_0_.refs_2_.refs_9_.refs_11_), channel_id=1, source_target_pairs={{0,2},{2,0},{4,6},{6,4},{1,3},{3,1},{5,7},{7,5},{8,10},{10,8},{12,... | collective-permute-start | bytes 4718600 | tf_op jit(solution)/shard_map/ppermute | solution.py:259
  40.7 36.3 %collective-permute-start.11 = (bf16[256,3072]{1,0:T(8,128)(2,1)S(1)}, bf16[256,3072]{1,0:T(8,128)(2,1)S(1)}, u32[]{:S(2)}, u32[]{:S(2)}) collective-permute-start(bf16[256,3072]{1,0:T(8,128)(2,1)S(1)} %collective-permute-done.4.refs_7_.refs_0_.refs_2_.refs_9_.refs_11_), channel_id=1, source_target_pairs={{0,4},{2,6},{4,0},{6,2},{1,5},{3,7},{5,1},{7,3},{8,12},{10,14},{12... | collective-permute-start | bytes 4718600 | tf_op jit(solution)/shard_map/ppermute | solution.py:259
  42.2 36.2 %collective-permute-start.10 = (bf16[256,3072]{1,0:T(8,128)(2,1)S(1)}, bf16[256,3072]{1,0:T(8,128)(2,1)S(1)}, u32[]{:S(2)}, u32[]{:S(2)}) collective-permute-start(bf16[256,3072]{1,0:T(8,128)(2,1)S(1)} %collective-permute-done.4.refs_7_.refs_0_.refs_2_.refs_9_.refs_11_), channel_id=1, source_target_pairs={{0,24},{8,0},{16,8},{24,16},{1,25},{9,1},{17,9},{25,17},{2,26},{10... | collective-permute-start | bytes 4718600 | tf_op jit(solution)/shard_map/ppermute | solution.py:262
  44.8 11.8 %collective-permute-start.6 = (bf16[768,256]{1,0:T(8,128)(2,1)S(1)}, bf16[768,256]{1,0:T(8,128)(2,1)S(1)}, u32[]{:S(2)}, u32[]{:S(2)}) collective-permute-start(bf16[768,256]{1,0:T(8,128)(2,1)S(1)} %get-tuple-element.115), channel_id=1, source_target_pairs={{0,1},{1,0},{2,3},{3,2},{4,5},{5,4},{6,7},{7,6},{8,9},{9,8},{10,11... | collective-permute-start | bytes 1179656 | tf_op jit(solution)/shard_map/ppermute | solution.py:262
  52.1 38.2 %collective-permute-start.8 = (bf16[3072,256]{1,0:T(8,128)(2,1)S(1)}, bf16[3072,256]{1,0:T(8,128)(2,1)S(1)}, u32[]{:S(2)}, u32[]{:S(2)}) collective-permute-start(bf16[3072,256]{1,0:T(8,128)(2,1)S(1)} %terms.7.refs_5_.refs_0_.refs_2_), channel_id=1, source_target_pairs={{0,1},{1,0},{2,3},{3,2},{4,5},{5,4},{6,7},{7,6},{8,9},{9,8},{10,11... | collective-permute-start | bytes 4718600 | tf_op jit(solution)/shard_map/ppermute | solution.py:262
  62.2 19.2 %collective-permute-start.7 = (bf16[3072,128]{1,0:T(8,128)(2,1)S(1)}, bf16[3072,128]{1,0:T(8,128)(2,1)S(1)}, u32[]{:S(2)}, u32[]{:S(2)}) collective-permute-start(bf16[3072,128]{1,0:T(8,128)(2,1)S(1)} %get-tuple-element.58), channel_id=1, source_target_pairs={{0,2},{2,0},{4,6},{6,4},{1,3},{3,1},{5,7},{7,5},{8,10},{10,8},{12,... | collective-permute-start | bytes 2359304 | tf_op jit(solution)/shard_map/ppermute | solution.py:259
  77.1 20.6 %collective-permute-start.15 = (bf16[256,3072]{1,0:T(8,128)(2,1)S(1)}, bf16[256,3072]{1,0:T(8,128)(2,1)S(1)}, u32[]{:S(2)}, u32[]{:S(2)}) collective-permute-start(bf16[256,3072]{1,0:T(8,128)(2,1)S(1)} %collective-permute-done.11.refs_7_.refs_0_.refs_2_.refs_11_.refs_13_), channel_id=1, source_target_pairs={{0,2},{2,0},{4,6},{6,4},{1,3},{3,1},{5,7},{7,5},{8,10},{10,8},{12,... | collective-permute-start | bytes 4718600 | tf_op jit(solution)/shard_map/ppermute | solution.py:259
  78.4 35.6 %collective-permute-start.17 = (bf16[256,3072]{1,0:T(8,128)(2,1)S(1)}, bf16[256,3072]{1,0:T(8,128)(2,1)}, u32[]{:S(2)}, u32[]{:S(2)}) collective-permute-start(bf16[256,3072]{1,0:T(8,128)(2,1)S(1)} %collective-permute-done.10.refs_6_.refs_0_.refs_2_.refs_17_.refs_3_), channel_id=1, source_target_pairs={{0,4},{2,6},{4,0},{6,2},{1,5},{3,7},{5,1},{7,3},{8,12},{10,14},{12... | collective-permute-start | bytes 4718600 | tf_op jit(solution)/shard_map/ppermute | solution.py:259
  78.9 36.6 %collective-permute-start.16 = (bf16[256,3072]{1,0:T(8,128)(2,1)S(1)}, bf16[256,3072]{1,0:T(8,128)(2,1)}, u32[]{:S(2)}, u32[]{:S(2)}) collective-permute-start(bf16[256,3072]{1,0:T(8,128)(2,1)S(1)} %collective-permute-done.10.refs_6_.refs_0_.refs_2_.refs_17_.refs_3_), channel_id=1, source_target_pairs={{0,24},{8,0},{16,8},{24,16},{1,25},{9,1},{17,9},{25,17},{2,26},{10... | collective-permute-start | bytes 4718600 | tf_op jit(solution)/shard_map/ppermute | solution.py:262
  81.4 42.7 %collective-permute-start.14 = (bf16[3072,256]{1,0:T(8,128)(2,1)}, bf16[3072,256]{1,0:T(8,128)(2,1)}, u32[]{:S(2)}, u32[]{:S(2)}) collective-permute-start(bf16[3072,256]{1,0:T(8,128)(2,1)} %terms.8.refs_5_.refs_0_.refs_2_), channel_id=1, source_target_pairs={{0,1},{1,0},{2,3},{3,2},{4,5},{5,4},{6,7},{7,6},{8,9},{9,8},{10,11... | collective-permute-start | bytes 4718600 | tf_op jit(solution)/shard_map/ppermute | solution.py:262
  97.6 19.4 %collective-permute-start.12 = (bf16[3072,128]{1,0:T(8,128)(2,1)S(1)}, bf16[3072,128]{1,0:T(8,128)(2,1)S(1)}, u32[]{:S(2)}, u32[]{:S(2)}) collective-permute-start(bf16[3072,128]{1,0:T(8,128)(2,1)S(1)} %get-tuple-element.62), channel_id=1, source_target_pairs={{0,2},{2,0},{4,6},{6,4},{1,3},{3,1},{5,7},{7,5},{8,10},{10,8},{12,... | collective-permute-start | bytes 2359304 | tf_op jit(solution)/shard_map/ppermute | solution.py:259
  114.0 17.6 %collective-permute-start.20 = (bf16[256,3072]{1,0:T(8,128)(2,1)}, bf16[256,3072]{1,0:T(8,128)(2,1)S(1)}, u32[]{:S(2)}, u32[]{:S(2)}) collective-permute-start(bf16[256,3072]{1,0:T(8,128)(2,1)} %collective-permute-done.17.refs_7_.refs_0_.refs_2_.refs_13_.refs_15_), channel_id=1, source_target_pairs={{0,2},{2,0},{4,6},{6,4},{1,3},{3,1},{5,7},{7,5},{8,10},{10,8},{12,... | collective-permute-start | bytes 4718600 | tf_op jit(solution)/shard_map/ppermute | solution.py:259
  114.0 43.7 %collective-permute-start.19 = (bf16[3072,256]{1,0:T(8,128)(2,1)S(1)}, bf16[3072,256]{1,0:T(8,128)(2,1)S(1)}, u32[]{:S(2)}, u32[]{:S(2)}) collective-permute-start(bf16[3072,256]{1,0:T(8,128)(2,1)S(1)} %terms.9.refs_5_.refs_0_.refs_2_), channel_id=1, source_target_pairs={{0,1},{1,0},{2,3},{3,2},{4,5},{5,4},{6,7},{7,6},{8,9},{9,8},{10,11... | collective-permute-start | bytes 4718600 | tf_op jit(solution)/shard_map/ppermute | solution.py:262
  115.5 36.7 %collective-permute-start.21 = (bf16[256,3072]{1,0:T(8,128)(2,1)}, bf16[256,3072]{1,0:T(8,128)(2,1)S(1)}, u32[]{:S(2)}, u32[]{:S(2)}) collective-permute-start(bf16[256,3072]{1,0:T(8,128)(2,1)} %collective-permute-done.16.refs_6_.refs_0_.refs_2_.refs_7_.refs_1_), channel_id=1, source_target_pairs={{0,4},{2,6},{4,0},{6,2},{1,5},{3,7},{5,1},{7,3},{8,12},{10,14},{12... | collective-permute-start | bytes 4718600 | tf_op jit(solution)/shard_map/ppermute | solution.py:259
  131.0 10.1 %collective-permute-start.18 = (bf16[3072,128]{1,0:T(8,128)(2,1)S(1)}, bf16[3072,128]{1,0:T(8,128)(2,1)S(1)}, u32[]{:S(2)}, u32[]{:S(2)}) collective-permute-start(bf16[3072,128]{1,0:T(8,128)(2,1)S(1)} %get-tuple-element.67), channel_id=1, source_target_pairs={{0,2},{2,0},{4,6},{6,4},{1,3},{3,1},{5,7},{7,5},{8,10},{10,8},{12,... | collective-permute-start | bytes 2359304 | tf_op jit(solution)/shard_map/ppermute | solution.py:259
  131.1 32.5 %collective-permute-start.25 = (bf16[256,3072]{1,0:T(8,128)(2,1)S(1)}, bf16[256,3072]{1,0:T(8,128)(2,1)S(1)}, u32[]{:S(2)}, u32[]{:S(2)}) collective-permute-start(bf16[256,3072]{1,0:T(8,128)(2,1)S(1)} %collective-permute-done.10.refs_6_.refs_0_.refs_2_.refs_17_.refs_3_), channel_id=1, source_target_pairs={{0,2},{2,0},{4,6},{6,4},{1,3},{3,1},{5,7},{7,5},{8,10},{10,8},{12,... | collective-permute-start | bytes 4718600 | tf_op jit(solution)/shard_map/ppermute | solution.py:259
  139.3 50.9 %collective-permute-start.27 = (bf16[3072,256]{1,0:T(8,128)(2,1)S(1)}, bf16[3072,256]{1,0:T(8,128)(2,1)S(1)}, u32[]{:S(2)}, u32[]{:S(2)}) collective-permute-start(bf16[3072,256]{1,0:T(8,128)(2,1)S(1)} %terms.10.refs_5_.refs_0_.refs_2_), channel_id=1, source_target_pairs={{0,1},{1,0},{2,3},{3,2},{4,5},{5,4},{6,7},{7,6},{8,9},{9,8},{10,11... | collective-permute-start | bytes 4718600 | tf_op jit(solution)/shard_map/ppermute | solution.py:262
  162.4 7.6 %collective-permute-start.22 = (bf16[3072,128]{1,0:T(8,128)(2,1)S(1)}, bf16[3072,128]{1,0:T(8,128)(2,1)S(1)}, u32[]{:S(2)}, u32[]{:S(2)}) collective-permute-start(bf16[3072,128]{1,0:T(8,128)(2,1)S(1)} %get-tuple-element.72), channel_id=1, source_target_pairs={{0,2},{2,0},{4,6},{6,4},{1,3},{3,1},{5,7},{7,5},{8,10},{10,8},{12,... | collective-permute-start | bytes 2359304 | tf_op jit(solution)/shard_map/ppermute | solution.py:259
  162.5 34.2 %collective-permute-start.28 = (bf16[256,3072]{1,0:T(8,128)(2,1)S(1)}, bf16[256,3072]{1,0:T(8,128)(2,1)S(1)}, u32[]{:S(2)}, u32[]{:S(2)}) collective-permute-start(bf16[256,3072]{1,0:T(8,128)(2,1)S(1)} %collective-permute-done.21.refs_6_.refs_0_.refs_2_.refs_19_.refs_5_), channel_id=1, source_target_pairs={{0,2},{2,0},{4,6},{6,4},{1,3},{3,1},{5,7},{7,5},{8,10},{10,8},{12,... | collective-permute-start | bytes 4718600 | tf_op jit(solution)/shard_map/ppermute | solution.py:259
  163.0 19.5 %collective-permute-start.13 = (bf16[3072,128]{1,0:T(8,128)(2,1)S(1)}, bf16[3072,128]{1,0:T(8,128)(2,1)S(1)}, u32[]{:S(2)}, u32[]{:S(2)}) collective-permute-start(bf16[3072,128]{1,0:T(8,128)(2,1)S(1)} %add_convert_fusion.11.refs_8_), channel_id=1, source_target_pairs={{0,4},{2,6},{4,0},{6,2},{1,5},{3,7},{5,1},{7,3},{8,12},{10,14},{12... | collective-permute-start | bytes 2359304 | tf_op jit(solution)/shard_map/ppermute | solution.py:259
  194.9 9.5 %collective-permute-start.29 = (bf16[3072,128]{1,0:T(8,128)(2,1)S(1)}, bf16[3072,128]{1,0:T(8,128)(2,1)S(1)}, u32[]{:S(2)}, u32[]{:S(2)}) collective-permute-start(bf16[3072,128]{1,0:T(8,128)(2,1)S(1)} %get-tuple-element.82), channel_id=1, source_target_pairs={{0,2},{2,0},{4,6},{6,4},{1,3},{3,1},{5,7},{7,5},{8,10},{10,8},{12,... | collective-permute-start | bytes 2359304 | tf_op jit(solution)/shard_map/ppermute | solution.py:259
  195.0 37.6 %collective-permute-start.26 = (bf16[3072,256]{1,0:T(8,128)(2,1)}, bf16[3072,256]{1,0:T(8,128)(2,1)}, u32[]{:S(2)}, u32[]{:S(2)}) collective-permute-start(bf16[3072,256]{1,0:T(8,128)(2,1)} %terms.11.refs_5_.refs_0_.refs_2_), channel_id=1, source_target_pairs={{0,1},{1,0},{2,3},{3,2},{4,5},{5,4},{6,7},{7,6},{8,9},{9,8},{10,11... | collective-permute-start | bytes 4718600 | tf_op jit(solution)/shard_map/ppermute | solution.py:262
  196.6 48.7 %collective-permute-start.34 = (bf16[256,3072]{1,0:T(8,128)(2,1)}, bf16[256,3072]{1,0:T(8,128)(2,1)}, u32[]{:S(2)}, u32[]{:S(2)}) collective-permute-start(bf16[256,3072]{1,0:T(8,128)(2,1)} %collective-permute-done.16.refs_6_.refs_0_.refs_2_.refs_7_.refs_1_), channel_id=1, source_target_pairs={{0,2},{2,0},{4,6},{6,4},{1,3},{3,1},{5,7},{7,5},{8,10},{10,8},{12,... | collective-permute-start | bytes 4718600 | tf_op jit(solution)/shard_map/ppermute | solution.py:259
  203.3 63.0 %collective-permute-start.36 = (bf16[3072,256]{1,0:T(8,128)(2,1)}, bf16[3072,256]{1,0:T(8,128)(2,1)}, u32[]{:S(2)}, u32[]{:S(2)}) collective-permute-start(bf16[3072,256]{1,0:T(8,128)(2,1)} %terms.12.refs_15_.refs_0_.refs_2_), channel_id=1, source_target_pairs={{0,1},{1,0},{2,3},{3,2},{4,5},{5,4},{6,7},{7,6},{8,9},{9,8},{10,11... | collective-permute-start | bytes 4718600 | tf_op jit(solution)/shard_map/ppermute | solution.py:262
  203.8 28.7 %collective-permute-start.23 = (bf16[3072,128]{1,0:T(8,128)(2,1)}, bf16[3072,128]{1,0:T(8,128)(2,1)S(1)}, u32[]{:S(2)}, u32[]{:S(2)}) collective-permute-start(bf16[3072,128]{1,0:T(8,128)(2,1)} %add_convert_fusion.8.refs_7_), channel_id=1, source_target_pairs={{0,4},{2,6},{4,0},{6,2},{1,5},{3,7},{5,1},{7,3},{8,12},{10,14},{12... | collective-permute-start | bytes 2359304 | tf_op jit(solution)/shard_map/ppermute | solution.py:259
  205.5 39.8 %collective-permute-start.31 = (bf16[3072,128]{1,0:T(8,128)(2,1)}, bf16[3072,128]{1,0:T(8,128)(2,1)S(1)}, u32[]{:S(2)}, u32[]{:S(2)}) collective-permute-start(bf16[3072,128]{1,0:T(8,128)(2,1)} %add_convert_fusion.6.refs_16_), channel_id=1, source_target_pairs={{0,4},{2,6},{4,0},{6,2},{1,5},{3,7},{5,1},{7,3},{8,12},{10,14},{12... | collective-permute-start | bytes 2359304 | tf_op jit(solution)/shard_map/ppermute | solution.py:259
  245.3 29.3 %collective-permute-start.30 = (bf16[3072,128]{1,0:T(8,128)(2,1)S(1)}, bf16[3072,128]{1,0:T(8,128)(2,1)S(1)}, u32[]{:S(2)}, u32[]{:S(2)}) collective-permute-start(bf16[3072,128]{1,0:T(8,128)(2,1)S(1)} %get-tuple-element.85), channel_id=1, source_target_pairs={{0,2},{2,0},{4,6},{6,4},{1,3},{3,1},{5,7},{7,5},{8,10},{10,8},{12,... | collective-permute-start | bytes 2359304 | tf_op jit(solution)/shard_map/ppermute | solution.py:259
  259.9 40.9 %collective-permute-start.35 = (bf16[3072,256]{1,0:T(8,128)(2,1)S(1)}, bf16[3072,256]{1,0:T(8,128)(2,1)S(1)}, u32[]{:S(2)}, u32[]{:S(2)}) collective-permute-start(bf16[3072,256]{1,0:T(8,128)(2,1)S(1)} %terms.13.refs_5_.refs_0_.refs_2_), channel_id=1, source_target_pairs={{0,1},{1,0},{2,3},{3,2},{4,5},{5,4},{6,7},{7,6},{8,9},{9,8},{10,11... | collective-permute-start | bytes 4718600 | tf_op jit(solution)/shard_map/ppermute | solution.py:262
  273.2 25.6 %collective-permute-start.38 = (bf16[3072,128]{1,0:T(8,128)(2,1)S(1)}, bf16[3072,128]{1,0:T(8,128)(2,1)}, u32[]{:S(2)}, u32[]{:S(2)}) collective-permute-start(bf16[3072,128]{1,0:T(8,128)(2,1)S(1)} %get-tuple-element.92), channel_id=1, source_target_pairs={{0,2},{2,0},{4,6},{6,4},{1,3},{3,1},{5,7},{7,5},{8,10},{10,8},{12,... | collective-permute-start | bytes 2359304 | tf_op jit(solution)/shard_map/ppermute | solution.py:259
  274.6 41.6 %collective-permute-start.24 = (bf16[3072,128]{1,0:T(8,128)(2,1)}, bf16[3072,128]{1,0:T(8,128)(2,1)S(1)}, u32[]{:S(2)}, u32[]{:S(2)}) collective-permute-start(bf16[3072,128]{1,0:T(8,128)(2,1)} %add_convert_fusion.7), channel_id=1, source_target_pairs={{0,8},{8,16},{16,24},{24,0},{1,9},{9,17},{17,25},{25,1},{2,10},{10... | collective-permute-start | bytes 2359304 | tf_op jit(solution)/shard_map/ppermute | solution.py:262
  300.2 31.7 %collective-permute-start.39 = (bf16[3072,128]{1,0:T(8,128)(2,1)S(1)}, bf16[3072,128]{1,0:T(8,128)(2,1)}, u32[]{:S(2)}, u32[]{:S(2)}) collective-permute-start(bf16[3072,128]{1,0:T(8,128)(2,1)S(1)} %add_convert_fusion.2.refs_12_), channel_id=1, source_target_pairs={{0,4},{2,6},{4,0},{6,2},{1,5},{3,7},{5,1},{7,3},{8,12},{10,14},{12... | collective-permute-start | bytes 2359304 | tf_op jit(solution)/shard_map/ppermute | solution.py:259
  311.0 20.9 %collective-permute-start.37 = (bf16[3072,128]{1,0:T(8,128)(2,1)S(1)}, bf16[3072,128]{1,0:T(8,128)(2,1)S(1)}, u32[]{:S(2)}, u32[]{:S(2)}) collective-permute-start(bf16[3072,128]{1,0:T(8,128)(2,1)S(1)} %get-tuple-element.90), channel_id=1, source_target_pairs={{0,2},{2,0},{4,6},{6,4},{1,3},{3,1},{5,7},{7,5},{8,10},{10,8},{12,... | collective-permute-start | bytes 2359304 | tf_op jit(solution)/shard_map/ppermute | solution.py:259
  311.8 36.8 %collective-permute-start.32 = (bf16[1536,128]{1,0:T(8,128)(2,1)}, bf16[1536,128]{1,0:T(8,128)(2,1)S(1)}, u32[]{:S(2)}, u32[]{:S(2)}) collective-permute-start(bf16[1536,128]{1,0:T(8,128)(2,1)} %get-tuple-element.112), channel_id=1, source_target_pairs={{0,16},{8,24},{16,0},{24,8},{1,17},{9,25},{17,1},{25,9},{2,18},{10... | collective-permute-start | bytes 1179656 | tf_op jit(solution)/shard_map/ppermute | solution.py:262
  334.3 48.2 %collective-permute-start.40 = (bf16[3072,128]{1,0:T(8,128)(2,1)S(1)}, bf16[3072,128]{1,0:T(8,128)(2,1)S(1)}, u32[]{:S(2)}, u32[]{:S(2)}) collective-permute-start(bf16[3072,128]{1,0:T(8,128)(2,1)S(1)} %get-tuple-element.110), channel_id=1, source_target_pairs={{0,24},{8,0},{16,8},{24,16},{1,25},{9,1},{17,9},{25,17},{2,26},{10... | collective-permute-start | bytes 2359304 | tf_op jit(solution)/shard_map/ppermute | solution.py:262
  348.6 5.2 %collective-permute-start.41 = (f32[8,128]{1,0:T(8,128)S(1)}, f32[8,128]{1,0:T(8,128)S(1)}, u32[]{:S(2)}, u32[]{:S(2)}) collective-permute-start(f32[8,128]{1,0:T(8,128)S(1)} %broadcast_in_dim.3), channel_id=1, source_target_pairs={{0,8},{8,16},{16,24},{24,0},{1,9},{9,17},{17,25},{25,1},{2,10},{10... | collective-permute-start | bytes 12296 | tf_op jit(solution)/shard_map/ppermute | solution.py:262
  350.7 4.5 %collective-permute-start.42 = (f32[8,128]{1,0:T(8,128)S(1)}, f32[8,128]{1,0:T(8,128)S(1)}, u32[]{:S(2)}, u32[]{:S(2)}) collective-permute-start(f32[8,128]{1,0:T(8,128)S(1)} %broadcast_in_dim.3), channel_id=1, source_target_pairs={{0,16},{8,24},{16,0},{24,8},{1,17},{9,25},{17,1},{25,9},{2,18},{10... | collective-permute-start | bytes 12296 | tf_op jit(solution)/shard_map/ppermute | solution.py:262
  352.5 4.3 %collective-permute-start.43 = (f32[8,128]{1,0:T(8,128)S(1)}, f32[8,128]{1,0:T(8,128)S(1)}, u32[]{:S(2)}, u32[]{:S(2)}) collective-permute-start(f32[8,128]{1,0:T(8,128)S(1)} %broadcast_in_dim.3), channel_id=1, source_target_pairs={{0,24},{8,0},{16,8},{24,16},{1,25},{9,1},{17,9},{25,17},{2,26},{10... | collective-permute-start | bytes 12296 | tf_op jit(solution)/shard_map/ppermute | solution.py:262
  352.5 30.0 %collective-permute-start.33 = (bf16[1536,128]{1,0:T(8,128)(2,1)S(1)}, bf16[1536,128]{1,0:T(8,128)(2,1)S(1)}, u32[]{:S(2)}, u32[]{:S(2)}) collective-permute-start(bf16[1536,128]{1,0:T(8,128)(2,1)S(1)} %get-tuple-element.113), channel_id=1, source_target_pairs={{0,16},{8,24},{16,0},{24,8},{1,17},{9,25},{17,1},{25,9},{2,18},{10... | collective-permute-start | bytes 1179656 | tf_op jit(solution)/shard_map/ppermute | solution.py:262
  356.8 1.9 collective-permute-start.44
  356.8 3.7 collective-permute-start.45
  358.3 3.0 collective-permute-start.46
  361.4 3.6 collective-permute-start.47
  (68 other events, 879.9 us)

commit v4 on v3

--- a/solution.py
+++ b/solution.py
@@ -280,7 +280,7 @@
     groups = [[(mask, step), (mask + 1, step)] for mask, step in leads]
     count = len(groups)
     last = count - 1
-    own_tie = {last - 3: "A in", last - 2: "A out", last - 1: "C in", last: "C out"}
+    own_tie = {last - 3: ("terms", last - 1), last - 2: "A out", last - 1: "C in", last: "C out"}
     far_tie = {last - 3: ("terms", last), last - 1: "norm"}
 
     def shards(tokens, w_in, w_out, out_grad):
@@ -329,7 +329,7 @@
             if g < last and all((p, step) in sums for p in pairs):
                 finish(step)
                 if step:
-                    tie("C in" if g + 3 == last - 1 else ("gelu", g + 3) if g + 3 < last else "norm", returned[-1][0])
+                    tie(("gelu", g + 3) if g + 3 < last else "norm", returned[-1][0])
 
         def finish(step):
             total = sums[0, step]
@@ -398,14 +398,15 @@
                 others = [[later(v) for v in part[-max(1, len(part) * (n_gz > 2)) :]] for part in d_parts]
                 d_terms = [jnp.concatenate(both, axis=0) for both in zip(*others)]
                 terms[0] = h_terms, d_terms if n_gz > 2 else [d_own] + d_terms
-            if g == last - 1:
-                gin, _ = run_grads("A in", 0, None, last - 2, none)
+            if g == last - 2:
+                gin, _ = run_grads("A in", 0, None, last - 3, none)
+            if g == last:
+                gout, _ = run_grads("A out", None, 0, last - 1, none)
             run_gelu(g - 1)
-        gout, _ = run_grads("A out", None, 0, last, none)
         run_gelu(last)
-        gin, gin_squares = run_grads("C in", last - 2, None, count, (gin, gout), True)
+        gin, gin_squares = run_grads("C in", last - 3, None, count, (gin, gout), True)
         finish(n_gx - 1)
-        gout, gout_squares = run_grads("C out", None, last, count, (gin, gout), True)
+        gout, gout_squares = run_grads("C out", None, last - 1, count, (gin, gout), True)
 
         square = jnp.broadcast_to(jnp.sum(gin_squares) + jnp.sum(gout_squares), (8, 128))
         square = over_gx(lax.optimization_barrier((square, waits("norm")))[0])

time: 386 us -> 383 us (level)
    unnamed x138 -> x146, local copies, waits for them, and re-layouts: 36.9 us -> 34.7 us
where the time goes in v4:
time: 383 us; the launch traced here: 382 us
  Pallas kernels  178 us (46%)
  waiting for transfers between devices  110 us (29%)
  starting transfers between devices  41.1 us (11%)
  local copies, waits for them, and re-layouts  35.4 us (9%)
  other arithmetic  13.3 us (3%)
    pallas_call x4, Pallas kernels, grad_call(): pl.pallas_call(kernel, grid=(cols // tile,), in_specs=specs + [ANY] * len...  65.1 us
    ppermute x21, waiting for transfers between devices, shift(): lax.ppermute(value, axis, [(i, (i + step) % size) for i in range(size)])  63.7 us
    pallas_call x8, Pallas kernels, gelu_call(): pl.pallas_call(kernel, grid=(row_steps + steps,), in_specs=[h_spec] * cou...  47.6 us
    ppermute x27, waiting for transfers between devices, swap(): return lax.ppermute(value, 'gy', [(i, i ^ mask) for i in range(n_gy)])  46.2 us
    pallas_call x7, Pallas kernels, terms_call(): pl.pallas_call(kernel, grid=(2 * steps,), in_specs=[once((rows, depth), 0...  43.9 us
    unnamed x146, local copies, waits for them, and re-layouts  34.7 us
    ppermute x21, starting transfers between devices, shift(): lax.ppermute(value, axis, [(i, (i + step) % size) for i in range(size)])  28.7 us
    pallas_call x2, Pallas kernels, scale_call(): pl.pallas_call(kernel, grid=((cols if flip else rows) // tile,), in_specs...  12.6 us
  transfers between devices with their start and end apart: 48, of which 21 were waited for; matrix products, arithmetic and copies ran while one was open for 3% of the time, Pallas kernels for 47%

profile of v4, /device:TPU:8, one launch (start us, length us, event | category | flops | bytes accessed | tf_op | source)
XLA Modules:
  0.0 381.7 jit_solution(4681602642475496363)
XLA Ops:
  5.5 3.7 copy-done
  9.2 2.9 half_terms.2.refs_3_.refs_0_
  13.8 3.7 copy-done.4
  17.4 2.8 half_terms.3.refs_0_.refs_2_
  20.9 3.6 flip.1.refs_4_.refs_6_
  24.6 14.4 %collective-permute-done.4.refs_7_.refs_0_.refs_2_.refs_8_.refs_10_ = bf16[256,3072]{1,0:T(8,128)(2,1)S(1)} collective-permute-done((bf16[256,3072]{1,0:T(8,128)(2,1)S(1)}, bf16[256,3072]{1,0:T(8,128)(2,1)S(1)}, u32[]{:S(2)}, u32[]{:S(2)}) %collective-permute-start.4) | collective-permute-done | bytes 1572896 | tf_op jit(solution)/shard_map/ppermute | solution.py:262
  42.2 2.6 collective-permute-start.10
  46.4 5.7 %terms.7.refs_5_.refs_0_.refs_2_ = bf16[3072,256]{1,0:T(8,128)(2,1)S(1)} custom-call(bf16[256,3072]{1,0:T(8,128)(2,1)S(1)} %collective-permute-done.3.refs_0_.refs_2_.refs_6_.refs_8_, bf16[256,3072]{1,0:T(8,128)(2,1)S(1)} %collective-permute-done.5.refs_1_.refs_3_.refs_7_.refs_9_, ...), custom_call_target="tpu_custom_call" | custom-call | tf_op jit(solution)/shard_map/terms/pallas_call | solution.py:91
  52.7 3.9 %collective-permute-done.6 = bf16[768,256]{1,0:T(8,128)(2,1)S(1)} collective-permute-done((bf16[768,256]{1,0:T(8,128)(2,1)S(1)}, bf16[768,256]{1,0:T(8,128)(2,1)S(1)}, u32[]{:S(2)}, u32[]{:S(2)}) %collective-permute-start.6) | collective-permute-done | bytes 393248 | tf_op jit(solution)/shard_map/ppermute | solution.py:262
  56.7 4.7 %gelu.8 = (bf16[1536,256]{1,0:T(8,128)(2,1)S(1)}, bf16[1536,256]{1,0:T(8,128)(2,1)S(1)}, bf16[3072,128]{1,0:T(8,128)(2,1)S(1)}, bf16[3072,128]{1,0:T(8,128)(2,1)S(1)}) custom-call(bf16[1536,256]{1,0:T(8,128)(2,1)S(1)} %half_terms.2.refs_3_.refs_0_, bf16[1536,256]{1,0:T(8,128)(2,1)S(1)} %collective-permute-done.1.refs_1_, ...), custom_call_target="tpu_custom_call" | custom-call | tf_op jit(solution)/shard_map/gelu/pallas_call | solution.py:171
  61.5 5.7 %terms.8.refs_5_.refs_0_.refs_2_ = bf16[3072,256]{1,0:T(8,128)(2,1)S(1)} custom-call(bf16[256,3072]{1,0:T(8,128)(2,1)S(1)} %collective-permute-done.4.refs_7_.refs_0_.refs_2_.refs_8_.refs_10_, bf16[256,3072]{1,0:T(8,128)(2,1)S(1)} %collective-permute-done.9.refs_1_.refs_3_.refs_9_.refs_11_, ...), custom_call_target="tpu_custom_call" | custom-call | tf_op jit(solution)/shard_map/terms/pallas_call | solution.py:91
  67.3 9.8 %collective-permute-done.11.refs_7_.refs_0_.refs_2_.refs_10_.refs_12_ = bf16[256,3072]{1,0:T(8,128)(2,1)S(1)} collective-permute-done((bf16[256,3072]{1,0:T(8,128)(2,1)S(1)}, bf16[256,3072]{1,0:T(8,128)(2,1)S(1)}, u32[]{:S(2)}, u32[]{:S(2)}) %collective-permute-start.11) | collective-permute-done | bytes 1572896 | tf_op jit(solution)/shard_map/ppermute | solution.py:259
  78.9 2.5 collective-permute-start.16
  83.2 7.1 %collective-permute-done.8.refs_1_.refs_3_ = bf16[3072,256]{1,0:T(8,128)(2,1)S(1)} collective-permute-done((bf16[3072,256]{1,0:T(8,128)(2,1)S(1)}, bf16[3072,256]{1,0:T(8,128)(2,1)S(1)}, u32[]{:S(2)}, u32[]{:S(2)}) %collective-permute-start.8) | collective-permute-done | bytes 1572896 | tf_op jit(solution)/shard_map/ppermute | solution.py:262
  92.9 4.7 %gelu.9 = (bf16[1536,256]{1,0:T(8,128)(2,1)S(1)}, bf16[1536,256]{1,0:T(8,128)(2,1)S(1)}, bf16[3072,128]{1,0:T(8,128)(2,1)S(1)}, bf16[3072,128]{1,0:T(8,128)(2,1)S(1)}) custom-call(bf16[3072,256]{1,0:T(8,128)(2,1)S(1)} %terms.7.refs_5_.refs_0_.refs_2_, bf16[3072,256]{1,0:T(8,128)(2,1)S(1)} %copy-done.31, bf16[3072,256]{1,0:T(8,128)(2,1)S(1)} %terms.7.refs_5_.refs_0_.refs_2_, ...), custom_call_target="tpu_custom_call" | custom-call | tf_op jit(solution)/shard_map/gelu/pallas_call | solution.py:171
  97.7 5.7 %terms.9.refs_5_.refs_0_.refs_2_ = bf16[3072,256]{1,0:T(8,128)(2,1)S(1)} custom-call(bf16[256,3072]{1,0:T(8,128)(2,1)S(1)} %collective-permute-done.11.refs_7_.refs_0_.refs_2_.refs_10_.refs_12_, bf16[256,3072]{1,0:T(8,128)(2,1)S(1)} %collective-permute-done.15.refs_1_.refs_3_.refs_11_.refs_13_, ...), custom_call_target="tpu_custom_call" | custom-call | tf_op jit(solution)/shard_map/terms/pallas_call | solution.py:91
  103.5 10.4 %collective-permute-done.17.refs_7_.refs_0_.refs_2_.refs_14_.refs_4_ = bf16[256,3072]{1,0:T(8,128)(2,1)S(1)} collective-permute-done((bf16[256,3072]{1,0:T(8,128)(2,1)S(1)}, bf16[256,3072]{1,0:T(8,128)(2,1)S(1)}, u32[]{:S(2)}, u32[]{:S(2)}) %collective-permute-start.17) | collective-permute-done | bytes 1572896 | tf_op jit(solution)/shard_map/ppermute | solution.py:259
  118.0 6.0 %collective-permute-done.14.refs_1_.refs_3_ = bf16[3072,256]{1,0:T(8,128)(2,1)S(1)} collective-permute-done((bf16[3072,256]{1,0:T(8,128)(2,1)S(1)}, bf16[3072,256]{1,0:T(8,128)(2,1)S(1)}, u32[]{:S(2)}, u32[]{:S(2)}) %collective-permute-start.14) | collective-permute-done | bytes 1572896 | tf_op jit(solution)/shard_map/ppermute | solution.py:262
  124.0 4.7 %gelu.10 = (bf16[1536,256]{1,0:T(8,128)(2,1)S(1)}, bf16[1536,256]{1,0:T(8,128)(2,1)S(1)}, bf16[3072,128]{1,0:T(8,128)(2,1)S(1)}, bf16[3072,128]{1,0:T(8,128)(2,1)S(1)}) custom-call(bf16[3072,256]{1,0:T(8,128)(2,1)S(1)} %terms.8.refs_5_.refs_0_.refs_2_, bf16[3072,256]{1,0:T(8,128)(2,1)S(1)} %collective-permute-done.14.refs_1_.refs_3_, ...), custom_call_target="tpu_custom_call" | custom-call | tf_op jit(solution)/shard_map/gelu/pallas_call | solution.py:171
  129.3 6.5 %terms.10.refs_5_.refs_0_.refs_2_ = bf16[3072,256]{1,0:T(8,128)(2,1)} custom-call(bf16[256,3072]{1,0:T(8,128)(2,1)S(1)} %collective-permute-done.17.refs_7_.refs_0_.refs_2_.refs_14_.refs_4_, bf16[256,3072]{1,0:T(8,128)(2,1)S(1)} %collective-permute-done.20.refs_1_.refs_3_.refs_15_.refs_5_, ...), custom_call_target="tpu_custom_call" | custom-call | tf_op jit(solution)/shard_map/terms/pallas_call | solution.py:91
  137.9 14.0 %collective-permute-done.21.refs_6_.refs_0_.refs_2_.refs_8_ = bf16[256,3072]{1,0:T(8,128)(2,1)S(1)} collective-permute-done((bf16[256,3072]{1,0:T(8,128)(2,1)S(1)}, bf16[256,3072]{1,0:T(8,128)(2,1)S(1)}, u32[]{:S(2)}, u32[]{:S(2)}) %collective-permute-start.21) | collective-permute-done | bytes 1572896 | tf_op jit(solution)/shard_map/ppermute | solution.py:259
  151.9 5.8 %collective-permute-done.19.refs_1_.refs_3_ = bf16[3072,256]{1,0:T(8,128)(2,1)S(1)} collective-permute-done((bf16[3072,256]{1,0:T(8,128)(2,1)S(1)}, bf16[3072,256]{1,0:T(8,128)(2,1)S(1)}, u32[]{:S(2)}, u32[]{:S(2)}) %collective-permute-start.19) | collective-permute-done | bytes 1572896 | tf_op jit(solution)/shard_map/ppermute | solution.py:262
  160.3 5.5 %gelu.11 = (bf16[1536,256]{1,0:T(8,128)(2,1)S(1)}, bf16[1536,256]{1,0:T(8,128)(2,1)S(1)}, bf16[3072,128]{1,0:T(8,128)(2,1)S(1)}, bf16[3072,128]{1,0:T(8,128)(2,1)}) custom-call(bf16[3072,256]{1,0:T(8,128)(2,1)S(1)} %terms.9.refs_5_.refs_0_.refs_2_, bf16[3072,256]{1,0:T(8,128)(2,1)S(1)} %copy-done.29, bf16[3072,256]{1,0:T(8,128)(2,1)S(1)} %terms.9.refs_5_.refs_0_.refs_2_, ...), custom_call_target="tpu_custom_call" | custom-call | tf_op jit(solution)/shard_map/gelu/pallas_call | solution.py:171
  166.5 6.5 %terms.11.refs_12_.refs_0_.refs_2_ = bf16[3072,256]{1,0:T(8,128)(2,1)} custom-call(bf16[256,3072]{1,0:T(8,128)(2,1)S(1)} %collective-permute-done.10.refs_6_.refs_0_.refs_2_.refs_16_, bf16[256,3072]{1,0:T(8,128)(2,1)S(1)} %collective-permute-done.25.refs_1_.refs_3_.refs_17_.refs_7_, ...), custom_call_target="tpu_custom_call" | custom-call | tf_op jit(solution)/shard_map/terms/pallas_call | solution.py:91
  174.9 14.8 %grad.4 = (bf16[1536,3072]{1,0:T(8,128)(2,1)}, f32[8,512]{1,0:T(8,128)}) custom-call(bf16[1536,256]{1,0:T(8,128)(2,1)} %copy-done.44, bf16[1536,256]{1,0:T(8,128)(2,1)} %copy-done.46, bf16[1536,256]{1,0:T(8,128)(2,1)} %copy-done.47, bf16[1536,256]{1,0:T(8,128)(2,1)} %copy-done.49, bf16[256,3072]{1,0:T(8,128)(2,1)} %copy-done.13, ...), custom_call_target="tpu_custom_call" | custom-call | tf_op jit(solution)/shard_map/grad/pallas_call | solution.py:219
  191.5 3.7 copy-done.1
  195.2 7.4 %gelu.12 = (bf16[1536,256]{1,0:T(8,128)(2,1)S(1)}, bf16[1536,256]{1,0:T(8,128)(2,1)S(1)}, bf16[3072,128]{1,0:T(8,128)(2,1)S(1)}, bf16[3072,128]{1,0:T(8,128)(2,1)S(1)}) custom-call(bf16[3072,256]{1,0:T(8,128)(2,1)} %terms.10.refs_5_.refs_0_.refs_2_, bf16[3072,256]{1,0:T(8,128)(2,1)} %collective-permute-done.28.refs_1_.refs_3_, ...), custom_call_target="tpu_custom_call" | custom-call | tf_op jit(solution)/shard_map/gelu/pallas_call | solution.py:171
  205.2 3.8 %copy-done.5 = bf16[1536,3072]{1,0:T(8,128)(2,1)S(1)} copy-done((bf16[1536,3072]{1,0:T(8,128)(2,1)S(1)}, bf16[1536,3072]{1,0:T(8,128)(2,1)}, u32[]{:S(2)}) %copy-start.5) | copy-done | bytes 9437208
  209.1 8.0 %terms.12.refs_5_.refs_0_.refs_2_ = bf16[3072,256]{1,0:T(8,128)(2,1)} custom-call(bf16[256,3072]{1,0:T(8,128)(2,1)S(1)} %collective-permute-done.21.refs_6_.refs_0_.refs_2_.refs_8_, bf16[256,3072]{1,0:T(8,128)(2,1)} %collective-permute-done.27.refs_1_.refs_3_.refs_9_, bf16[256,3072]{1,0:T(8,128)(2,1)S(1)} %collective-permute-done.21.refs_6_.refs_0_.refs_2_.refs_8_, ...), custom_call_target="tpu_custom_call" | custom-call | tf_op jit(solution)/shard_map/terms/pallas_call | solution.py:91
  219.4 5.8 %collective-permute-done.26.refs_1_.refs_3_ = bf16[3072,256]{1,0:T(8,128)(2,1)} collective-permute-done((bf16[3072,256]{1,0:T(8,128)(2,1)}, bf16[3072,256]{1,0:T(8,128)(2,1)}, u32[]{:S(2)}, u32[]{:S(2)}) %collective-permute-start.26) | collective-permute-done | bytes 1572896 | tf_op jit(solution)/shard_map/ppermute | solution.py:262
  225.3 6.9 %gelu.13 = (bf16[1536,256]{1,0:T(8,128)(2,1)S(1)}, bf16[1536,256]{1,0:T(8,128)(2,1)S(1)}, bf16[3072,128]{1,0:T(8,128)(2,1)S(1)}, bf16[3072,128]{1,0:T(8,128)(2,1)S(1)}) custom-call(bf16[3072,256]{1,0:T(8,128)(2,1)} %terms.11.refs_12_.refs_0_.refs_2_, bf16[3072,256]{1,0:T(8,128)(2,1)} %collective-permute-done.26.refs_1_.refs_3_, ...), custom_call_target="tpu_custom_call" | custom-call | tf_op jit(solution)/shard_map/gelu/pallas_call | solution.py:171
  233.6 5.9 %collective-permute-done.31.refs_7_ = bf16[3072,128]{1,0:T(8,128)(2,1)S(1)} collective-permute-done((bf16[3072,128]{1,0:T(8,128)(2,1)S(1)}, bf16[3072,128]{1,0:T(8,128)(2,1)S(1)}, u32[]{:S(2)}, u32[]{:S(2)}) %collective-permute-start.31) | collective-permute-done | bytes 786464 | tf_op jit(solution)/shard_map/ppermute | solution.py:259
  239.6 5.7 %terms.13.refs_18_.refs_0_.refs_2_ = bf16[3072,256]{1,0:T(8,128)(2,1)S(1)} custom-call(bf16[256,3072]{1,0:T(8,128)(2,1)S(1)} %copy-done.8, bf16[256,3072]{1,0:T(8,128)(2,1)S(1)} %collective-permute-done.34.refs_1_.refs_3_.refs_11_.refs_5_, bf16[256,3072]{1,0:T(8,128)(2,1)S(1)} %copy-done.8, ...), custom_call_target="tpu_custom_call" | custom-call | tf_op jit(solution)/shard_map/terms/pallas_call | solution.py:91
  248.7 20.3 %grad.5 = (bf16[1536,3072]{1,0:T(8,128)(2,1)}, f32[8,512]{1,0:T(8,128)}) custom-call(bf16[1536,256]{1,0:T(8,128)(2,1)} %copy-done.39, bf16[1536,256]{1,0:T(8,128)(2,1)} %copy-done.40, bf16[1536,256]{1,0:T(8,128)(2,1)} %copy-done.41, bf16[1536,256]{1,0:T(8,128)(2,1)} %copy-done.42, bf16[1536,256]{1,0:T(8,128)(2,1)} %copy-done.32, ...), custom_call_target="tpu_custom_call" | custom-call | tf_op jit(solution)/shard_map/grad/pallas_call | solution.py:219
  269.9 3.7 copy-done.2
  275.4 7.1 %gelu.14 = (bf16[1536,256]{1,0:T(8,128)(2,1)S(1)}, bf16[1536,256]{1,0:T(8,128)(2,1)S(1)}, bf16[3072,128]{1,0:T(8,128)(2,1)S(1)}, bf16[3072,128]{1,0:T(8,128)(2,1)S(1)}) custom-call(bf16[3072,256]{1,0:T(8,128)(2,1)} %terms.12.refs_5_.refs_0_.refs_2_, bf16[3072,256]{1,0:T(8,128)(2,1)} %collective-permute-done.36.refs_1_.refs_3_, ...), custom_call_target="tpu_custom_call" | custom-call | tf_op jit(solution)/shard_map/gelu/pallas_call | solution.py:171
  282.6 2.3 collective-permute-done.38
  286.5 4.8 %collective-permute-done.35.refs_1_.refs_3_ = bf16[3072,256]{1,0:T(8,128)(2,1)} collective-permute-done((bf16[3072,256]{1,0:T(8,128)(2,1)S(1)}, bf16[3072,256]{1,0:T(8,128)(2,1)}, u32[]{:S(2)}, u32[]{:S(2)}) %collective-permute-start.35) | collective-permute-done | bytes 1572896 | tf_op jit(solution)/shard_map/ppermute | solution.py:262
  291.4 6.6 %gelu.15 = (bf16[1536,256]{1,0:T(8,128)(2,1)S(1)}, bf16[1536,256]{1,0:T(8,128)(2,1)S(1)}, bf16[3072,128]{1,0:T(8,128)(2,1)S(1)}, bf16[3072,128]{1,0:T(8,128)(2,1)S(1)}) custom-call(bf16[3072,256]{1,0:T(8,128)(2,1)S(1)} %copy-done.23, bf16[3072,256]{1,0:T(8,128)(2,1)} %collective-permute-done.35.refs_1_.refs_3_, bf16[3072,256]{1,0:T(8,128)(2,1)S(1)} %copy-done.23, ...), custom_call_target="tpu_custom_call" | custom-call | tf_op jit(solution)/shard_map/gelu/pallas_call | solution.py:171
  300.9 16.7 %grad.6 = (bf16[1536,3072]{1,0:T(8,128)(2,1)}, f32[8,512]{1,0:T(8,128)}) custom-call(bf16[1536,256]{1,0:T(8,128)(2,1)} %copy-done.43, bf16[1536,256]{1,0:T(8,128)(2,1)} %copy-done.45, bf16[1536,256]{1,0:T(8,128)(2,1)} %copy-done.48, bf16[1536,256]{1,0:T(8,128)(2,1)} %copy-done.50, bf16[256,3072]{1,0:T(8,128)(2,1)} %copy-done.11, ...), custom_call_target="tpu_custom_call" | custom-call | tf_op jit(solution)/shard_map/grad/pallas_call | solution.py:219
  317.6 2.4 add_convert_fusion.1
  321.8 13.3 %grad.7 = (bf16[1536,3072]{1,0:T(8,128)(2,1)}, f32[8,512]{1,0:T(8,128)}) custom-call(bf16[1536,256]{1,0:T(8,128)(2,1)} %copy-done.34, bf16[1536,256]{1,0:T(8,128)(2,1)} %copy-done.35, bf16[256,3072]{1,0:T(8,128)(2,1)} %copy-done.6, bf16[256,3072]{1,0:T(8,128)(2,1)} %collective-permute-done.27.refs_1_.refs_3_.refs_9_, bf16[256,3072]{1,0:T(8,128)(2,1)} %copy-done.7, ...), custom_call_target="tpu_custom_call" | custom-call | tf_op jit(solution)/shard_map/grad/pallas_call | solution.py:219
  339.3 3.2 collective-permute-start.42
  344.1 9.8 %collective-permute-done.43 = f32[8,128]{1,0:T(8,128)S(1)} collective-permute-done((f32[8,128]{1,0:T(8,128)S(1)}, f32[8,128]{1,0:T(8,128)S(1)}, u32[]{:S(2)}, u32[]{:S(2)}) %collective-permute-start.43) | collective-permute-done | bytes 4128 | tf_op jit(solution)/shard_map/ppermute | solution.py:262
  359.3 2.1 collective-permute-done.47
  362.6 3.7 copy-done.24
  366.3 7.8 %scale.2.refs_0_ = bf16[3072,1536]{1,0:T(8,128)(2,1)} custom-call(f32[1,1]{1,0:T(1,128)S(6)} %sqrt.3.factor_ref, bf16[1536,3072]{1,0:T(8,128)(2,1)S(1)} %copy-done.24), custom_call_target="tpu_custom_call" | custom-call | tf_op jit(solution)/shard_map/scale/pallas_call | solution.py:238
  374.2 4.7 %scale.3 = bf16[1536,3072]{1,0:T(8,128)(2,1)} custom-call(f32[1,1]{1,0:T(1,128)S(6)} %sqrt.3.factor_ref, bf16[1536,3072]{1,0:T(8,128)(2,1)S(1)} %copy-done.25, bf16[3072,1536]{1,0:T(8,128)(2,1)} %scale.2.refs_0_), custom_call_target="tpu_custom_call" | custom-call | tf_op jit(solution)/shard_map/scale/pallas_call | solution.py:238
  (244 shorter events, 64.5 us)
Async XLA Ops:
  2.1 3.5 collective-permute-start
  2.1 36.8 %collective-permute-start.4 = (bf16[256,3072]{1,0:T(8,128)(2,1)S(1)}, bf16[256,3072]{1,0:T(8,128)(2,1)S(1)}, u32[]{:S(2)}, u32[]{:S(2)}) collective-permute-start(bf16[256,3072]{1,0:T(8,128)(2,1)S(1)} %constant_dynamic-update-slice_fusion.refs_0_.refs_4_.refs_6_), channel_id=1, source_target_pairs={{0,24},{8,0},{16,8},{24,16},{1,25},{9,1},{17,9},{25,17},{2,26},{10... | collective-permute-start | bytes 4718600 | tf_op jit(solution)/shard_map/ppermute | solution.py:262
  2.2 36.7 %collective-permute-start.3 = (bf16[256,3072]{1,0:T(8,128)(2,1)S(1)}, bf16[256,3072]{1,0:T(8,128)(2,1)S(1)}, u32[]{:S(2)}, u32[]{:S(2)}) collective-permute-start(bf16[256,3072]{1,0:T(8,128)(2,1)S(1)} %constant_dynamic-update-slice_fusion.refs_0_.refs_4_.refs_6_), channel_id=1, source_target_pairs={{0,4},{2,6},{4,0},{6,2},{1,5},{3,7},{5,1},{7,3},{8,12},{10,14},{12... | collective-permute-start | bytes 4718600 | tf_op jit(solution)/shard_map/ppermute | solution.py:259
  12.2 28.1 %collective-permute-start.1 = (bf16[1536,256]{1,0:T(8,128)(2,1)S(1)}, bf16[1536,256]{1,0:T(8,128)(2,1)S(1)}, u32[]{:S(2)}, u32[]{:S(2)}) collective-permute-start(bf16[1536,256]{1,0:T(8,128)(2,1)S(1)} %half_terms.2.refs_3_.refs_0_), channel_id=1, source_target_pairs={{0,1},{1,0},{2,3},{3,2},{4,5},{5,4},{6,7},{7,6},{8,9},{9,8},{10,11... | collective-permute-start | bytes 2359304 | tf_op jit(solution)/shard_map/ppermute | solution.py:262
  20.4 19.9 %collective-permute-start.2 = (bf16[768,256]{1,0:T(8,128)(2,1)S(1)}, bf16[768,256]{1,0:T(8,128)(2,1)S(1)}, u32[]{:S(2)}, u32[]{:S(2)}) collective-permute-start(bf16[768,256]{1,0:T(8,128)(2,1)S(1)} %get-tuple-element.114), channel_id=1, source_target_pairs={{0,1},{1,0},{2,3},{3,2},{4,5},{5,4},{6,7},{7,6},{8,9},{9,8},{10,11... | collective-permute-start | bytes 1179656 | tf_op jit(solution)/shard_map/ppermute | solution.py:262
  40.2 6.1 %collective-permute-start.5 = (bf16[256,3072]{1,0:T(8,128)(2,1)S(1)}, bf16[256,3072]{1,0:T(8,128)(2,1)S(1)}, u32[]{:S(2)}, u32[]{:S(2)}) collective-permute-start(bf16[256,3072]{1,0:T(8,128)(2,1)S(1)} %collective-permute-done.3.refs_0_.refs_2_.refs_6_.refs_8_), channel_id=1, source_target_pairs={{0,2},{2,0},{4,6},{6,4},{1,3},{3,1},{5,7},{7,5},{8,10},{10,8},{12,... | collective-permute-start | bytes 4718600 | tf_op jit(solution)/shard_map/ppermute | solution.py:259
  40.2 21.2 %collective-permute-start.9 = (bf16[256,3072]{1,0:T(8,128)(2,1)S(1)}, bf16[256,3072]{1,0:T(8,128)(2,1)S(1)}, u32[]{:S(2)}, u32[]{:S(2)}) collective-permute-start(bf16[256,3072]{1,0:T(8,128)(2,1)S(1)} %collective-permute-done.4.refs_7_.refs_0_.refs_2_.refs_8_.refs_10_), channel_id=1, source_target_pairs={{0,2},{2,0},{4,6},{6,4},{1,3},{3,1},{5,7},{7,5},{8,10},{10,8},{12,... | collective-permute-start | bytes 4718600 | tf_op jit(solution)/shard_map/ppermute | solution.py:259
  40.7 36.3 %collective-permute-start.11 = (bf16[256,3072]{1,0:T(8,128)(2,1)S(1)}, bf16[256,3072]{1,0:T(8,128)(2,1)S(1)}, u32[]{:S(2)}, u32[]{:S(2)}) collective-permute-start(bf16[256,3072]{1,0:T(8,128)(2,1)S(1)} %collective-permute-done.4.refs_7_.refs_0_.refs_2_.refs_8_.refs_10_), channel_id=1, source_target_pairs={{0,4},{2,6},{4,0},{6,2},{1,5},{3,7},{5,1},{7,3},{8,12},{10,14},{12... | collective-permute-start | bytes 4718600 | tf_op jit(solution)/shard_map/ppermute | solution.py:259
  42.2 36.2 %collective-permute-start.10 = (bf16[256,3072]{1,0:T(8,128)(2,1)S(1)}, bf16[256,3072]{1,0:T(8,128)(2,1)S(1)}, u32[]{:S(2)}, u32[]{:S(2)}) collective-permute-start(bf16[256,3072]{1,0:T(8,128)(2,1)S(1)} %collective-permute-done.4.refs_7_.refs_0_.refs_2_.refs_8_.refs_10_), channel_id=1, source_target_pairs={{0,24},{8,0},{16,8},{24,16},{1,25},{9,1},{17,9},{25,17},{2,26},{10... | collective-permute-start | bytes 4718600 | tf_op jit(solution)/shard_map/ppermute | solution.py:262
  44.8 11.8 %collective-permute-start.6 = (bf16[768,256]{1,0:T(8,128)(2,1)S(1)}, bf16[768,256]{1,0:T(8,128)(2,1)S(1)}, u32[]{:S(2)}, u32[]{:S(2)}) collective-permute-start(bf16[768,256]{1,0:T(8,128)(2,1)S(1)} %get-tuple-element.115), channel_id=1, source_target_pairs={{0,1},{1,0},{2,3},{3,2},{4,5},{5,4},{6,7},{7,6},{8,9},{9,8},{10,11... | collective-permute-start | bytes 1179656 | tf_op jit(solution)/shard_map/ppermute | solution.py:262
  52.1 38.2 %collective-permute-start.8 = (bf16[3072,256]{1,0:T(8,128)(2,1)S(1)}, bf16[3072,256]{1,0:T(8,128)(2,1)S(1)}, u32[]{:S(2)}, u32[]{:S(2)}) collective-permute-start(bf16[3072,256]{1,0:T(8,128)(2,1)S(1)} %terms.7.refs_5_.refs_0_.refs_2_), channel_id=1, source_target_pairs={{0,1},{1,0},{2,3},{3,2},{4,5},{5,4},{6,7},{7,6},{8,9},{9,8},{10,11... | collective-permute-start | bytes 4718600 | tf_op jit(solution)/shard_map/ppermute | solution.py:262
  61.4 20.0 %collective-permute-start.7 = (bf16[3072,128]{1,0:T(8,128)(2,1)S(1)}, bf16[3072,128]{1,0:T(8,128)(2,1)S(1)}, u32[]{:S(2)}, u32[]{:S(2)}) collective-permute-start(bf16[3072,128]{1,0:T(8,128)(2,1)S(1)} %get-tuple-element.58), channel_id=1, source_target_pairs={{0,2},{2,0},{4,6},{6,4},{1,3},{3,1},{5,7},{7,5},{8,10},{10,8},{12,... | collective-permute-start | bytes 2359304 | tf_op jit(solution)/shard_map/ppermute | solution.py:259
  77.1 20.6 %collective-permute-start.15 = (bf16[256,3072]{1,0:T(8,128)(2,1)S(1)}, bf16[256,3072]{1,0:T(8,128)(2,1)S(1)}, u32[]{:S(2)}, u32[]{:S(2)}) collective-permute-start(bf16[256,3072]{1,0:T(8,128)(2,1)S(1)} %collective-permute-done.11.refs_7_.refs_0_.refs_2_.refs_10_.refs_12_), channel_id=1, source_target_pairs={{0,2},{2,0},{4,6},{6,4},{1,3},{3,1},{5,7},{7,5},{8,10},{10,8},{12,... | collective-permute-start | bytes 4718600 | tf_op jit(solution)/shard_map/ppermute | solution.py:259
  78.4 35.5 %collective-permute-start.17 = (bf16[256,3072]{1,0:T(8,128)(2,1)S(1)}, bf16[256,3072]{1,0:T(8,128)(2,1)S(1)}, u32[]{:S(2)}, u32[]{:S(2)}) collective-permute-start(bf16[256,3072]{1,0:T(8,128)(2,1)S(1)} %collective-permute-done.10.refs_6_.refs_0_.refs_2_.refs_16_), channel_id=1, source_target_pairs={{0,4},{2,6},{4,0},{6,2},{1,5},{3,7},{5,1},{7,3},{8,12},{10,14},{12... | collective-permute-start | bytes 4718600 | tf_op jit(solution)/shard_map/ppermute | solution.py:259
  78.9 36.4 %collective-permute-start.16 = (bf16[256,3072]{1,0:T(8,128)(2,1)S(1)}, bf16[256,3072]{1,0:T(8,128)(2,1)S(1)}, u32[]{:S(2)}, u32[]{:S(2)}) collective-permute-start(bf16[256,3072]{1,0:T(8,128)(2,1)S(1)} %collective-permute-done.10.refs_6_.refs_0_.refs_2_.refs_16_), channel_id=1, source_target_pairs={{0,24},{8,0},{16,8},{24,16},{1,25},{9,1},{17,9},{25,17},{2,26},{10... | collective-permute-start | bytes 4718600 | tf_op jit(solution)/shard_map/ppermute | solution.py:262
  81.4 42.6 %collective-permute-start.14 = (bf16[3072,256]{1,0:T(8,128)(2,1)S(1)}, bf16[3072,256]{1,0:T(8,128)(2,1)S(1)}, u32[]{:S(2)}, u32[]{:S(2)}) collective-permute-start(bf16[3072,256]{1,0:T(8,128)(2,1)S(1)} %terms.8.refs_5_.refs_0_.refs_2_), channel_id=1, source_target_pairs={{0,1},{1,0},{2,3},{3,2},{4,5},{5,4},{6,7},{7,6},{8,9},{9,8},{10,11... | collective-permute-start | bytes 4718600 | tf_op jit(solution)/shard_map/ppermute | solution.py:262
  97.6 19.3 %collective-permute-start.12 = (bf16[3072,128]{1,0:T(8,128)(2,1)S(1)}, bf16[3072,128]{1,0:T(8,128)(2,1)S(1)}, u32[]{:S(2)}, u32[]{:S(2)}) collective-permute-start(bf16[3072,128]{1,0:T(8,128)(2,1)S(1)} %get-tuple-element.62), channel_id=1, source_target_pairs={{0,2},{2,0},{4,6},{6,4},{1,3},{3,1},{5,7},{7,5},{8,10},{10,8},{12,... | collective-permute-start | bytes 2359304 | tf_op jit(solution)/shard_map/ppermute | solution.py:259
  113.9 15.5 %collective-permute-start.20 = (bf16[256,3072]{1,0:T(8,128)(2,1)S(1)}, bf16[256,3072]{1,0:T(8,128)(2,1)S(1)}, u32[]{:S(2)}, u32[]{:S(2)}) collective-permute-start(bf16[256,3072]{1,0:T(8,128)(2,1)S(1)} %collective-permute-done.17.refs_7_.refs_0_.refs_2_.refs_14_.refs_4_), channel_id=1, source_target_pairs={{0,2},{2,0},{4,6},{6,4},{1,3},{3,1},{5,7},{7,5},{8,10},{10,8},{12,... | collective-permute-start | bytes 4718600 | tf_op jit(solution)/shard_map/ppermute | solution.py:259
  113.9 43.8 %collective-permute-start.19 = (bf16[3072,256]{1,0:T(8,128)(2,1)S(1)}, bf16[3072,256]{1,0:T(8,128)(2,1)S(1)}, u32[]{:S(2)}, u32[]{:S(2)}) collective-permute-start(bf16[3072,256]{1,0:T(8,128)(2,1)S(1)} %terms.9.refs_5_.refs_0_.refs_2_), channel_id=1, source_target_pairs={{0,1},{1,0},{2,3},{3,2},{4,5},{5,4},{6,7},{7,6},{8,9},{9,8},{10,11... | collective-permute-start | bytes 4718600 | tf_op jit(solution)/shard_map/ppermute | solution.py:262
  115.4 36.5 %collective-permute-start.21 = (bf16[256,3072]{1,0:T(8,128)(2,1)S(1)}, bf16[256,3072]{1,0:T(8,128)(2,1)S(1)}, u32[]{:S(2)}, u32[]{:S(2)}) collective-permute-start(bf16[256,3072]{1,0:T(8,128)(2,1)S(1)} %collective-permute-done.16.refs_6_.refs_0_.refs_2_.refs_10_.refs_4_), channel_id=1, source_target_pairs={{0,4},{2,6},{4,0},{6,2},{1,5},{3,7},{5,1},{7,3},{8,12},{10,14},{12... | collective-permute-start | bytes 4718600 | tf_op jit(solution)/shard_map/ppermute | solution.py:259
  128.8 8.9 %collective-permute-start.18 = (bf16[3072,128]{1,0:T(8,128)(2,1)S(1)}, bf16[3072,128]{1,0:T(8,128)(2,1)S(1)}, u32[]{:S(2)}, u32[]{:S(2)}) collective-permute-start(bf16[3072,128]{1,0:T(8,128)(2,1)S(1)} %get-tuple-element.67), channel_id=1, source_target_pairs={{0,2},{2,0},{4,6},{6,4},{1,3},{3,1},{5,7},{7,5},{8,10},{10,8},{12,... | collective-permute-start | bytes 2359304 | tf_op jit(solution)/shard_map/ppermute | solution.py:259
  128.8 37.7 %collective-permute-start.25 = (bf16[256,3072]{1,0:T(8,128)(2,1)S(1)}, bf16[256,3072]{1,0:T(8,128)(2,1)S(1)}, u32[]{:S(2)}, u32[]{:S(2)}) collective-permute-start(bf16[256,3072]{1,0:T(8,128)(2,1)S(1)} %collective-permute-done.10.refs_6_.refs_0_.refs_2_.refs_16_), channel_id=1, source_target_pairs={{0,2},{2,0},{4,6},{6,4},{1,3},{3,1},{5,7},{7,5},{8,10},{10,8},{12,... | collective-permute-start | bytes 4718600 | tf_op jit(solution)/shard_map/ppermute | solution.py:259
  135.9 55.6 %collective-permute-start.28 = (bf16[3072,256]{1,0:T(8,128)(2,1)}, bf16[3072,256]{1,0:T(8,128)(2,1)}, u32[]{:S(2)}, u32[]{:S(2)}) collective-permute-start(bf16[3072,256]{1,0:T(8,128)(2,1)} %terms.10.refs_5_.refs_0_.refs_2_), channel_id=1, source_target_pairs={{0,1},{1,0},{2,3},{3,2},{4,5},{5,4},{6,7},{7,6},{8,9},{9,8},{10,11... | collective-permute-start | bytes 4718600 | tf_op jit(solution)/shard_map/ppermute | solution.py:262
  165.8 23.9 %collective-permute-start.22 = (bf16[3072,128]{1,0:T(8,128)(2,1)}, bf16[3072,128]{1,0:T(8,128)(2,1)}, u32[]{:S(2)}, u32[]{:S(2)}) collective-permute-start(bf16[3072,128]{1,0:T(8,128)(2,1)} %get-tuple-element.72), channel_id=1, source_target_pairs={{0,2},{2,0},{4,6},{6,4},{1,3},{3,1},{5,7},{7,5},{8,10},{10,8},{12,... | collective-permute-start | bytes 2359304 | tf_op jit(solution)/shard_map/ppermute | solution.py:259
  165.8 25.5 %collective-permute-start.13 = (bf16[3072,128]{1,0:T(8,128)(2,1)}, bf16[3072,128]{1,0:T(8,128)(2,1)}, u32[]{:S(2)}, u32[]{:S(2)}) collective-permute-start(bf16[3072,128]{1,0:T(8,128)(2,1)} %add_convert_fusion.11.refs_8_), channel_id=1, source_target_pairs={{0,4},{2,6},{4,0},{6,2},{1,5},{3,7},{5,1},{7,3},{8,12},{10,14},{12... | collective-permute-start | bytes 2359304 | tf_op jit(solution)/shard_map/ppermute | solution.py:259
  166.4 38.8 %collective-permute-start.27 = (bf16[256,3072]{1,0:T(8,128)(2,1)S(1)}, bf16[256,3072]{1,0:T(8,128)(2,1)}, u32[]{:S(2)}, u32[]{:S(2)}) collective-permute-start(bf16[256,3072]{1,0:T(8,128)(2,1)S(1)} %collective-permute-done.21.refs_6_.refs_0_.refs_2_.refs_8_), channel_id=1, source_target_pairs={{0,2},{2,0},{4,6},{6,4},{1,3},{3,1},{5,7},{7,5},{8,10},{10,8},{12,... | collective-permute-start | bytes 4718600 | tf_op jit(solution)/shard_map/ppermute | solution.py:259
  173.1 52.2 %collective-permute-start.26 = (bf16[3072,256]{1,0:T(8,128)(2,1)}, bf16[3072,256]{1,0:T(8,128)(2,1)}, u32[]{:S(2)}, u32[]{:S(2)}) collective-permute-start(bf16[3072,256]{1,0:T(8,128)(2,1)} %terms.11.refs_12_.refs_0_.refs_2_), channel_id=1, source_target_pairs={{0,1},{1,0},{2,3},{3,2},{4,5},{5,4},{6,7},{7,6},{8,9},{9,8},{10,11... | collective-permute-start | bytes 4718600 | tf_op jit(solution)/shard_map/ppermute | solution.py:262
  202.6 2.4 collective-permute-start.29
  202.7 30.9 %collective-permute-start.34 = (bf16[256,3072]{1,0:T(8,128)(2,1)S(1)}, bf16[256,3072]{1,0:T(8,128)(2,1)S(1)}, u32[]{:S(2)}, u32[]{:S(2)}) collective-permute-start(bf16[256,3072]{1,0:T(8,128)(2,1)S(1)} %copy-done.8), channel_id=1, source_target_pairs={{0,2},{2,0},{4,6},{6,4},{1,3},{3,1},{5,7},{7,5},{8,10},{10,8},{12,... | collective-permute-start | bytes 4718600 | tf_op jit(solution)/shard_map/ppermute | solution.py:259
  203.2 22.0 %collective-permute-start.23 = (bf16[3072,128]{1,0:T(8,128)(2,1)S(1)}, bf16[3072,128]{1,0:T(8,128)(2,1)S(1)}, u32[]{:S(2)}, u32[]{:S(2)}) collective-permute-start(bf16[3072,128]{1,0:T(8,128)(2,1)S(1)} %add_convert_fusion.8.refs_7_), channel_id=1, source_target_pairs={{0,4},{2,6},{4,0},{6,2},{1,5},{3,7},{5,1},{7,3},{8,12},{10,14},{12... | collective-permute-start | bytes 2359304 | tf_op jit(solution)/shard_map/ppermute | solution.py:259
  217.1 52.8 %collective-permute-start.36 = (bf16[3072,256]{1,0:T(8,128)(2,1)}, bf16[3072,256]{1,0:T(8,128)(2,1)}, u32[]{:S(2)}, u32[]{:S(2)}) collective-permute-start(bf16[3072,256]{1,0:T(8,128)(2,1)} %terms.12.refs_5_.refs_0_.refs_2_), channel_id=1, source_target_pairs={{0,1},{1,0},{2,3},{3,2},{4,5},{5,4},{6,7},{7,6},{8,9},{9,8},{10,11... | collective-permute-start | bytes 4718600 | tf_op jit(solution)/shard_map/ppermute | solution.py:262
  218.8 20.7 %collective-permute-start.31 = (bf16[3072,128]{1,0:T(8,128)(2,1)S(1)}, bf16[3072,128]{1,0:T(8,128)(2,1)S(1)}, u32[]{:S(2)}, u32[]{:S(2)}) collective-permute-start(bf16[3072,128]{1,0:T(8,128)(2,1)S(1)} %add_convert_fusion.6.refs_7_), channel_id=1, source_target_pairs={{0,4},{2,6},{4,0},{6,2},{1,5},{3,7},{5,1},{7,3},{8,12},{10,14},{12... | collective-permute-start | bytes 2359304 | tf_op jit(solution)/shard_map/ppermute | solution.py:259
  232.2 14.9 %collective-permute-start.30 = (bf16[3072,128]{1,0:T(8,128)(2,1)S(1)}, bf16[3072,128]{1,0:T(8,128)(2,1)S(1)}, u32[]{:S(2)}, u32[]{:S(2)}) collective-permute-start(bf16[3072,128]{1,0:T(8,128)(2,1)S(1)} %get-tuple-element.84), channel_id=1, source_target_pairs={{0,2},{2,0},{4,6},{6,4},{1,3},{3,1},{5,7},{7,5},{8,10},{10,8},{12,... | collective-permute-start | bytes 2359304 | tf_op jit(solution)/shard_map/ppermute | solution.py:259
  233.6 35.3 %collective-permute-start.24 = (bf16[3072,128]{1,0:T(8,128)(2,1)}, bf16[3072,128]{1,0:T(8,128)(2,1)S(1)}, u32[]{:S(2)}, u32[]{:S(2)}) collective-permute-start(bf16[3072,128]{1,0:T(8,128)(2,1)} %add_convert_fusion.7), channel_id=1, source_target_pairs={{0,8},{8,16},{16,24},{24,0},{1,9},{9,17},{17,25},{25,1},{2,10},{10... | collective-permute-start | bytes 2359304 | tf_op jit(solution)/shard_map/ppermute | solution.py:262
  245.3 46.1 %collective-permute-start.35 = (bf16[3072,256]{1,0:T(8,128)(2,1)S(1)}, bf16[3072,256]{1,0:T(8,128)(2,1)}, u32[]{:S(2)}, u32[]{:S(2)}) collective-permute-start(bf16[3072,256]{1,0:T(8,128)(2,1)S(1)} %terms.13.refs_18_.refs_0_.refs_2_), channel_id=1, source_target_pairs={{0,1},{1,0},{2,3},{3,2},{4,5},{5,4},{6,7},{7,6},{8,9},{9,8},{10,11... | collective-permute-start | bytes 4718600 | tf_op jit(solution)/shard_map/ppermute | solution.py:262
  282.6 2.4 collective-permute-start.38
  286.0 31.6 %collective-permute-start.39 = (bf16[3072,128]{1,0:T(8,128)(2,1)}, bf16[3072,128]{1,0:T(8,128)(2,1)}, u32[]{:S(2)}, u32[]{:S(2)}) collective-permute-start(bf16[3072,128]{1,0:T(8,128)(2,1)} %add_convert_fusion.2.refs_14_), channel_id=1, source_target_pairs={{0,4},{2,6},{4,0},{6,2},{1,5},{3,7},{5,1},{7,3},{8,12},{10,14},{12... | collective-permute-start | bytes 2359304 | tf_op jit(solution)/shard_map/ppermute | solution.py:259
  299.9 17.7 %collective-permute-start.37 = (bf16[3072,128]{1,0:T(8,128)(2,1)S(1)}, bf16[3072,128]{1,0:T(8,128)(2,1)S(1)}, u32[]{:S(2)}, u32[]{:S(2)}) collective-permute-start(bf16[3072,128]{1,0:T(8,128)(2,1)S(1)} %get-tuple-element.89), channel_id=1, source_target_pairs={{0,2},{2,0},{4,6},{6,4},{1,3},{3,1},{5,7},{7,5},{8,10},{10,8},{12,... | collective-permute-start | bytes 2359304 | tf_op jit(solution)/shard_map/ppermute | solution.py:259
  300.0 37.8 %collective-permute-start.32 = (bf16[1536,128]{1,0:T(8,128)(2,1)S(1)}, bf16[1536,128]{1,0:T(8,128)(2,1)S(1)}, u32[]{:S(2)}, u32[]{:S(2)}) collective-permute-start(bf16[1536,128]{1,0:T(8,128)(2,1)S(1)} %get-tuple-element.112), channel_id=1, source_target_pairs={{0,16},{8,24},{16,0},{24,8},{1,17},{9,25},{17,1},{25,9},{2,18},{10... | collective-permute-start | bytes 1179656 | tf_op jit(solution)/shard_map/ppermute | solution.py:262
  320.0 58.9 %collective-permute-start.40 = (bf16[3072,128]{1,0:T(8,128)(2,1)S(1)}, bf16[3072,128]{1,0:T(8,128)(2,1)S(1)}, u32[]{:S(2)}, u32[]{:S(2)}) collective-permute-start(bf16[3072,128]{1,0:T(8,128)(2,1)S(1)} %get-tuple-element.110), channel_id=1, source_target_pairs={{0,24},{8,0},{16,8},{24,16},{1,25},{9,1},{17,9},{25,17},{2,26},{10... | collective-permute-start | bytes 2359304 | tf_op jit(solution)/shard_map/ppermute | solution.py:262
  337.8 5.3 %collective-permute-start.41 = (f32[8,128]{1,0:T(8,128)S(1)}, f32[8,128]{1,0:T(8,128)S(1)}, u32[]{:S(2)}, u32[]{:S(2)}) collective-permute-start(f32[8,128]{1,0:T(8,128)S(1)} %broadcast_in_dim.3), channel_id=1, source_target_pairs={{0,8},{8,16},{16,24},{24,0},{1,9},{9,17},{17,25},{25,1},{2,10},{10... | collective-permute-start | bytes 12296 | tf_op jit(solution)/shard_map/ppermute | solution.py:262
  339.3 4.8 %collective-permute-start.42 = (f32[8,128]{1,0:T(8,128)S(1)}, f32[8,128]{1,0:T(8,128)S(1)}, u32[]{:S(2)}, u32[]{:S(2)}) collective-permute-start(f32[8,128]{1,0:T(8,128)S(1)} %broadcast_in_dim.3), channel_id=1, source_target_pairs={{0,16},{8,24},{16,0},{24,8},{1,17},{9,25},{17,1},{25,9},{2,18},{10... | collective-permute-start | bytes 12296 | tf_op jit(solution)/shard_map/ppermute | solution.py:262
  342.5 11.5 %collective-permute-start.43 = (f32[8,128]{1,0:T(8,128)S(1)}, f32[8,128]{1,0:T(8,128)S(1)}, u32[]{:S(2)}, u32[]{:S(2)}) collective-permute-start(f32[8,128]{1,0:T(8,128)S(1)} %broadcast_in_dim.3), channel_id=1, source_target_pairs={{0,24},{8,0},{16,8},{24,16},{1,25},{9,1},{17,9},{25,17},{2,26},{10... | collective-permute-start | bytes 12296 | tf_op jit(solution)/shard_map/ppermute | solution.py:262
  342.8 36.1 %collective-permute-start.33 = (bf16[1536,128]{1,0:T(8,128)(2,1)S(1)}, bf16[1536,128]{1,0:T(8,128)(2,1)S(1)}, u32[]{:S(2)}, u32[]{:S(2)}) collective-permute-start(bf16[1536,128]{1,0:T(8,128)(2,1)S(1)} %get-tuple-element.113), channel_id=1, source_target_pairs={{0,16},{8,24},{16,0},{24,8},{1,17},{9,25},{17,1},{25,9},{2,18},{10... | collective-permute-start | bytes 1179656 | tf_op jit(solution)/shard_map/ppermute | solution.py:262
  354.0 1.9 collective-permute-start.44
  354.0 3.7 collective-permute-start.45
  354.6 3.1 collective-permute-start.46
  357.7 3.7 collective-permute-start.47
  (72 other events, 999.1 us)
